TPU v7x, 128 devices: a whole 4x4x4 slice. The times are simulated.
128 devices in a mesh: batch: 8 (over x_hi, y), tensor: 16 (over x_lo, z, core).
Axes of the slice: x: 4 (x_hi: 2, x_lo: 2; x = x_hi * 2 + x_lo), y: 4, z: 4, core: 2. Of those that a mesh axis runs over, the one named last changes fastest.
Arguments:
- tokens: bfloat16 [16384, 2048], P('batch'), may hold values from -6 to 6
- ln1_gain: float32 [2048], replicated, may hold values from 0.5 to 1.5
- ln1_shift: float32 [2048], replicated, may hold values from -0.12 to 0.12
- qkv_weight: bfloat16 [3, 2048, 2048], P(None, None, 'tensor'), may hold values from -0.125 to 0.125
- out_weight: bfloat16 [2048, 2048], P('tensor'), may hold values from -2 to 2
- ln2_gain: float32 [2048], replicated, may hold values from 0.5 to 1.5
- ln2_shift: float32 [2048], replicated, may hold values from -0.6 to 0.6
- up_weight: bfloat16 [2048, 8192], P(None, 'tensor'), may hold values from -0.125 to 0.125
- down_weight: bfloat16 [8192, 2048], P('tensor'), may hold values from -0.0625 to 0.0625
- lengths: int32 [8], P('batch'), may hold values from 512 to 2048, as said below
- cotangent: bfloat16 [16384, 2048], P(('batch', 'tensor')), may hold values from -6 to 6
Outputs:
- output: bfloat16 [16384, 2048], P(('batch', 'tensor'))
- grad_tokens: bfloat16 [16384, 2048], P(('batch', 'tensor'))
- grad_qkv: float32 [3, 2048, 2048], P(None, 'batch', 'tensor')
- grad_out: float32 [2048, 2048], P('tensor', 'batch')
- grad_up: float32 [2048, 8192], P('batch', 'tensor')
- grad_down: float32 [8192, 2048], P('tensor', 'batch')
- grad_gains: float32 [2, 2048], replicated
- grad_shifts: float32 [2, 2048], replicated
Inputs may be any that keep to these rules, and one draw needn't show every extreme that they name: `lengths`: live tokens of each sequence; the rest of its 2048 slots are padding.
All inputs are finite; a program needn't handle non-finite values.
Results may differ from a plain program's by a relative error of at most 0.025.
Values may be sent and summed in bfloat16 or wider, within the bound.
No kernel may reach another device: no remote copies, remote signals or barrier semaphores. Data moves between devices by JAX's collectives and lax.ppermute only.
A program may use at most 256 MiB of HBM per device.

v0:
```python
from functools import partial

import jax
import jax.numpy as jnp
from jax import lax
from jax.sharding import PartitionSpec as P

HD = 128


EPS = 1e-05
MASKED_SCORE = -1e30


def norm_stats(values):
    centre = jnp.mean(values, axis=-1, keepdims=True)
    offsets = values - centre
    spread = jnp.mean(offsets * offsets, axis=-1, keepdims=True)
    inverse = lax.rsqrt(spread + EPS)
    return (offsets * inverse, inverse)


def norm_back(grad_normed, gain, unit_rows, inverse):
    scaled = grad_normed * gain
    return inverse * (
        scaled
        - jnp.mean(scaled, axis=-1, keepdims=True)
        - unit_rows * jnp.mean(scaled * unit_rows, axis=-1, keepdims=True)
    )


def block_mask(start_row, stop_row, length):
    query_index = start_row + jnp.arange(stop_row - start_row, dtype=jnp.int32)[:, None]
    key_index = jnp.arange(stop_row, dtype=jnp.int32)[None, :]
    return (key_index <= query_index) & (key_index < length)


def block_scores(queries, key_rows, start_row, stop_row, length):
    score_scale = queries.shape[-1] ** (-0.5)
    scores = (
        jnp.einsum(
            "qhe,khe->hqk",
            queries[start_row:stop_row],
            key_rows[:stop_row],
            preferred_element_type=jnp.float32,
        )
        * score_scale
    )
    return jnp.where(block_mask(start_row, stop_row, length)[None], scores, MASKED_SCORE)


def attend_forward(queries, key_rows, value_rows, length):
    seq_len = queries.shape[0]
    block_rows = min(512, seq_len)
    pieces = []
    totals = []
    for start_row in range(0, seq_len, block_rows):
        stop_row = start_row + block_rows
        scores = block_scores(queries, key_rows, start_row, stop_row, length)
        row_peak = jnp.max(scores, axis=-1, keepdims=True)
        log_total = jnp.log(jnp.sum(jnp.exp(scores - row_peak), axis=-1, keepdims=True)) + row_peak
        attn_probs = jnp.exp(scores - log_total).astype(jnp.bfloat16)
        attended = jnp.einsum(
            "hqk,khe->qhe", attn_probs, value_rows[:stop_row], preferred_element_type=jnp.float32
        )
        pieces.append(attended.astype(jnp.bfloat16))
        totals.append(log_total[..., 0])
    return (jnp.concatenate(pieces, axis=0), jnp.concatenate(totals, axis=1))


def attend_backward(queries, key_rows, value_rows, grad_attended, totals, length):
    seq_len = queries.shape[0]
    block_rows = min(512, seq_len)
    score_scale = queries.shape[-1] ** (-0.5)
    grad_queries = []
    grad_keys = jnp.zeros(key_rows.shape, jnp.float32)
    grad_values = jnp.zeros(value_rows.shape, jnp.float32)
    for start_row in range(0, seq_len, block_rows):
        stop_row = start_row + block_rows
        scores = block_scores(queries, key_rows, start_row, stop_row, length)
        attn_probs = jnp.exp(scores - totals[:, start_row:stop_row, None])
        grad_probs = jnp.einsum(
            "qhe,khe->hqk",
            grad_attended[start_row:stop_row],
            value_rows[:stop_row],
            preferred_element_type=jnp.float32,
        )
        centre = jnp.sum(attn_probs * grad_probs, axis=-1, keepdims=True)
        grad_scores = (attn_probs * (grad_probs - centre)).astype(jnp.bfloat16)
        grad_queries.append(
            jnp.einsum(
                "hqk,khe->qhe", grad_scores, key_rows[:stop_row], preferred_element_type=jnp.float32
            )
            * score_scale
        )
        grad_keys = grad_keys.at[:stop_row].add(
            jnp.einsum(
                "hqk,qhe->khe",
                grad_scores,
                queries[start_row:stop_row],
                preferred_element_type=jnp.float32,
            )
            * score_scale
        )
        grad_values = grad_values.at[:stop_row].add(
            jnp.einsum(
                "hqk,qhe->khe",
                attn_probs.astype(jnp.bfloat16),
                grad_attended[start_row:stop_row],
                preferred_element_type=jnp.float32,
            )
        )
    grad_queries = jnp.concatenate(grad_queries, axis=0)
    return (
        grad_queries.astype(jnp.bfloat16),
        grad_keys.astype(jnp.bfloat16),
        grad_values.astype(jnp.bfloat16),
    )


def body(
    tokens,
    ln1_gain,
    ln1_shift,
    qkv_weight,
    out_weight,
    ln2_gain,
    ln2_shift,
    up_weight,
    down_weight,
    lengths,
    cotangent,
):
    shard_rows = tokens.shape[0]
    seq_count = lengths.shape[0]
    seq_len = shard_rows // seq_count
    row_share = shard_rows // lax.axis_size("tensor")
    first_row = lax.axis_index("tensor") * row_share
    local_width = qkv_weight.shape[2]
    local_heads = local_width // HD
    inputs = tokens.astype(jnp.float32)
    unit_first, inverse_first = norm_stats(inputs)
    normed_first = (unit_first * ln1_gain + ln1_shift).astype(jnp.bfloat16)
    projected = jnp.einsum(
        "td,cdh->cth", normed_first, qkv_weight, preferred_element_type=jnp.float32
    ).astype(jnp.bfloat16)
    shaped = projected.reshape(3, seq_count, seq_len, local_heads, HD)
    attended, totals = lax.map(
        lambda packed: attend_forward(packed[0], packed[1], packed[2], packed[3]),
        (shaped[0], shaped[1], shaped[2], lengths),
    )
    attended_flat = attended.reshape(shard_rows, local_width)
    branch = lax.psum(
        jnp.dot(attended_flat, out_weight, preferred_element_type=jnp.float32).astype(jnp.bfloat16),
        "tensor",
    ).astype(jnp.float32)
    middle = inputs + branch
    unit_second, inverse_second = norm_stats(middle)
    normed_second = (unit_second * ln2_gain + ln2_shift).astype(jnp.bfloat16)
    middle_rows = lax.dynamic_slice_in_dim(middle, first_row, row_share, 0)
    unit_second_rows = lax.dynamic_slice_in_dim(unit_second, first_row, row_share, 0)
    inverse_second_rows = lax.dynamic_slice_in_dim(inverse_second, first_row, row_share, 0)
    hidden = jnp.dot(normed_second, up_weight, preferred_element_type=jnp.float32)
    activated = jax.nn.gelu(hidden, approximate=True).astype(jnp.bfloat16)
    mixed = lax.psum(
        jnp.dot(activated, down_weight, preferred_element_type=jnp.float32).astype(jnp.bfloat16),
        "tensor",
    ).astype(jnp.float32)
    mixed_rows = lax.dynamic_slice_in_dim(mixed, first_row, row_share, 0)
    output = (middle_rows + mixed_rows).astype(jnp.bfloat16)
    positions = first_row + jnp.arange(row_share, dtype=jnp.int32)
    seq_index = positions // seq_len
    length_rows = jnp.sum(
        jnp.where(
            seq_index[:, None] == jnp.arange(seq_count, dtype=jnp.int32)[None, :],
            lengths[None, :],
            0,
        ),
        axis=1,
    )
    live_rows = (positions % seq_len < length_rows).astype(jnp.float32)
    incoming_rows = cotangent.astype(jnp.float32) * live_rows[:, None]
    incoming = lax.all_gather(incoming_rows.astype(jnp.bfloat16), "tensor", axis=0, tiled=True)
    grad_down = jnp.einsum("tf,td->fd", activated, incoming, preferred_element_type=jnp.float32)
    grad_act = jnp.einsum("td,fd->tf", incoming, down_weight, preferred_element_type=jnp.float32)
    gelu_pull = jax.vjp(partial(jax.nn.gelu, approximate=True), hidden)[1]
    grad_hidden = gelu_pull(grad_act)[0].astype(jnp.bfloat16)
    grad_up = jnp.einsum(
        "td,tf->df", normed_second, grad_hidden, preferred_element_type=jnp.float32
    )
    grad_normed_second = lax.psum_scatter(
        jnp.einsum(
            "tf,df->td",
            lax.slice_in_dim(grad_hidden, 0, row_share * lax.axis_size("tensor"), axis=0),
            up_weight,
            preferred_element_type=jnp.float32,
        ).astype(jnp.bfloat16),
        "tensor",
        scatter_dimension=0,
        tiled=True,
    ).astype(jnp.float32)
    grad_middle = incoming_rows + norm_back(
        grad_normed_second, ln2_gain, unit_second_rows, inverse_second_rows
    )
    gain_second = jnp.sum(grad_normed_second * unit_second_rows, axis=0)
    shift_second = jnp.sum(grad_normed_second, axis=0)
    grad_branch = lax.all_gather(grad_middle.astype(jnp.bfloat16), "tensor", axis=0, tiled=True)
    grad_out = jnp.einsum(
        "th,td->hd", attended_flat, grad_branch, preferred_element_type=jnp.float32
    )
    grad_attended = jnp.einsum(
        "td,hd->th", grad_branch, out_weight, preferred_element_type=jnp.float32
    ).astype(jnp.bfloat16)
    grad_attended = grad_attended.reshape(seq_count, seq_len, local_heads, HD)
    grad_queries, grad_keys, grad_values = lax.map(
        lambda packed: attend_backward(
            packed[0], packed[1], packed[2], packed[3], packed[4], packed[5]
        ),
        (shaped[0], shaped[1], shaped[2], grad_attended, totals, lengths),
    )
    stacked = jnp.stack([grad_queries, grad_keys, grad_values]).reshape(3, shard_rows, local_width)
    grad_qkv = jnp.einsum("td,cth->cdh", normed_first, stacked, preferred_element_type=jnp.float32)
    grad_qkv, grad_out, grad_up, grad_down = (
        lax.psum_scatter(
            grad_qkv.astype(jnp.bfloat16), "batch", scatter_dimension=1, tiled=True
        ).astype(jnp.float32),
        lax.psum_scatter(
            grad_out.astype(jnp.bfloat16), "batch", scatter_dimension=1, tiled=True
        ).astype(jnp.float32),
        lax.psum_scatter(
            grad_up.astype(jnp.bfloat16), "batch", scatter_dimension=0, tiled=True
        ).astype(jnp.float32),
        lax.psum_scatter(
            grad_down.astype(jnp.bfloat16), "batch", scatter_dimension=1, tiled=True
        ).astype(jnp.float32),
    )
    grad_normed_first = lax.psum_scatter(
        jnp.einsum("cth,cdh->td", stacked, qkv_weight, preferred_element_type=jnp.float32).astype(
            jnp.bfloat16
        ),
        "tensor",
        scatter_dimension=0,
        tiled=True,
    ).astype(jnp.float32)
    unit_first_rows = lax.dynamic_slice_in_dim(unit_first, first_row, row_share, 0)
    inverse_first_rows = lax.dynamic_slice_in_dim(inverse_first, first_row, row_share, 0)
    grad_tokens = (
        grad_middle + norm_back(grad_normed_first, ln1_gain, unit_first_rows, inverse_first_rows)
    ).astype(jnp.bfloat16)
    gain_first = jnp.sum(grad_normed_first * unit_first_rows, axis=0)
    shift_first = jnp.sum(grad_normed_first, axis=0)
    grad_gains, grad_shifts = lax.psum(
        (jnp.stack([gain_first, gain_second]), jnp.stack([shift_first, shift_second])),
        ("batch", "tensor"),
    )
    return (output, grad_tokens, grad_qkv, grad_out, grad_up, grad_down, grad_gains, grad_shifts)


def solution(mesh):
    return jax.shard_map(
        body,
        mesh=mesh,
        in_specs=(
            P("batch", None),
            P(),
            P(),
            P(None, None, "tensor"),
            P("tensor", None),
            P(),
            P(),
            P(None, "tensor"),
            P("tensor", None),
            P("batch"),
            P(("batch", "tensor"), None),
        ),
        out_specs=(
            P(("batch", "tensor"), None),
            P(("batch", "tensor"), None),
            P(None, "batch", "tensor"),
            P("tensor", "batch"),
            P("batch", "tensor"),
            P("tensor", "batch"),
            P(),
            P(),
        ),
        check_vma=False,
    )
```

profile of v0, /device:TPU:0, one launch (start us, length us, event | category | flops | bytes accessed | tf_op | source)
XLA Modules:
  0.0 1004.1 jit_solution(16600903392765366377)
XLA Ops:
  32.6 5.6 convolution_convert_fusion.2
  40.8 143.0 %all-reduce.6.cloned.1.call-done = bf16[2048,2048]{1,0:T(8,128)(2,1)} async-done(((bf16[2048,2048]{1,0:T(8,128)(2,1)}), bf16[2048,2048]{1,0:T(8,128)(2,1)}) %all-reduce.6.cloned.1.call-update) | async-done | bytes 8388624 | tf_op jit(solution)/shard_map/psum | solution.py:153
  183.8 14.3 %fusion = (f32[2048,2048]{1,0:T(8,128)}, f32[2048]{0:T(1024)S(1)}) fusion(bf16[2048,2048]{1,0:T(8,128)(2,1)} %param.31, f32[2048]{0:T(1024)} %copy-done.28, f32[2048]{0:T(1024)S(1)} %broadcast_multiply_fusion.1, bf16[2048,2048]{1,0:T(8,128)(2,1)} %all-reduce.6.cloned.1.call-done), kind=kLoop, calls=%fused_computation.3 | loop fusion | flops 25163776 | bytes 33579008 | tf_op jit(solution)/shard_map/mul | solution.py:20
  198.1 6.7 multiply_reduce_fusion
  205.5 14.8 %subtract_multiply_fusion = (f32[2048,2048]{1,0:T(8,128)}, f32[2048,2048]{1,0:T(8,128)}) fusion(f32[2048]{0:T(1024)S(1)} %add_rsqrt_fusion, f32[2048]{0:T(1024)S(1)} %broadcast_multiply_fusion, bf16[2048,2048]{1,0:T(8,128)(2,1)S(1)} %copy-done.7, bf16[2048,2048]{1,0:T(8,128)(2,1)} %param.31), kind=kLoop, calls=%fused_computation.10 | loop fusion | flops 20971520 | bytes 50348032 | tf_op jit(solution)/shard_map/mul | solution.py:20
  220.2 18.2 %all-gather.3.cloned.1.call-done = bf16[2048,2048]{1,0:T(8,128)(2,1)} async-done(((bf16[128,2048]{1,0:T(8,128)(2,1)}), bf16[2048,2048]{1,0:T(8,128)(2,1)}) %all-gather.3.cloned.1.call-update) | async-done | bytes 8388624 | tf_op jit(solution)/shard_map/all_gather | solution.py:183
  238.5 10.6 %fusion.105 = f32[2048,512]{1,0:T(8,128)} fusion(bf16[2048,2048]{1,0:T(8,128)(2,1)} %all-gather.3.cloned.1.call-done, bf16[512,2048]{1,0:T(8,128)(2,1)} %param.39), kind=kOutput, calls=%fused_computation.202 | convolution fusion | flops 4294967296 | bytes 14680064 | tf_op jit(solution)/shard_map/td,fd->tf/dot_general | solution.py:185
  249.1 9.8 fusion.10
  260.2 7.3 convolution_convert_fusion
  268.4 75.3 %reduce-scatter.7.cloned.1.call-done = bf16[128,2048]{1,0:T(8,128)(2,1)} async-done(((bf16[2048,2048]{1,0:T(8,128)(2,1)}), bf16[128,2048]{1,0:T(8,128)(2,1)}) %reduce-scatter.7.cloned.1.call-update) | async-done | bytes 524304 | tf_op jit(solution)/shard_map/reduce_scatter | solution.py:191
  349.1 11.0 %convolution_convert_fusion.3 = bf16[512,2048]{1,0:T(8,128)(2,1)} fusion(bf16[2048,2048]{1,0:T(8,128)(2,1)} %all-gather.3.cloned.1.call-done, f32[2048,512]{1,0:T(8,128)} %get-tuple-element.244), kind=kOutput, calls=%fused_computation.41 | convolution fusion | flops 4305453056 | bytes 14680064 | tf_op jit(solution)/shard_map/tf,td->fd/dot_general | solution.py:184
  360.4 12.6 %convolution_convert_fusion.4 = bf16[2048,512]{1,0:T(8,128)(2,1)} fusion(bf16[2048,512]{1,0:T(8,128)(2,1)} %copy-done.40, f32[2048,2048]{1,0:T(8,128)} %get-tuple-element.231, f32[2048]{0:T(1024)S(1)} %copy-done.37, f32[2048]{0:T(1024)S(1)} %copy-done.25), kind=kOutput, calls=%fused_computation.42 | convolution fusion | flops 4308598784 | bytes 20987904 | tf_op jit(solution)/shard_map/td,tf->df/dot_general | solution.py:188
  373.0 11.2 %convolution_convert_fusion.1 = bf16[2048,2048]{1,0:T(8,128)(2,1)} fusion(bf16[512,2048]{1,0:T(8,128)(2,1)} %param.39, f32[2048,512]{1,0:T(8,128)} %get-tuple-element.244), kind=kOutput, calls=%fused_computation.13 | convolution fusion | flops 4308598784 | bytes 14680064 | tf_op jit(solution)/shard_map/dot_general | solution.py:166
  384.5 15.0 %all-gather.5.cloned.1.call-done = bf16[2048,2048]{1,0:T(8,128)(2,1)} async-done(((bf16[128,2048]{1,0:T(8,128)(2,1)}), bf16[2048,2048]{1,0:T(8,128)(2,1)}) %all-gather.5.cloned.1.call-update) | async-done | bytes 8388624 | tf_op jit(solution)/shard_map/all_gather | solution.py:207
  399.5 5.7 convolution_convert_fusion.8
  424.8 8.5 fusion.16
  433.4 8.3 bitcast_convert_fusion
  441.8 37.2 %reduce-scatter.17.cloned.1.call-done = bf16[512,256]{1,0:T(8,128)(2,1)} async-done(((bf16[512,2048]{1,0:T(8,128)(2,1)}), bf16[512,256]{1,0:T(8,128)(2,1)}) %reduce-scatter.17.cloned.1.call-update) | async-done | bytes 262160 | tf_op jit(solution)/shard_map/reduce_scatter | solution.py:233
  480.7 75.5 %reduce-scatter.15.cloned.1.call-done = bf16[256,512]{1,0:T(8,128)(2,1)} async-done(((bf16[2048,512]{1,0:T(8,128)(2,1)}), bf16[256,512]{1,0:T(8,128)(2,1)}) %reduce-scatter.15.cloned.1.call-update) | async-done | bytes 262160 | tf_op jit(solution)/shard_map/reduce_scatter | solution.py:230
  558.1 142.6 %all-reduce.8.cloned.1.call-done = bf16[2048,2048]{1,0:T(8,128)(2,1)} async-done(((bf16[2048,2048]{1,0:T(8,128)(2,1)}), bf16[2048,2048]{1,0:T(8,128)(2,1)}) %all-reduce.8.cloned.1.call-update) | async-done | bytes 8388624 | tf_op jit(solution)/shard_map/psum | solution.py:165
  703.1 72.2 %reduce-scatter.13.cloned.1.call-done = bf16[128,256]{1,0:T(8,128)(2,1)} async-done(((bf16[128,2048]{1,0:T(8,128)(2,1)}), bf16[128,256]{1,0:T(8,128)(2,1)}) %reduce-scatter.13.cloned.1.call-update) | async-done | bytes 65552 | tf_op jit(solution)/shard_map/reduce_scatter | solution.py:227
  776.8 75.2 %reduce-scatter.11.cloned.1.call-done = bf16[3,256,128]{1,2,0:T(8,128)(2,1)} async-done(((bf16[3,2048,128]{1,2,0:T(8,128)(2,1)}), bf16[3,256,128]{1,2,0:T(8,128)(2,1)}) %reduce-scatter.11.cloned.1.call-update) | async-done | bytes 196624 | tf_op jit(solution)/shard_map/reduce_scatter | solution.py:224
  853.8 74.4 %reduce-scatter.9.cloned.1.call-done = bf16[128,2048]{1,0:T(8,128)(2,1)} async-done(((bf16[2048,2048]{1,0:T(8,128)(2,1)}), bf16[128,2048]{1,0:T(8,128)(2,1)}) %reduce-scatter.9.cloned.1.call-update) | async-done | bytes 524304 | tf_op jit(solution)/shard_map/reduce_scatter | solution.py:237
  930.0 64.4 %all-reduce.2 = (f32[2,2048]{1,0:T(2,128)}, f32[2,2048]{1,0:T(2,128)}) all-reduce(f32[2,2048]{1,0:T(2,128)S(1)} %pad_maximum_fusion, f32[2,2048]{1,0:T(2,128)S(1)} %pad_maximum_fusion.1), channel_id=1, replica_groups=mesh['batch'=8,'tensor'=16] {'batch','tensor'}, use_global_device_ids=true, to_apply=%region_30.31 | all-reduce | flops 8192 | bytes 65536 | tf_op jit(solution)/shard_map/psum | solution.py:252
  (178 shorter events, 68.7 us)
Async XLA Ops:
  7.2 241.9 %copy-start = (bf16[2048,512]{1,0:T(8,128)(2,1)S(1)}, bf16[2048,512]{1,0:T(8,128)(2,1)}, u32[]{:S(2)}) copy-start(bf16[2048,512]{1,0:T(8,128)(2,1)} %param.38) | copy-start | bytes 6291460
  7.2 176.6 %all-reduce.6.cloned.1.call-start = ((), (), s32[]{:S(2)}) async-start(), calls=%async_computation.6 | async-start | bytes 16777216 | tf_op jit(solution)/shard_map/psum | solution.py:153
  38.2 200.3 %all-gather.3.cloned.1.call-start = ((), (), s32[]{:S(2)}) async-start(), calls=%async_computation.8 | async-start | bytes 8912896 | tf_op jit(solution)/shard_map/all_gather | solution.py:183
  40.8 303.0 %reduce-scatter.7.cloned.1.call-start = ((), (), s32[]{:S(2)}) async-start(), calls=%async_computation.9 | async-start | bytes 8912896 | tf_op jit(solution)/shard_map/reduce_scatter | solution.py:191
  183.8 14.4 %copy-start.7 = (bf16[2048,2048]{1,0:T(8,128)(2,1)S(1)}, bf16[2048,2048]{1,0:T(8,128)(2,1)}, u32[]{:S(2)}) copy-start(bf16[2048,2048]{1,0:T(8,128)(2,1)} %all-reduce.6.cloned.1.call-done) | copy-start | bytes 25165828
  238.5 10.6 %copy-start.10 = (f32[2048,2048]{1,0:T(8,128)S(1)}, f32[2048,2048]{1,0:T(8,128)}, u32[]{:S(2)}) copy-start(f32[2048,2048]{1,0:T(8,128)} %get-tuple-element.231) | copy-start | bytes 50331652
  238.5 10.6 %copy-start.24 = (f32[2048]{0:T(1024)S(1)}, f32[2048]{0:T(1024)}, u32[]{:S(2)}) copy-start(f32[2048]{0:T(1024)} %param.36) | copy-start | bytes 24580
  238.5 10.6 %copy-start.36 = (f32[2048]{0:T(1024)S(1)}, f32[2048]{0:T(1024)}, u32[]{:S(2)}) copy-start(f32[2048]{0:T(1024)} %param.37) | copy-start | bytes 24580
  267.5 76.2 %copy-start.25 = (f32[2048]{0:T(1024)S(1)}, f32[2048]{0:T(1024)}, u32[]{:S(2)}) copy-start(f32[2048]{0:T(1024)} %param.36) | copy-start | bytes 24580
  267.5 78.5 %copy-start.14 = (bf16[128,2048]{1,0:T(8,128)(2,1)S(1)}, bf16[128,2048]{1,0:T(8,128)(2,1)}, u32[]{:S(2)}) copy-start(bf16[128,2048]{1,0:T(8,128)(2,1)} %param.41) | copy-start | bytes 1572868
  267.5 78.5 %copy-start.34 = (f32[128]{0:T(128)S(1)}, f32[128]{0:T(128)}, u32[]{:S(2)}) copy-start(f32[128]{0:T(128)} %copy-done.33) | copy-start | bytes 1540
  267.6 132.0 %all-gather.5.cloned.1.call-start = ((), (), s32[]{:S(2)}) async-start(), calls=%async_computation.10 | async-start | bytes 8912896 | tf_op jit(solution)/shard_map/all_gather | solution.py:207
  349.0 130.0 %reduce-scatter.17.cloned.1.call-start = ((), (), s32[]{:S(2)}) async-start(), calls=%async_computation.15 | async-start | bytes 2359296 | tf_op jit(solution)/shard_map/reduce_scatter | solution.py:233
  349.1 11.3 %copy-start.37 = (f32[2048]{0:T(1024)S(1)}, f32[2048]{0:T(1024)}, u32[]{:S(2)}) copy-start(f32[2048]{0:T(1024)} %param.37) | copy-start | bytes 24580
  360.1 196.1 %reduce-scatter.15.cloned.1.call-start = ((), (), s32[]{:S(2)}) async-start(), calls=%async_computation.14 | async-start | bytes 2359296 | tf_op jit(solution)/shard_map/reduce_scatter | solution.py:230
  373.0 327.7 %all-reduce.8.cloned.1.call-start = ((), (), s32[]{:S(2)}) async-start(), calls=%async_computation.7 | async-start | bytes 16777216 | tf_op jit(solution)/shard_map/psum | solution.py:165
  384.2 15.3 %copy-start.16 = (bf16[128,2048]{1,0:T(8,128)(2,1)S(1)}, bf16[128,2048]{1,0:T(8,128)(2,1)}, u32[]{:S(2)}) copy-start(bf16[128,2048]{1,0:T(8,128)(2,1)} %param.35) | copy-start | bytes 1572868
  384.3 391.1 %reduce-scatter.13.cloned.1.call-start = ((), (), s32[]{:S(2)}) async-start(), calls=%async_computation.13 | async-start | bytes 589824 | tf_op jit(solution)/shard_map/reduce_scatter | solution.py:227
  424.7 427.3 %reduce-scatter.11.cloned.1.call-start = ((), (), s32[]{:S(2)}) async-start(), calls=%async_computation.12 | async-start | bytes 1769472 | tf_op jit(solution)/shard_map/reduce_scatter | solution.py:224
  433.3 494.9 %reduce-scatter.9.cloned.1.call-start = ((), (), s32[]{:S(2)}) async-start(), calls=%async_computation.11 | async-start | bytes 8912896 | tf_op jit(solution)/shard_map/reduce_scatter | solution.py:237
  441.6 488.3 %copy-start.32 = (f32[2048]{0:T(1024)S(1)}, f32[2048]{0:T(1024)}, u32[]{:S(2)}) copy-start(f32[2048]{0:T(1024)} %get-tuple-element.221) | copy-start | bytes 24580
  441.7 488.3 %copy-start.31 = (f32[2048]{0:T(1024)S(1)}, f32[2048]{0:T(1024)}, u32[]{:S(2)}) copy-start(f32[2048]{0:T(1024)} %get-tuple-element.226) | copy-start | bytes 24580
  441.7 552.8 %copy-start.13 = (f32[128,2048]{1,0:T(8,128)S(1)}, f32[128,2048]{1,0:T(8,128)}, u32[]{:S(2)}) copy-start(f32[128,2048]{1,0:T(8,128)} %get-tuple-element.230) | copy-start | bytes 3145732
  700.7 296.3 %copy-start.1 = (bf16[2048,512]{1,0:T(8,128)(2,1)S(1)}, bf16[2048,512]{1,0:T(8,128)(2,1)}, u32[]{:S(2)}) copy-start(bf16[2048,512]{1,0:T(8,128)(2,1)} %param.38) | copy-start | bytes 6291460
  (29 other events, 69.3 us)
Sparse Core Ops, SparseCore 0:
  38.3 145.4 all-reduce.5
  186.1 52.3 all-gather.2
  267.7 75.9 reduce-scatter.6
  349.1 50.3 all-gather.4
  403.1 75.8 reduce-scatter.16
  482.5 73.6 reduce-scatter.14
  558.8 141.8 all-reduce.7
  704.8 70.4 reduce-scatter.12
  779.5 72.5 reduce-scatter.10
  854.3 73.8 reduce-scatter.8
where the time goes:
time: 1010 us; the launch traced here: 1000 us
  waiting for transfers between devices  729 us (72%)
  matrix products  115 us (11%)
  other arithmetic  66.4 us (7%)
  blocking collectives  64.4 us (6%)
  between operations  15.9 us (2%)
  local copies, waits for them, and re-layouts  12.8 us (1%)
    psum x1, waiting for transfers between devices, body(): lax.psum(jnp.dot(attended_flat, out_weight, preferred_element_type=jnp.fl...  143 us
    psum x1, waiting for transfers between devices, body(): lax.psum(jnp.dot(activated, down_weight, preferred_element_type=jnp.float...  143 us
    reduce_scatter x1, waiting for transfers between devices, body(): lax.psum_scatter(grad_up.astype(jnp.bfloat16), 'batch', scatter_dimension...  75.5 us
    reduce_scatter x1, waiting for transfers between devices, body(): lax.psum_scatter(jnp.einsum('tf,df->td', lax.slice_in_dim(grad_hidden, 0,...  75.3 us
    reduce_scatter x1, waiting for transfers between devices, body(): lax.psum_scatter(grad_qkv.astype(jnp.bfloat16), 'batch', scatter_dimensio...  75.2 us
    reduce_scatter x1, waiting for transfers between devices, body(): lax.psum_scatter(jnp.einsum('cth,cdh->td', stacked, qkv_weight, preferred...  74.4 us
    reduce_scatter x1, waiting for transfers between devices, body(): lax.psum_scatter(grad_out.astype(jnp.bfloat16), 'batch', scatter_dimensio...  72.2 us
    psum x1, blocking collectives, body(): lax.psum((jnp.stack([gain_first, gain_second]), jnp.stack([shift_first, s...  64.4 us
  transfers between devices with their start and end apart: 10, of which 10 were waited for; matrix products, arithmetic and copies ran while one was open for 12% of the time, Pallas kernels for 0%

commit v1 on v0

v1 whole, which is shorter than its diff:
```python
from functools import partial

import jax
import jax.numpy as jnp
from jax import lax
from jax.sharding import PartitionSpec as P

HD = 128
EPS = 1e-05
MASKED_SCORE = -1e30
BF = jnp.bfloat16
F32 = jnp.float32


def place(index):
    batch, tensor = divmod(index, 16)
    return [batch // 4, batch % 4, tensor // 8, (tensor // 2) % 4, tensor % 2]


def index_of(at):
    x_hi, y, x_lo, z, core = at
    return (x_hi * 4 + y) * 16 + x_lo * 8 + z * 2 + core


def mover(step):
    pairs = [(i, index_of(step(place(i)))) for i in range(128)]
    return lambda values: lax.ppermute(values, ("batch", "tensor"), pairs)


def along_z(by):
    return mover(lambda a: [a[0], a[1], a[2], (a[3] + by) % 4, a[4]])


def along_y(by):
    return mover(lambda a: [a[0], (a[1] + by) % 4, a[2], a[3], a[4]])


def along_x(by):
    def step(a):
        ring = (a[0] * 2 + a[2] + by) % 4
        return [ring // 2, a[1], ring % 2, a[3], a[4]]

    return mover(step)


z_up, z_down, z_far = along_z(1), along_z(-1), along_z(2)
y_up, y_down, y_far = along_y(1), along_y(-1), along_y(2)
x_up, x_down, x_far = along_x(1), along_x(-1), along_x(2)
x_pair = mover(lambda a: [a[0], a[1], 1 - a[2], a[3], a[4]])
core_swap = mover(lambda a: [a[0], a[1], a[2], a[3], 1 - a[4]])


def norm_stats(values):
    centre = jnp.mean(values, axis=-1, keepdims=True)
    offsets = values - centre
    spread = jnp.mean(offsets * offsets, axis=-1, keepdims=True)
    inverse = lax.rsqrt(spread + EPS)
    return (offsets * inverse, inverse)


def norm_back(grad_normed, gain, unit_rows, inverse):
    scaled = grad_normed * gain
    return inverse * (
        scaled
        - jnp.mean(scaled, axis=-1, keepdims=True)
        - unit_rows * jnp.mean(scaled * unit_rows, axis=-1, keepdims=True)
    )


def dot(left, right, dims):
    return lax.dot_general(left, right, ((dims[:1], dims[1:]), ((), ())), preferred_element_type=F32)


def block_scores(queries, key_rows, start_row, stop_row, length):
    scores = dot(queries[start_row:stop_row], key_rows[:stop_row], (1, 1)) * HD ** (-0.5)
    query_index = start_row + jnp.arange(stop_row - start_row, dtype=jnp.int32)[:, None]
    key_index = jnp.arange(stop_row, dtype=jnp.int32)[None, :]
    return jnp.where((key_index <= query_index) & (key_index < length), scores, MASKED_SCORE)


def attend_forward(queries, key_rows, value_rows, length):
    seq_len = queries.shape[0]
    pieces = []
    totals = []
    for start_row in range(0, seq_len, 512):
        stop_row = start_row + 512
        scores = block_scores(queries, key_rows, start_row, stop_row, length)
        row_peak = jnp.max(scores, axis=-1, keepdims=True)
        log_total = jnp.log(jnp.sum(jnp.exp(scores - row_peak), axis=-1, keepdims=True)) + row_peak
        attn_probs = jnp.exp(scores - log_total).astype(BF)
        pieces.append(dot(attn_probs, value_rows[:stop_row], (1, 0)).astype(BF))
        totals.append(log_total)
    return (jnp.concatenate(pieces, axis=0), jnp.concatenate(totals, axis=0))


def attend_backward(queries, key_rows, value_rows, grad_attended, totals, length):
    seq_len = queries.shape[0]
    score_scale = HD ** (-0.5)
    grad_queries = []
    grad_keys = jnp.zeros(key_rows.shape, F32)
    grad_values = jnp.zeros(value_rows.shape, F32)
    for start_row in range(0, seq_len, 512):
        stop_row = start_row + 512
        scores = block_scores(queries, key_rows, start_row, stop_row, length)
        attn_probs = jnp.exp(scores - totals[start_row:stop_row])
        grad_probs = dot(grad_attended[start_row:stop_row], value_rows[:stop_row], (1, 1))
        centre = jnp.sum(attn_probs * grad_probs, axis=-1, keepdims=True)
        grad_scores = (attn_probs * (grad_probs - centre)).astype(BF)
        grad_queries.append(dot(grad_scores, key_rows[:stop_row], (1, 0)) * score_scale)
        grad_keys = grad_keys.at[:stop_row].add(
            dot(grad_scores, queries[start_row:stop_row], (0, 0)) * score_scale
        )
        grad_values = grad_values.at[:stop_row].add(
            dot(attn_probs.astype(BF), grad_attended[start_row:stop_row], (0, 0))
        )
    grad_queries = jnp.concatenate(grad_queries, axis=0)
    return (grad_queries.astype(BF), grad_keys.astype(BF), grad_values.astype(BF))


def gather_rows(rows):
    mine = jnp.concatenate([rows, z_up(rows), z_down(rows), z_far(rows)], axis=0)
    return mine, core_swap(mine)


def scatter_rows(mine, others):
    halves = (mine.astype(F32) + core_swap(others).astype(F32)).astype(BF)
    part = [halves[i * 128 : (i + 1) * 128] for i in range(4)]
    return (
        part[0].astype(F32)
        + z_down(part[1]).astype(F32)
        + z_up(part[2]).astype(F32)
        + z_far(part[3]).astype(F32)
    )


def take(values, index, size, axis):
    return lax.dynamic_slice_in_dim(values, index * size, size, axis)


def sum_along_y(values, y, axis):
    size = values.shape[axis] // 4
    parts = [take(values, (y + by) % 4, size, axis) for by in range(4)]
    return (
        parts[0].astype(F32)
        + y_up(parts[1]).astype(F32)
        + y_far(parts[2]).astype(F32)
        + y_down(parts[3]).astype(F32)
    )


def sum_along_x(own, partner, x_hi, x_lo, axis):
    size = own.shape[axis] // 2
    up_hi = jnp.where(x_lo == 0, x_hi, 1 - x_hi)
    return (
        take(own, x_hi, size, axis).astype(F32)
        + x_far(take(own, 1 - x_hi, size, axis)).astype(F32)
        + x_up(take(partner, up_hi, size, axis)).astype(F32)
        + x_down(take(partner, 1 - up_hi, size, axis)).astype(F32)
    )


def sum_of_all(values):
    for move in (core_swap, z_far, z_up, x_far, x_up, y_far, y_up):
        values = values + move(values)
    return values


def body(
    tokens,
    ln1_gain,
    ln1_shift,
    qkv_weight,
    out_weight,
    ln2_gain,
    ln2_shift,
    up_weight,
    down_weight,
    lengths,
    cotangent,
):
    batch, tensor = lax.axis_index("batch"), lax.axis_index("tensor")
    x_hi, y = batch // 4, batch % 4
    x_lo, z, core = tensor // 8, (tensor // 2) % 4, tensor % 2
    length = lengths[0]
    first_row = tensor * 128

    out_full = lax.all_gather(out_weight, "tensor", axis=0, tiled=True)
    live_rows = (first_row + jnp.arange(128, dtype=jnp.int32) < length).astype(F32)[:, None]
    incoming_rows = cotangent.astype(F32) * live_rows
    incoming = jnp.concatenate(gather_rows(incoming_rows.astype(BF)), axis=0)
    up_both = jnp.concatenate(
        [
            up_weight,
            jnp.concatenate([x_up(up_weight[:1024]), x_down(up_weight[1024:])], axis=0),
        ],
        axis=1,
    )
    down_both = jnp.concatenate(
        [down_weight, x_up(down_weight[:256]), x_down(down_weight[256:])], axis=0
    )

    inputs = tokens.astype(F32)
    unit_first, _ = norm_stats(inputs)
    normed_first = (unit_first * ln1_gain + ln1_shift).astype(BF)
    projected = jnp.einsum("td,cdh->cth", normed_first, qkv_weight, preferred_element_type=F32).astype(BF)
    attended, totals = attend_forward(projected[0], projected[1], projected[2], length)
    attended_rows = lax.all_to_all(attended, "tensor", 0, 1, tiled=True)
    branch_rows = dot(attended_rows, out_full, (1, 0))
    token_rows = take(tokens, tensor, 128, 0).astype(F32)
    middle_rows = token_rows + branch_rows
    unit_second, inverse_second = norm_stats(middle_rows)
    normed_rows = (unit_second * ln2_gain + ln2_shift).astype(BF)

    normed_second = jnp.concatenate(gather_rows(normed_rows), axis=0)
    hidden = dot(normed_second, up_both, (1, 0))
    activated, gelu_pull = jax.vjp(partial(jax.nn.gelu, approximate=True), hidden)
    activated = activated.astype(BF)
    grad_act = dot(incoming, down_both, (1, 1))
    grad_hidden = gelu_pull(grad_act)[0].astype(BF)
    grad_normed_part = dot(grad_hidden, up_both, (1, 1)).astype(BF)
    grad_normed_second = scatter_rows(grad_normed_part[:512], grad_normed_part[512:])

    mixed_part = dot(activated, down_both, (1, 0)).astype(BF)
    grad_down = dot(activated, incoming, (0, 0)).astype(BF)
    grad_up = dot(normed_second, grad_hidden, (0, 0)).astype(BF)

    grad_middle = incoming_rows + norm_back(grad_normed_second, ln2_gain, unit_second, inverse_second)
    gain_second = jnp.sum(grad_normed_second * unit_second, axis=0)
    shift_second = jnp.sum(grad_normed_second, axis=0)
    grad_branch = grad_middle.astype(BF)
    grad_attended = lax.all_to_all(dot(grad_branch, out_full, (1, 1)).astype(BF), "tensor", 1, 0, tiled=True)

    mixed_rows = scatter_rows(mixed_part[:512], mixed_part[512:])
    output = (middle_rows + mixed_rows).astype(BF)

    branch_back = jnp.concatenate(gather_rows(grad_branch), axis=0)
    order = [(0, 0), (-1, 0), (1, 0), (2, 0), (0, 1), (-1, 1), (1, 1), (2, 1)]
    spots = [((z + by) % 4) * 2 + (core + swap) % 2 for by, swap in order]
    own_half = jnp.concatenate([take(attended, x_lo * 8 + spot, 128, 0) for spot in spots], axis=0)
    sent_half = jnp.concatenate([take(attended, (1 - x_lo) * 8 + spot, 128, 0) for spot in spots], axis=0)
    both_heads = jnp.concatenate([own_half, x_pair(sent_half)], axis=1)
    grad_out = dot(both_heads, branch_back, (0, 0)).astype(BF)

    grad_queries, grad_keys, grad_values = attend_backward(
        projected[0], projected[1], projected[2], grad_attended, totals, length
    )
    stacked = jnp.stack([grad_queries, grad_keys, grad_values])
    grad_first_part = jnp.einsum("cth,cdh->td", stacked, qkv_weight, preferred_element_type=F32).astype(BF)
    grad_qkv_part = jnp.einsum("td,cth->cdh", normed_first, stacked, preferred_element_type=F32)

    columns = jnp.sum(stacked.astype(F32), axis=1)
    weights = qkv_weight.astype(F32)
    shift_first = jnp.sum(weights * columns[:, None, :], axis=(0, 2))
    gain_first = (jnp.sum(weights * grad_qkv_part, axis=(0, 2)) - ln1_shift * shift_first) / ln1_gain
    sums = sum_of_all(jnp.stack([gain_first, gain_second, shift_first, shift_second]))

    by_core = grad_first_part.reshape(8, 2, 128, 2048)
    kept = lax.dynamic_index_in_dim(by_core, core, 1, False)
    sent = lax.dynamic_index_in_dim(by_core, 1 - core, 1, False)
    halves = (kept.astype(F32) + core_swap(sent).astype(F32)).astype(BF).reshape(2, 4, 128, 2048)

    def over_x(values):
        return take(values, x_lo, 1, 0)[0].astype(F32) + x_pair(take(values, 1 - x_lo, 1, 0)[0]).astype(F32)

    def over_z(values):
        part = [lax.dynamic_index_in_dim(values, (z + by) % 4, values.ndim - 3, False) for by in range(4)]
        return (
            part[0].astype(F32)
            + z_up(part[1]).astype(F32)
            + z_far(part[2]).astype(F32)
            + z_down(part[3]).astype(F32)
        )

    left, right = halves[..., :1024], halves[..., 1024:]
    grad_normed_first = jnp.concatenate(
        [over_x(over_z(left).astype(BF)), over_z(over_x(right).astype(BF))], axis=-1
    )
    unit_rows, inverse_rows = norm_stats(token_rows)
    grad_tokens = (grad_middle + norm_back(grad_normed_first, ln1_gain, unit_rows, inverse_rows)).astype(BF)

    grad_down = sum_along_y(
        sum_along_x(grad_down[:512], grad_down[512:], x_hi, x_lo, 1).astype(BF), y, 1
    )
    up_sums = sum_along_y(grad_up.reshape(2, 4, 256, 1024), y, 1)[:, 0].astype(BF)
    up_sums = up_sums.reshape(512, 1024)
    grad_up = sum_along_x(up_sums[:, :512], up_sums[:, 512:], x_hi, x_lo, 0)
    grad_out = sum_along_y(
        sum_along_x(grad_out[:128], grad_out[128:], x_hi, x_lo, 1).astype(BF), y, 1
    )
    qkv_sums = sum_along_y(grad_qkv_part.astype(BF).reshape(3, 2, 4, 256, 128), y, 2)[:, :, 0].astype(BF)
    grad_qkv = lax.dynamic_index_in_dim(qkv_sums, x_hi, 1, False).astype(F32) + x_far(
        lax.dynamic_index_in_dim(qkv_sums, 1 - x_hi, 1, False)
    ).astype(F32)
    return (output, grad_tokens, grad_qkv, grad_out, grad_up, grad_down, sums[:2], sums[2:])


def solution(mesh):
    return jax.shard_map(
        body,
        mesh=mesh,
        in_specs=(
            P("batch", None),
            P(),
            P(),
            P(None, None, "tensor"),
            P("tensor", None),
            P(),
            P(),
            P(None, "tensor"),
            P("tensor", None),
            P("batch"),
            P(("batch", "tensor"), None),
        ),
        out_specs=(
            P(("batch", "tensor"), None),
            P(("batch", "tensor"), None),
            P(None, "batch", "tensor"),
            P("tensor", "batch"),
            P("batch", "tensor"),
            P("tensor", "batch"),
            P(),
            P(),
        ),
        check_vma=False,
    )
```

time: 1010 us -> 526 us (0.52)
  waiting for transfers between devices: 729 us -> 191 us
  starting transfers between devices: 0.8 us -> 93.8 us
  local copies, waits for them, and re-layouts: 12.8 us -> 77.7 us
  blocking collectives: 64.4 us -> 0 us
  matrix products: 115 us -> 87.9 us
  other arithmetic: 66.4 us -> 52.5 us
    reduce_scatter x6 -> x0, waiting for transfers between devices: 410 us -> none  [the longest x1 75.5 us: body(): lax.psum_scatter(grad_up.astype(jnp.bfloat16), 'batch', scatter_dimension...]
    psum x2 -> x0, waiting for transfers between devices: 286 us -> none  [the longest x1 143 us: body(): lax.psum(jnp.dot(attended_flat, out_weight, preferred_element_type=jnp.fl...]
    ppermute x0 -> x63, waiting for transfers between devices: none -> 165 us  [mover(): return lambda values: lax.ppermute(values, ('batch', 'tensor'), pairs)]
    ppermute x0 -> x63, starting transfers between devices: none -> 85.3 us  [mover(): return lambda values: lax.ppermute(values, ('batch', 'tensor'), pairs)]
    psum x1 -> x0, blocking collectives: 64.4 us -> none  [body(): lax.psum((jnp.stack([gain_first, gain_second]), jnp.stack([shift_first, s...]
    unnamed x87 -> x141, local copies, waits for them, and re-layouts: 11.7 us -> 44.6 us
    mul x2 -> x0, other arithmetic: 29.1 us -> none  [norm_stats(): return (offsets * inverse, inverse)]
    dot_general x35, matrix products: 110 us -> 82.7 us  [the longest x33 72.3 us: dot(): lax.dot_general(left, right, ((dims[:1], dims[1:]), ((), ())), preferred_...]
  transfers between devices with their start and end apart: 10 -> 66, of which waited for: 10 -> 25; matrix products, arithmetic and copies ran while one was open for 12% -> 34% of each run, Pallas kernels for 0% -> 0%
where the time goes in v1:
time: 526 us; the launch traced here: 520 us
  waiting for transfers between devices  191 us (36%)
  starting transfers between devices  93.8 us (18%)
  matrix products  87.9 us (17%)
  local copies, waits for them, and re-layouts  77.7 us (15%)
  other arithmetic  52.5 us (10%)
  between operations  16.5 us (3%)
    ppermute x63, waiting for transfers between devices, mover(): return lambda values: lax.ppermute(values, ('batch', 'tensor'), pairs)  165 us
    ppermute x63, starting transfers between devices, mover(): return lambda values: lax.ppermute(values, ('batch', 'tensor'), pairs)  85.3 us
    dot_general x33, matrix products, dot(): lax.dot_general(left, right, ((dims[:1], dims[1:]), ((), ())), preferred_...  72.3 us
    unnamed x141, local copies, waits for them, and re-layouts  44.6 us
    all_gather x1, waiting for transfers between devices, body(): out_full = lax.all_gather(out_weight, 'tensor', axis=0, tiled=True)  25.6 us
    dynamic_slice x10, local copies, waits for them, and re-layouts, take(): return lax.dynamic_slice_in_dim(values, index * size, size, axis)  12.2 us
  transfers between devices with their start and end apart: 66, of which 25 were waited for; matrix products, arithmetic and copies ran while one was open for 34% of the time, Pallas kernels for 0%

profile of v1, /device:TPU:0, one launch (start us, length us, event | category | flops | bytes accessed | tf_op | source)
XLA Modules:
  0.0 519.6 jit_solution(6290381174093674751)
XLA Ops:
  16.8 4.7 convert_reduce_fusion
  25.3 5.2 %fusion.21 = bf16[3,2048,128]{2,1,0:T(8,128)(2,1)S(1)} fusion(bf16[3,2048,128]{2,1,0:T(8,128)(2,1)S(1)} %copy-done.18, bf16[2048,2048]{1,0:T(8,128)(2,1)S(1)} %copy-done.4, f32[2048]{0:T(1024)S(1)} %copy-done.40, f32[2048]{0:T(1024)S(1)} %copy-done.25, f32[2048]{0:T(1024)S(1)} %add_rsqrt_fusion, f32[2048]{0:T(1024)S(1)} %broadcast_multiply_fusion), kind=kOutput, calls=%fused_computation.53 | convolution fusion | flops 3247177728 | bytes 11567104 | tf_op jit(solution)/shard_map/td,cdh->cth/dot_general | solution.py:205
  72.0 25.6 %all-gather.2.cloned.1.call-done = bf16[2048,2048]{1,0:T(8,128)(2,1)} async-done(((bf16[128,2048]{1,0:T(8,128)(2,1)}), bf16[2048,2048]{1,0:T(8,128)(2,1)}) %all-gather.2.cloned.1.call-update) | async-done | bytes 8388624 | tf_op jit(solution)/shard_map/all_gather | solution.py:187
  97.6 5.1 fusion.105
  110.0 8.9 %collective-permute-done = bf16[128,2048]{1,0:T(8,128)(2,1)S(1)} collective-permute-done((bf16[128,2048]{1,0:T(8,128)(2,1)S(1)}, bf16[128,2048]{1,0:T(8,128)(2,1)S(1)}, u32[]{:S(2)}, u32[]{:S(2)}) %collective-permute-start) | collective-permute-done | bytes 524320 | tf_op jit(solution)/shard_map/ppermute | solution.py:27
  118.9 5.8 %collective-permute-start.5 = (bf16[1024,512]{1,0:T(8,128)(2,1)S(1)}, bf16[1024,512]{1,0:T(8,128)(2,1)S(1)}, u32[]{:S(2)}, u32[]{:S(2)}) collective-permute-start(bf16[1024,512]{1,0:T(8,128)(2,1)S(1)} %get-tuple-element.155), channel_id=1, source_target_pairs={{0,72},{1,73},{2,74},{3,75},{4,76},{5,77},{6,78},{7,79},{8,0},{9,1... | collective-permute-start | bytes 3145736 | tf_op jit(solution)/shard_map/ppermute | solution.py:27
  128.9 5.8 %collective-permute-start.7 = (bf16[256,2048]{1,0:T(8,128)(2,1)S(1)}, bf16[256,2048]{1,0:T(8,128)(2,1)S(1)}, u32[]{:S(2)}, u32[]{:S(2)}) collective-permute-start(bf16[256,2048]{1,0:T(8,128)(2,1)S(1)} %copy-done.22), channel_id=1, source_target_pairs={{0,72},{1,73},{2,74},{3,75},{4,76},{5,77},{6,78},{7,79},{8,0},{9,1... | collective-permute-start | bytes 3145736 | tf_op jit(solution)/shard_map/ppermute | solution.py:27
  139.7 29.0 %collective-permute-done.7 = bf16[256,2048]{1,0:T(8,128)(2,1)S(1)} collective-permute-done((bf16[256,2048]{1,0:T(8,128)(2,1)S(1)}, bf16[256,2048]{1,0:T(8,128)(2,1)S(1)}, u32[]{:S(2)}, u32[]{:S(2)}) %collective-permute-start.7) | collective-permute-done | bytes 1048608 | tf_op jit(solution)/shard_map/ppermute | solution.py:27
  178.7 5.3 %convolution_convert_fusion.3 = bf16[1024,2048]{1,0:T(8,128)(2,1)S(1)} fusion(bf16[1024,2048]{1,0:T(8,128)(2,1)S(1)} %constant_dynamic-update-slice_fusion.5, f32[1024,1024]{1,0:T(8,128)S(1)} %fusion.36), kind=kOutput, calls=%fused_computation.38 | convolution fusion | flops 4306501632 | bytes 12582912 | tf_op jit(solution)/shard_map/dot_general | solution.py:71
  184.0 7.0 %fusion.14 = bf16[1024,1024]{1,0:T(8,128)(2,1)S(1)} fusion(f32[1024,1024]{1,0:T(8,128)S(1)} %fusion.36, bf16[1024,2048]{1,0:T(8,128)(2,1)S(1)} %constant_dynamic-update-slice_fusion.8, bf16[1024,2048]{1,0:T(8,128)(2,1)S(1)} %constant_dynamic-update-slice_fusion.5), kind=kOutput, calls=%fused_computation.20 | convolution fusion | flops 4315938816 | bytes 14680064 | tf_op jit(solution)/shard_map/dot_general | solution.py:71
  192.4 10.1 %convolution_convert_fusion.2 = bf16[1024,2048]{1,0:T(8,128)(2,1)S(1)} fusion(bf16[1024,1024]{1,0:T(8,128)(2,1)S(1)} %fusion.14, bf16[1024,512]{1,0:T(8,128)(2,1)S(1)} %copy-done.50, bf16[1024,512]{1,0:T(8,128)(2,1)S(1)} %collective-permute-done.4, bf16[2048,512]{1,0:T(8,128)(2,1)S(1)} %copy-done.15), kind=kOutput, calls=%fused_computation.37 | convolution fusion | flops 4309647360 | bytes 10485760 | tf_op jit(solution)/shard_map/dot_general | solution.py:71
  204.8 7.9 %convolution_convert_fusion = bf16[1024,2048]{1,0:T(8,128)(2,1)S(1)} fusion(bf16[1024,2048]{1,0:T(8,128)(2,1)S(1)} %copy-done.30, f32[1024,1024]{1,0:T(8,128)} %copy-done.51), kind=kOutput, calls=%fused_computation.35 | convolution fusion | flops 4306501632 | bytes 12582912 | tf_op jit(solution)/shard_map/dot_general | solution.py:71
  214.9 6.4 %convolution_convert_fusion.1 = bf16[2048,1024]{1,0:T(8,128)(2,1)S(1)} fusion(bf16[1024,2048]{1,0:T(8,128)(2,1)S(1)} %copy-done.32, bf16[1024,1024]{1,0:T(8,128)(2,1)} %copy-done.52), kind=kOutput, calls=%fused_computation.36 | convolution fusion | flops 4297064448 | bytes 10485760 | tf_op jit(solution)/shard_map/dot_general | solution.py:71
  234.5 35.4 %collective-permute-done.46 = bf16[2,1,256,1024]{3,2,1,0:T(8,128)(2,1)S(1)} collective-permute-done((bf16[2,1,256,1024]{3,2,1,0:T(8,128)(2,1)}, bf16[2,1,256,1024]{3,2,1,0:T(8,128)(2,1)S(1)}, u32[]{:S(2)}, u32[]{:S(2)}) %collective-permute-start.46) | collective-permute-done | bytes 1048608 | tf_op jit(solution)/shard_map/ppermute | solution.py:27
  288.6 4.5 collective-permute-done.10
  309.8 21.6 %collective-permute-done.52 = bf16[512,1024]{1,0:T(8,128)(2,1)} collective-permute-done((bf16[512,1024]{1,0:T(8,128)(2,1)}, bf16[512,1024]{1,0:T(8,128)(2,1)}, u32[]{:S(2)}, u32[]{:S(2)}) %collective-permute-start.52) | collective-permute-done | bytes 1048608 | tf_op jit(solution)/shard_map/ppermute | solution.py:27
  340.1 4.8 collective-permute-start.55
  372.0 5.0 bitcast_convert_fusion
  377.1 5.4 %bitcast_convert_fusion.1 = (bf16[3,2048,128]{1,2,0:T(8,128)(2,1)}, f32[3,128,2048]{2,1,0:T(8,128)S(1)}) fusion(bf16[2048,2048]{1,0:T(8,128)(2,1)S(1)} %bitcast.201, f32[2048]{0:T(1024)S(1)} %copy-done.41, f32[2048]{0:T(1024)S(1)} %copy-done.26, f32[2048]{0:T(1024)S(1)} %copy-done.43, f32[2048]{0:T(1024)S(1)} %copy-done.38, ...), kind=kOutput, calls=%fused_computation.44 | convolution fusion | flops 3256614912 | bytes 14712832 | tf_op jit(solution)/shard_map/td,cth->cdh/dot_general | solution.py:249
  397.3 4.7 collective-permute-done.53
  407.7 5.1 constant_dynamic-slice_fusion.21
  440.3 9.5 %collective-permute-done.29 = bf16[3,2,1,256,128]{4,3,0,2,1:T(8,128)(2,1)S(1)} collective-permute-done((bf16[3,2,1,256,128]{4,3,0,2,1:T(8,128)(2,1)S(1)}, bf16[3,2,1,256,128]{4,3,0,2,1:T(8,128)(2,1)S(1)}, u32[]{:S(2)}, u32[]{:S(2)}) %collective-permute-start.29) | collective-permute-done | bytes 393248 | tf_op jit(solution)/shard_map/ppermute | solution.py:27
  476.2 6.7 %collective-permute-done.23 = bf16[2,128,1024]{2,1,0:T(8,128)(2,1)S(1)} collective-permute-done((bf16[2,128,1024]{2,1,0:T(8,128)(2,1)S(1)}, bf16[2,128,1024]{2,1,0:T(8,128)(2,1)S(1)}, u32[]{:S(2)}, u32[]{:S(2)}) %collective-permute-start.23) | collective-permute-done | bytes 524320 | tf_op jit(solution)/shard_map/ppermute | solution.py:27
  485.9 5.8 %collective-permute-done.21 = bf16[2,128,1024]{2,1,0:T(8,128)(2,1)S(1)} collective-permute-done((bf16[2,128,1024]{2,1,0:T(8,128)(2,1)S(1)}, bf16[2,128,1024]{2,1,0:T(8,128)(2,1)S(1)}, u32[]{:S(2)}, u32[]{:S(2)}) %collective-permute-start.21) | collective-permute-done | bytes 524320 | tf_op jit(solution)/shard_map/ppermute | solution.py:27
  (397 shorter events, 267.7 us)
Async XLA Ops:
  7.2 90.4 %all-gather.2.cloned.1.call-start = ((), (), s32[]{:S(2)}) async-start(), calls=%async_computation.2 | async-start | bytes 8912896 | tf_op jit(solution)/shard_map/all_gather | solution.py:187
  10.7 58.1 %collective-permute-start.12 = (bf16[128,2048]{1,0:T(8,128)(2,1)}, bf16[128,2048]{1,0:T(8,128)(2,1)}, u32[]{:S(2)}, u32[]{:S(2)}) collective-permute-start(bf16[128,2048]{1,0:T(8,128)(2,1)} %get-tuple-element.133), channel_id=1, source_target_pairs={{0,2},{1,3},{2,4},{3,5},{4,6},{5,7},{6,0},{7,1},{8,10},{9,11},{10,... | collective-permute-start | bytes 1572872 | tf_op jit(solution)/shard_map/ppermute | solution.py:27
  12.7 56.2 %collective-permute-start.13 = (bf16[128,2048]{1,0:T(8,128)(2,1)}, bf16[128,2048]{1,0:T(8,128)(2,1)}, u32[]{:S(2)}, u32[]{:S(2)}) collective-permute-start(bf16[128,2048]{1,0:T(8,128)(2,1)} %get-tuple-element.133), channel_id=1, source_target_pairs={{0,6},{1,7},{2,0},{3,1},{4,2},{5,3},{6,4},{7,5},{8,14},{9,15},{10,... | collective-permute-start | bytes 1572872 | tf_op jit(solution)/shard_map/ppermute | solution.py:27
  14.8 54.0 %collective-permute-start.14 = (bf16[128,2048]{1,0:T(8,128)(2,1)}, bf16[128,2048]{1,0:T(8,128)(2,1)}, u32[]{:S(2)}, u32[]{:S(2)}) collective-permute-start(bf16[128,2048]{1,0:T(8,128)(2,1)} %get-tuple-element.133), channel_id=1, source_target_pairs={{0,4},{1,5},{2,6},{3,7},{4,0},{5,1},{6,2},{7,3},{8,12},{9,13},{10,... | collective-permute-start | bytes 1572872 | tf_op jit(solution)/shard_map/ppermute | solution.py:27
  48.7 89.6 %collective-permute-start.6 = (bf16[256,2048]{1,0:T(8,128)(2,1)}, bf16[256,2048]{1,0:T(8,128)(2,1)}, u32[]{:S(2)}, u32[]{:S(2)}) collective-permute-start(bf16[256,2048]{1,0:T(8,128)(2,1)} %get-tuple-element.157), channel_id=1, source_target_pairs={{0,8},{1,9},{2,10},{3,11},{4,12},{5,13},{6,14},{7,15},{8,64},{9,65... | collective-permute-start | bytes 3145736 | tf_op jit(solution)/shard_map/ppermute | solution.py:27
  72.0 96.7 %collective-permute-start.15 = (bf16[512,2048]{1,0:T(8,128)(2,1)}, bf16[512,2048]{1,0:T(8,128)(2,1)}, u32[]{:S(2)}, u32[]{:S(2)}) collective-permute-start(bf16[512,2048]{1,0:T(8,128)(2,1)} %pad_maximum_fusion.1), channel_id=1, source_target_pairs={{0,1},{1,0},{2,3},{3,2},{4,5},{5,4},{6,7},{7,6},{8,9},{9,8},{10,11... | collective-permute-start | bytes 6291464 | tf_op jit(solution)/shard_map/ppermute | solution.py:27
  118.9 52.2 %collective-permute-start.5 = (bf16[1024,512]{1,0:T(8,128)(2,1)S(1)}, bf16[1024,512]{1,0:T(8,128)(2,1)S(1)}, u32[]{:S(2)}, u32[]{:S(2)}) collective-permute-start(bf16[1024,512]{1,0:T(8,128)(2,1)S(1)} %get-tuple-element.155), channel_id=1, source_target_pairs={{0,72},{1,73},{2,74},{3,75},{4,76},{5,77},{6,78},{7,79},{8,0},{9,1... | collective-permute-start | bytes 3145736 | tf_op jit(solution)/shard_map/ppermute | solution.py:27
  128.9 39.7 %collective-permute-start.7 = (bf16[256,2048]{1,0:T(8,128)(2,1)S(1)}, bf16[256,2048]{1,0:T(8,128)(2,1)S(1)}, u32[]{:S(2)}, u32[]{:S(2)}) collective-permute-start(bf16[256,2048]{1,0:T(8,128)(2,1)S(1)} %copy-done.22), channel_id=1, source_target_pairs={{0,72},{1,73},{2,74},{3,75},{4,76},{5,77},{6,78},{7,79},{8,0},{9,1... | collective-permute-start | bytes 3145736 | tf_op jit(solution)/shard_map/ppermute | solution.py:27
  223.1 46.8 %collective-permute-start.46 = (bf16[2,1,256,1024]{3,2,1,0:T(8,128)(2,1)}, bf16[2,1,256,1024]{3,2,1,0:T(8,128)(2,1)S(1)}, u32[]{:S(2)}, u32[]{:S(2)}) collective-permute-start(bf16[2,1,256,1024]{3,2,1,0:T(8,128)(2,1)} %get-tuple-element.139), channel_id=1, source_target_pairs={{0,48},{1,49},{2,50},{3,51},{4,52},{5,53},{6,54},{7,55},{8,56},{9,... | collective-permute-start | bytes 3145736 | tf_op jit(solution)/shard_map/ppermute | solution.py:27
  225.9 44.9 %collective-permute-start.45 = (bf16[2,1,256,1024]{3,2,1,0:T(8,128)(2,1)}, bf16[2,1,256,1024]{3,2,1,0:T(8,128)(2,1)}, u32[]{:S(2)}, u32[]{:S(2)}) collective-permute-start(bf16[2,1,256,1024]{3,2,1,0:T(8,128)(2,1)} %get-tuple-element.140), channel_id=1, source_target_pairs={{0,32},{1,33},{2,34},{3,35},{4,36},{5,37},{6,38},{7,39},{8,40},{9,... | collective-permute-start | bytes 3145736 | tf_op jit(solution)/shard_map/ppermute | solution.py:27
  226.7 47.0 %collective-permute-start.44 = (bf16[2,1,256,1024]{3,2,1,0:T(8,128)(2,1)}, bf16[2,1,256,1024]{3,2,1,0:T(8,128)(2,1)}, u32[]{:S(2)}, u32[]{:S(2)}) collective-permute-start(bf16[2,1,256,1024]{3,2,1,0:T(8,128)(2,1)} %get-tuple-element.138), channel_id=1, source_target_pairs={{0,16},{1,17},{2,18},{3,19},{4,20},{5,21},{6,22},{7,23},{8,24},{9,... | collective-permute-start | bytes 3145736 | tf_op jit(solution)/shard_map/ppermute | solution.py:27
  231.8 41.8 %collective-permute-start.19 = (bf16[128,2048]{1,0:T(8,128)(2,1)S(1)}, bf16[128,2048]{1,0:T(8,128)(2,1)S(1)}, u32[]{:S(2)}, u32[]{:S(2)}) collective-permute-start(bf16[128,2048]{1,0:T(8,128)(2,1)S(1)} %get-tuple-element.149), channel_id=1, source_target_pairs={{0,4},{1,5},{2,6},{3,7},{4,0},{5,1},{6,2},{7,3},{8,12},{9,13},{10,... | collective-permute-start | bytes 1572872 | tf_op jit(solution)/shard_map/ppermute | solution.py:27
  231.9 49.0 %collective-permute-start.18 = (bf16[128,2048]{1,0:T(8,128)(2,1)S(1)}, bf16[128,2048]{1,0:T(8,128)(2,1)S(1)}, u32[]{:S(2)}, u32[]{:S(2)}) collective-permute-start(bf16[128,2048]{1,0:T(8,128)(2,1)S(1)} %get-tuple-element.150), channel_id=1, source_target_pairs={{0,2},{1,3},{2,4},{3,5},{4,6},{5,7},{6,0},{7,1},{8,10},{9,11},{10,... | collective-permute-start | bytes 1572872 | tf_op jit(solution)/shard_map/ppermute | solution.py:27
  280.9 50.5 %collective-permute-start.52 = (bf16[512,1024]{1,0:T(8,128)(2,1)}, bf16[512,1024]{1,0:T(8,128)(2,1)}, u32[]{:S(2)}, u32[]{:S(2)}) collective-permute-start(bf16[512,1024]{1,0:T(8,128)(2,1)} %get-tuple-element.144), channel_id=1, source_target_pairs={{0,72},{1,73},{2,74},{3,75},{4,76},{5,77},{6,78},{7,79},{8,0},{9,1... | collective-permute-start | bytes 3145736 | tf_op jit(solution)/shard_map/ppermute | solution.py:27
  285.0 50.1 %collective-permute-start.51 = (bf16[512,1024]{1,0:T(8,128)(2,1)}, bf16[512,1024]{1,0:T(8,128)(2,1)}, u32[]{:S(2)}, u32[]{:S(2)}) collective-permute-start(bf16[512,1024]{1,0:T(8,128)(2,1)} %get-tuple-element.143), channel_id=1, source_target_pairs={{0,8},{1,9},{2,10},{3,11},{4,12},{5,13},{6,14},{7,15},{8,64},{9,65... | collective-permute-start | bytes 3145736 | tf_op jit(solution)/shard_map/ppermute | solution.py:27
  286.4 48.7 %collective-permute-start.50 = (bf16[512,1024]{1,0:T(8,128)(2,1)}, bf16[512,1024]{1,0:T(8,128)(2,1)}, u32[]{:S(2)}, u32[]{:S(2)}) collective-permute-start(bf16[512,1024]{1,0:T(8,128)(2,1)} %constant_dynamic-slice_fusion.5), channel_id=1, source_target_pairs={{0,64},{1,65},{2,66},{3,67},{4,68},{5,69},{6,70},{7,71},{8,72},{9,... | collective-permute-start | bytes 3145736 | tf_op jit(solution)/shard_map/ppermute | solution.py:27
  293.2 51.8 %collective-permute-start.49 = (bf16[256,512]{1,0:T(8,128)(2,1)}, bf16[256,512]{1,0:T(8,128)(2,1)}, u32[]{:S(2)}, u32[]{:S(2)}) collective-permute-start(bf16[256,512]{1,0:T(8,128)(2,1)} %get-tuple-element.174), channel_id=1, source_target_pairs={{0,72},{1,73},{2,74},{3,75},{4,76},{5,77},{6,78},{7,79},{8,0},{9,1... | collective-permute-start | bytes 786440 | tf_op jit(solution)/shard_map/ppermute | solution.py:27
  296.9 48.1 %collective-permute-start.48 = (bf16[256,512]{1,0:T(8,128)(2,1)}, bf16[256,512]{1,0:T(8,128)(2,1)}, u32[]{:S(2)}, u32[]{:S(2)}) collective-permute-start(bf16[256,512]{1,0:T(8,128)(2,1)} %get-tuple-element.173), channel_id=1, source_target_pairs={{0,8},{1,9},{2,10},{3,11},{4,12},{5,13},{6,14},{7,15},{8,64},{9,65... | collective-permute-start | bytes 786440 | tf_op jit(solution)/shard_map/ppermute | solution.py:27
  305.5 48.5 %all-to-all-start.1 = ((bf16[128,16,128]{2,0,1:T(8,128)(2,1)}), bf16[128,16,128]{2,0,1:T(8,128)(2,1)}, u32[]{:S(2)}, u32[]{:S(2)}) async-start(bf16[128,16,128]{2,0,1:T(8,128)(2,1)} %bitcast.211), calls=%async_computation.1 | async-start | bytes 1048576 | tf_op jit(solution)/shard_map/all_to_all | solution.py:231
  340.1 54.0 %collective-permute-start.55 = (bf16[512,256]{1,0:T(8,128)(2,1)}, bf16[512,256]{1,0:T(8,128)(2,1)}, u32[]{:S(2)}, u32[]{:S(2)}) collective-permute-start(bf16[512,256]{1,0:T(8,128)(2,1)} %get-tuple-element.163), channel_id=1, source_target_pairs={{0,48},{1,49},{2,50},{3,51},{4,52},{5,53},{6,54},{7,55},{8,56},{9,... | collective-permute-start | bytes 786440 | tf_op jit(solution)/shard_map/ppermute | solution.py:27
  350.6 35.8 %collective-permute-start.34 = (bf16[128,2048]{1,0:T(8,128)(2,1)}, bf16[128,2048]{1,0:T(8,128)(2,1)}, u32[]{:S(2)}, u32[]{:S(2)}) collective-permute-start(bf16[128,2048]{1,0:T(8,128)(2,1)} %get-tuple-element.129), channel_id=1, source_target_pairs={{0,2},{1,3},{2,4},{3,5},{4,6},{5,7},{6,0},{7,1},{8,10},{9,11},{10,... | collective-permute-start | bytes 1572872 | tf_op jit(solution)/shard_map/ppermute | solution.py:27
  350.6 36.7 %collective-permute-start.35 = (bf16[128,2048]{1,0:T(8,128)(2,1)}, bf16[128,2048]{1,0:T(8,128)(2,1)}, u32[]{:S(2)}, u32[]{:S(2)}) collective-permute-start(bf16[128,2048]{1,0:T(8,128)(2,1)} %get-tuple-element.129), channel_id=1, source_target_pairs={{0,6},{1,7},{2,0},{3,1},{4,2},{5,3},{6,4},{7,5},{8,14},{9,15},{10,... | collective-permute-start | bytes 1572872 | tf_op jit(solution)/shard_map/ppermute | solution.py:27
  385.9 76.9 %collective-permute-start.20 = (bf16[8,128,2048]{2,1,0:T(8,128)(2,1)}, bf16[8,128,2048]{2,1,0:T(8,128)(2,1)}, u32[]{:S(2)}, u32[]{:S(2)}) collective-permute-start(bf16[8,128,2048]{2,1,0:T(8,128)(2,1)} %dynamic-slice_bitcast_fusion), channel_id=1, source_target_pairs={{0,1},{1,0},{2,3},{3,2},{4,5},{5,4},{6,7},{7,6},{8,9},{9,8},{10,11... | collective-permute-start | bytes 12582920 | tf_op jit(solution)/shard_map/ppermute | solution.py:27
  394.1 57.6 %collective-permute-start.37 = (bf16[512,2048]{1,0:T(8,128)(2,1)}, bf16[512,2048]{1,0:T(8,128)(2,1)}, u32[]{:S(2)}, u32[]{:S(2)}) collective-permute-start(bf16[512,2048]{1,0:T(8,128)(2,1)} %pad_maximum_fusion.2), channel_id=1, source_target_pairs={{0,1},{1,0},{2,3},{3,2},{4,5},{5,4},{6,7},{7,6},{8,9},{9,8},{10,11... | collective-permute-start | bytes 6291464 | tf_op jit(solution)/shard_map/ppermute | solution.py:27
  (101 other events, 1825.2 us)
Sparse Core Ops, SparseCore 0:
  9.7 87.8 all-gather.1

commit v2 on v1

v2 whole, which is shorter than its diff:
```python
from functools import partial

import jax
import jax.numpy as jnp
from jax import lax
from jax.sharding import Mesh
from jax.sharding import PartitionSpec as P

HD = 128
EPS = 1e-05
MASKED_SCORE = -1e30
BF = jnp.bfloat16
F32 = jnp.float32


AXES = ("x_hi", "y", "x_lo", "z", "core")
BATCH, TENSOR = AXES[:2], AXES[2:]


def core_swap(values):
    return lax.ppermute(values, "core", [(0, 1), (1, 0)])


def x_pair(values):
    return lax.ppermute(values, "x_lo", [(0, 1), (1, 0)])


def x_partner(values):
    pairs = [(r * 2 + c, ((r + (1, -1)[c]) % 4) * 2 + c) for r in range(4) for c in range(2)]
    return lax.ppermute(values, ("x_hi", "x_lo", "core"), pairs)


def exchange(values, axes):
    return lax.all_to_all(values, axes, 0, 0)


def spread(values, axes, count=4):
    return exchange(jnp.broadcast_to(values[None], (count, *values.shape)), axes)


def total(values):
    return jnp.sum(values.astype(F32), axis=0)


def norm_stats(values):
    centre = jnp.mean(values, axis=-1, keepdims=True)
    offsets = values - centre
    spread = jnp.mean(offsets * offsets, axis=-1, keepdims=True)
    inverse = lax.rsqrt(spread + EPS)
    return (offsets * inverse, inverse)


def norm_back(grad_normed, gain, unit_rows, inverse):
    scaled = grad_normed * gain
    return inverse * (
        scaled
        - jnp.mean(scaled, axis=-1, keepdims=True)
        - unit_rows * jnp.mean(scaled * unit_rows, axis=-1, keepdims=True)
    )


def dot(left, right, dims):
    return lax.dot_general(left, right, ((dims[:1], dims[1:]), ((), ())), preferred_element_type=F32)


def block_scores(queries, key_rows, start_row, stop_row, length):
    scores = dot(queries[start_row:stop_row], key_rows[:stop_row], (1, 1)) * HD ** (-0.5)
    query_index = start_row + jnp.arange(stop_row - start_row, dtype=jnp.int32)[:, None]
    key_index = jnp.arange(stop_row, dtype=jnp.int32)[None, :]
    return jnp.where((key_index <= query_index) & (key_index < length), scores, MASKED_SCORE)


def attend_forward(queries, key_rows, value_rows, length):
    seq_len = queries.shape[0]
    pieces = []
    totals = []
    for start_row in range(0, seq_len, 512):
        stop_row = start_row + 512
        scores = block_scores(queries, key_rows, start_row, stop_row, length)
        row_peak = jnp.max(scores, axis=-1, keepdims=True)
        log_total = jnp.log(jnp.sum(jnp.exp(scores - row_peak), axis=-1, keepdims=True)) + row_peak
        attn_probs = jnp.exp(scores - log_total).astype(BF)
        pieces.append(dot(attn_probs, value_rows[:stop_row], (1, 0)).astype(BF))
        totals.append(log_total)
    return (jnp.concatenate(pieces, axis=0), jnp.concatenate(totals, axis=0))


def attend_backward(queries, key_rows, value_rows, grad_attended, totals, length):
    seq_len = queries.shape[0]
    score_scale = HD ** (-0.5)
    grad_queries = []
    grad_keys = jnp.zeros(key_rows.shape, F32)
    grad_values = jnp.zeros(value_rows.shape, F32)
    for start_row in range(0, seq_len, 512):
        stop_row = start_row + 512
        scores = block_scores(queries, key_rows, start_row, stop_row, length)
        attn_probs = jnp.exp(scores - totals[start_row:stop_row])
        grad_probs = dot(grad_attended[start_row:stop_row], value_rows[:stop_row], (1, 1))
        centre = jnp.sum(attn_probs * grad_probs, axis=-1, keepdims=True)
        grad_scores = (attn_probs * (grad_probs - centre)).astype(BF)
        grad_queries.append(dot(grad_scores, key_rows[:stop_row], (1, 0)) * score_scale)
        grad_keys = grad_keys.at[:stop_row].add(
            dot(grad_scores, queries[start_row:stop_row], (0, 0)) * score_scale
        )
        grad_values = grad_values.at[:stop_row].add(
            dot(attn_probs.astype(BF), grad_attended[start_row:stop_row], (0, 0))
        )
    grad_queries = jnp.concatenate(grad_queries, axis=0)
    return (grad_queries.astype(BF), grad_keys.astype(BF), grad_values.astype(BF))


def gather_rows(rows):
    mine = spread(rows, "z").reshape(512, rows.shape[1])
    return jnp.concatenate([mine, core_swap(mine)], axis=0)


def scatter_rows(partial_sums):
    mine, others = partial_sums[:512], partial_sums[512:]
    halves = (mine.astype(F32) + core_swap(others).astype(F32)).astype(BF)
    return total(exchange(halves.reshape(4, 128, 2048), "z"))


def pick(values, index, axis):
    return lax.dynamic_index_in_dim(values, index, axis, False)


def sum_of_all(values):
    values = values + core_swap(values)
    for axes in ("z", ("x_hi", "x_lo"), "y"):
        values = total(spread(values, axes))
    return values


def body(
    tokens,
    ln1_gain,
    ln1_shift,
    qkv_weight,
    out_weight,
    ln2_gain,
    ln2_shift,
    up_weight,
    down_weight,
    lengths,
    cotangent,
):
    x_hi, y, x_lo, z, core = (lax.axis_index(axis) for axis in AXES)
    tensor = x_lo * 8 + z * 2 + core
    length = lengths[0]

    out_groups = []
    for half in range(2):
        mine = spread(out_weight[:, half * 1024 : (half + 1) * 1024], "z").reshape(512, 1024)
        both = [mine, x_partner(mine)]
        out_groups.append([group for part in both for group in (part, core_swap(part))])
    live_rows = (tensor * 128 + jnp.arange(128, dtype=jnp.int32) < length).astype(F32)[:, None]
    incoming_rows = cotangent.astype(F32) * live_rows
    up_both = jnp.concatenate([up_weight, x_partner(up_weight)], axis=1)
    down_both = jnp.concatenate([down_weight, x_partner(down_weight)], axis=0)
    incoming = gather_rows(incoming_rows.astype(BF))

    inputs = tokens.astype(F32)
    unit_first, _ = norm_stats(inputs)
    normed_first = (unit_first * ln1_gain + ln1_shift).astype(BF)
    projected = jnp.einsum("td,cdh->cth", normed_first, qkv_weight, preferred_element_type=F32).astype(BF)
    attended, totals = attend_forward(projected[0], projected[1], projected[2], length)
    attended_rows = exchange(attended.reshape(16, 128, HD), TENSOR).reshape(2, 4, 2, 128, HD)
    head_groups = [
        pick(pick(attended_rows, at_x, 0), at_core, 1).transpose(1, 0, 2).reshape(128, 512)
        for at_x in (x_lo, 1 - x_lo)
        for at_core in (core, 1 - core)
    ]
    branch_rows = jnp.concatenate(
        [sum(dot(heads, w, (1, 0)) for heads, w in zip(head_groups, groups)) for groups in out_groups], axis=1
    )
    token_rows = lax.dynamic_slice_in_dim(tokens, tensor * 128, 128, 0).astype(F32)
    middle_rows = token_rows + branch_rows
    unit_second, inverse_second = norm_stats(middle_rows)
    normed_rows = (unit_second * ln2_gain + ln2_shift).astype(BF)

    normed_second = gather_rows(normed_rows)
    hidden = dot(normed_second, up_both, (1, 0))
    activated, gelu_pull = jax.vjp(partial(jax.nn.gelu, approximate=True), hidden)
    activated = activated.astype(BF)
    grad_act = dot(incoming, down_both, (1, 1))
    grad_hidden = gelu_pull(grad_act)[0].astype(BF)
    grad_normed_part = dot(grad_hidden, up_both, (1, 1)).astype(BF)
    grad_normed_second = scatter_rows(grad_normed_part)

    mixed_part = dot(activated, down_both, (1, 0)).astype(BF)
    grad_down = dot(activated, incoming, (0, 0)).astype(BF)
    grad_up = dot(normed_second, grad_hidden, (0, 0)).astype(BF)

    grad_middle = incoming_rows + norm_back(grad_normed_second, ln2_gain, unit_second, inverse_second)
    gain_second = jnp.sum(grad_normed_second * unit_second, axis=0)
    shift_second = jnp.sum(grad_normed_second, axis=0)
    grad_branch = grad_middle.astype(BF)
    grad_heads = jnp.stack(
        [
            sum(dot(grad_branch[:, i * 1024 : (i + 1) * 1024], out_groups[i][g], (1, 1)) for i in range(2)).astype(BF)
            for g in range(4)
        ]
    ).reshape(2, 2, 128, 4, HD)
    grad_heads = jnp.where(x_lo == 0, grad_heads, grad_heads[::-1])
    grad_heads = jnp.where(core == 0, grad_heads, grad_heads[:, ::-1])
    grad_attended = exchange(grad_heads.transpose(0, 3, 1, 2, 4).reshape(16, 128, HD), TENSOR).reshape(2048, HD)

    mixed_rows = scatter_rows(mixed_part)
    output = (middle_rows + mixed_rows).astype(BF)

    branch_back = gather_rows(grad_branch)
    by_place = attended.reshape(2, 4, 2, 128, HD)
    own_half, sent_half = (
        jnp.concatenate([pick(pick(by_place, at_x, 0), at_core, 1) for at_core in (core, 1 - core)]).reshape(1024, HD)
        for at_x in (x_lo, 1 - x_lo)
    )
    both_heads = jnp.concatenate([own_half, x_pair(sent_half)], axis=1)
    grad_out = dot(both_heads, branch_back, (0, 0)).astype(BF)

    grad_queries, grad_keys, grad_values = attend_backward(
        projected[0], projected[1], projected[2], grad_attended, totals, length
    )
    stacked = jnp.stack([grad_queries, grad_keys, grad_values])
    grad_first_part = jnp.einsum("cth,cdh->td", stacked, qkv_weight, preferred_element_type=F32).astype(BF)
    grad_qkv_part = jnp.einsum("td,cth->cdh", normed_first, stacked, preferred_element_type=F32)

    columns = jnp.sum(stacked.astype(F32), axis=1)
    weights = qkv_weight.astype(F32)
    shift_first = jnp.sum(weights * columns[:, None, :], axis=(0, 2))
    gain_first = (jnp.sum(weights * grad_qkv_part, axis=(0, 2)) - ln1_shift * shift_first) / ln1_gain
    sums = sum_of_all(jnp.stack([gain_first, gain_second, shift_first, shift_second]))

    by_core = grad_first_part.reshape(8, 2, 128, 2048)
    sent = core_swap(pick(by_core, 1 - core, 1))
    halves = (pick(by_core, core, 1).astype(F32) + sent.astype(F32)).astype(BF).reshape(2, 4, 128, 2048)

    def over_x(values):
        return pick(values, x_lo, 0).astype(F32) + x_pair(pick(values, 1 - x_lo, 0)).astype(F32)

    left = total(exchange(halves[..., :1024].transpose(1, 0, 2, 3), "z")).astype(BF)
    right = over_x(halves[..., 1024:]).astype(BF)
    grad_normed_first = jnp.concatenate([over_x(left), total(exchange(right, "z"))], axis=-1)
    unit_rows, inverse_rows = norm_stats(token_rows)
    grad_tokens = (grad_middle + norm_back(grad_normed_first, ln1_gain, unit_rows, inverse_rows)).astype(BF)

    def own_first(values):
        return jnp.where(x_lo == 0, values, values[::-1])

    def sum_columns(grad):
        rows = grad.shape[0] // 2
        blocks = own_first(grad.reshape(2, rows, 2, 1024)).transpose(2, 0, 1, 3).reshape(4, rows, 1024)
        over_x = total(exchange(blocks, ("x_hi", "x_lo"))).astype(BF)
        return total(exchange(over_x.reshape(rows, 4, 256).transpose(1, 0, 2), "y"))

    grad_down = sum_columns(grad_down)
    grad_out = sum_columns(grad_out)
    up_sums = total(exchange(grad_up.reshape(2, 4, 256, 1024).transpose(1, 0, 2, 3), "y")).astype(BF)
    up_blocks = own_first(up_sums.reshape(2, 256, 2, 512).transpose(2, 0, 1, 3)).transpose(1, 0, 2, 3)
    grad_up = total(exchange(up_blocks.reshape(4, 256, 512), ("x_hi", "x_lo")))
    qkv_sums = total(
        exchange(grad_qkv_part.astype(BF).reshape(3, 2, 4, 256, 128).transpose(2, 1, 0, 3, 4), "y")
    ).astype(BF)
    grad_qkv = total(exchange(qkv_sums, "x_hi"))
    return (output, grad_tokens, grad_qkv, grad_out, grad_up, grad_down, sums[:2], sums[2:])


def solution(mesh):
    return jax.shard_map(
        body,
        mesh=Mesh(mesh.devices.reshape(2, 4, 2, 4, 2), AXES),
        in_specs=(
            P(BATCH, None),
            P(),
            P(),
            P(None, None, TENSOR),
            P(TENSOR, None),
            P(),
            P(),
            P(None, TENSOR),
            P(TENSOR, None),
            P(BATCH),
            P(AXES, None),
        ),
        out_specs=(
            P(AXES, None),
            P(AXES, None),
            P(None, BATCH, TENSOR),
            P(TENSOR, BATCH),
            P(BATCH, TENSOR),
            P(TENSOR, BATCH),
            P(),
            P(),
        ),
        check_vma=False,
    )
```

time: 526 us -> 638 us (1.21)
  waiting for transfers between devices: 191 us -> 241 us
  matrix products: 87.9 us -> 117 us
  other arithmetic: 52.5 us -> 74 us
  between operations: 16.5 us -> 3.03 us
  starting transfers between devices: 93.8 us -> 104 us
  blocking collectives: 0 us -> 9.99 us
    all_to_all x2 -> x21, waiting for transfers between devices: 0.01 us -> 218 us  [exchange(): return lax.all_to_all(values, axes, 0, 0)]
    ppermute x63 -> x18, waiting for transfers between devices: 165 us -> 23.3 us  [the longest x4 21.5 us: x_partner(): return lax.ppermute(values, ('x_hi', 'x_lo', 'core'), pairs)]
    all_to_all x2 -> x21, starting transfers between devices: 8.51 us -> 89.1 us  [exchange(): return lax.all_to_all(values, axes, 0, 0)]
    ppermute x63 -> x18, starting transfers between devices: 85.3 us -> 14.8 us  [the longest x4 7.14 us: x_partner(): return lax.ppermute(values, ('x_hi', 'x_lo', 'core'), pairs)]
    dot_general x33 -> x47, matrix products: 72.3 us -> 98.8 us  [dot(): lax.dot_general(left, right, ((dims[:1], dims[1:]), ((), ())), preferred_...]
    unnamed x141, local copies, waits for them, and re-layouts: 44.6 us -> 18.2 us
    all_gather x1 -> x0, waiting for transfers between devices: 25.6 us -> none  [body(): out_full = lax.all_gather(out_weight, 'tensor', axis=0, tiled=True)]
    reduce_sum x0 -> x15, other arithmetic: none -> 23.3 us  [the longest x14 20.7 us: total(): return jnp.sum(values.astype(F32), axis=0)]
  transfers between devices with their start and end apart: 66 -> 39, of which waited for: 25 -> 23; matrix products, arithmetic and copies ran while one was open for 34% -> 33% of each run, Pallas kernels for 0% -> 0%
where the time goes in v2:
time: 638 us; the launch traced here: 630 us
  waiting for transfers between devices  241 us (38%)
  matrix products  117 us (18%)
  starting transfers between devices  104 us (16%)
  local copies, waits for them, and re-layouts  80.1 us (13%)
  other arithmetic  74 us (12%)
  blocking collectives  9.99 us (2%)
    all_to_all x21, waiting for transfers between devices, exchange(): return lax.all_to_all(values, axes, 0, 0)  218 us
    dot_general x47, matrix products, dot(): lax.dot_general(left, right, ((dims[:1], dims[1:]), ((), ())), preferred_...  98.8 us
    all_to_all x21, starting transfers between devices, exchange(): return lax.all_to_all(values, axes, 0, 0)  89.1 us
    ppermute x4, waiting for transfers between devices, x_partner(): return lax.ppermute(values, ('x_hi', 'x_lo', 'core'), pairs)  21.5 us
    reduce_sum x14, other arithmetic, total(): return jnp.sum(values.astype(F32), axis=0)  20.7 us
    unnamed x141, local copies, waits for them, and re-layouts  18.2 us
  transfers between devices with their start and end apart: 39, of which 23 were waited for; matrix products, arithmetic and copies ran while one was open for 33% of the time, Pallas kernels for 0%

profile of v2, /device:TPU:0, one launch (start us, length us, event | category | flops | bytes accessed | tf_op | source)
XLA Modules:
  0.0 629.9 jit_solution(3330066465317263984)
XLA Ops:
  45.6 7.1 %all-to-all-done.2 = bf16[4,128,1024]{2,1,0:T(8,128)(2,1)} async-done(((bf16[4,128,1024]{2,1,0:T(8,128)(2,1)}), bf16[4,128,1024]{2,1,0:T(8,128)(2,1)}, u32[]{:S(2)}, u32[]{:S(2)}) %all-to-all-start.2) | async-done | bytes 1048608 | tf_op jit(solution)/shard_map/all_to_all | solution.py:34
  61.6 14.1 %all-to-all-done = bf16[16,128,128]{2,1,0:T(8,128)(2,1)} async-done(((bf16[16,128,128]{2,1,0:T(8,128)(2,1)}), bf16[16,128,128]{2,1,0:T(8,128)(2,1)}, u32[]{:S(2)}, u32[]{:S(2)}) %all-to-all-start) | async-done | bytes 524320 | tf_op jit(solution)/shard_map/all_to_all | solution.py:34
  102.2 24.9 %all-to-all-done.3 = bf16[4,128,2048]{2,1,0:T(8,128)(2,1)} async-done(((bf16[4,128,2048]{2,1,0:T(8,128)(2,1)}), bf16[4,128,2048]{2,1,0:T(8,128)(2,1)}, u32[]{:S(2)}, u32[]{:S(2)}) %all-to-all-start.3) | async-done | bytes 2097184 | tf_op jit(solution)/shard_map/all_to_all | solution.py:34
  139.0 21.3 %all-to-all-done.5 = bf16[4,128,2048]{2,1,0:T(8,128)(2,1)} async-done(((bf16[4,128,2048]{2,1,0:T(8,128)(2,1)}), bf16[4,128,2048]{2,1,0:T(8,128)(2,1)}, u32[]{:S(2)}, u32[]{:S(2)}) %all-to-all-start.5) | async-done | bytes 2097184 | tf_op jit(solution)/shard_map/all_to_all | solution.py:34
  165.8 20.6 %collective-permute-done.8 = bf16[512,2048]{1,0:T(8,128)(2,1)} collective-permute-done((bf16[512,2048]{1,0:T(8,128)(2,1)}, bf16[512,2048]{1,0:T(8,128)(2,1)}, u32[]{:S(2)}, u32[]{:S(2)}) %collective-permute-start.8) | collective-permute-done | bytes 2097184 | tf_op jit(solution)/shard_map/ppermute | solution.py:30
  188.1 6.5 %fusion.26 = f32[1024,1024]{1,0:T(8,128)S(1)} fusion(bf16[2048,1024]{1,0:T(8,128)(2,1)S(1)} %constant_dynamic-update-slice_fusion, bf16[512,2048]{1,0:T(8,128)(2,1)} %collective-permute-done.6, bf16[512,2048]{1,0:T(8,128)(2,1)} %bitcast.39), kind=kOutput, calls=%fused_computation.64 | convolution fusion | flops 4303355904 | bytes 12582912 | tf_op jit(solution)/shard_map/dot_general | solution.py:63
  194.7 10.6 %fusion.14 = bf16[1024,1024]{1,0:T(8,128)(2,1)S(1)} fusion(f32[1024,1024]{1,0:T(8,128)S(1)} %fusion.26, bf16[1024,2048]{1,0:T(8,128)(2,1)S(1)} %constant_dynamic-update-slice_fusion.2, bf16[512,2048]{1,0:T(8,128)(2,1)S(1)} %collective-permute-done.10, bf16[512,2048]{1,0:T(8,128)(2,1)} %bitcast.41), kind=kOutput, calls=%fused_computation.23 | convolution fusion | flops 4324327424 | bytes 14680064 | tf_op jit(solution)/shard_map/dot_general | solution.py:63
  231.8 19.7 %all-to-all-done.6 = bf16[4,128,2048]{2,1,0:T(8,128)(2,1)} async-done(((bf16[4,128,2048]{2,1,0:T(8,128)(2,1)}), bf16[4,128,2048]{2,1,0:T(8,128)(2,1)}, u32[]{:S(2)}, u32[]{:S(2)}) %all-to-all-start.6) | async-done | bytes 2097184 | tf_op jit(solution)/shard_map/all_to_all | solution.py:34
  256.0 10.5 %convolution_convert_fusion = bf16[1024,2048]{1,0:T(8,128)(2,1)} fusion(bf16[512,2048]{1,0:T(8,128)(2,1)} %copy-done.64, bf16[512,2048]{1,0:T(8,128)(2,1)} %bitcast.41, f32[1024,1024]{1,0:T(8,128)} %copy-done.65), kind=kOutput, calls=%fused_computation.45 | convolution fusion | flops 4314890240 | bytes 12582912 | tf_op jit(solution)/shard_map/dot_general | solution.py:63
  270.0 11.9 %all-to-all-done.4 = bf16[4,128,2048]{2,1,0:T(8,128)(2,1)} async-done(((bf16[4,128,2048]{2,1,0:T(8,128)(2,1)}), bf16[4,128,2048]{2,1,0:T(8,128)(2,1)}, u32[]{:S(2)}, u32[]{:S(2)}) %all-to-all-start.4) | async-done | bytes 2097184 | tf_op jit(solution)/shard_map/all_to_all | solution.py:34
  305.7 7.4 %convolution_convert_fusion.1 = bf16[2048,1024]{1,0:T(8,128)(2,1)S(1)} fusion(bf16[1024,1024]{1,0:T(8,128)(2,1)} %copy-done.66, bf16[512,2048]{1,0:T(8,128)(2,1)} %collective-permute-done.6, bf16[512,2048]{1,0:T(8,128)(2,1)} %bitcast.39), kind=kOutput, calls=%fused_computation.46 | convolution fusion | flops 4305453056 | bytes 10485760 | tf_op jit(solution)/shard_map/dot_general | solution.py:63
  315.6 7.9 %reshape.563 = bf16[2,512,2,1024]{3,2,1,0:T(2,128)(2,1)} reshape(bf16[1024,2048]{1,0:T(8,128)(2,1)} %convolution_convert_fusion) | data formatting | bytes 8388608 | tf_op jit(solution)/shard_map/reshape | solution.py:251
  330.2 5.5 all-to-all-start.15
  357.4 27.9 %all-to-all-done.15 = bf16[4,2,256,1024]{3,2,1,0:T(8,128)(2,1)} async-done(((bf16[4,2,256,1024]{3,2,1,0:T(8,128)(2,1)}), bf16[4,2,256,1024]{3,2,1,0:T(8,128)(2,1)}, u32[]{:S(2)}, u32[]{:S(2)}) %all-to-all-start.15) | async-done | bytes 4194336 | tf_op jit(solution)/shard_map/all_to_all | solution.py:34
  395.8 8.8 %bitcast_convert_fusion.1 = (bf16[3,2048,128]{1,2,0:T(8,128)(2,1)}, f32[3,128,2048]{2,1,0:T(8,128)S(1)}) fusion(bf16[2048,2048]{1,0:T(8,128)(2,1)} %param.31, f32[2048]{0:T(1024)S(1)} %copy-done.58, f32[2048]{0:T(1024)S(1)} %copy-done.43, f32[2048]{0:T(1024)S(1)} %copy-done.60, f32[2048]{0:T(1024)S(1)} %copy-done.55, bf16[1,2048,128]{2,1,0:T(8,128)(2,1)S(1)} %fusion.41, ...), kind=kOutput, calls=%fused_computation.54 | convolution fusion | flops 3256614912 | bytes 14712832 | tf_op jit(solution)/shard_map/td,cth->cdh/dot_general | solution.py:225
  406.7 32.7 %all-to-all-done.17 = bf16[4,512,1024]{2,1,0:T(8,128)(2,1)} async-done(((bf16[4,512,1024]{2,1,0:T(8,128)(2,1)}), bf16[4,512,1024]{2,1,0:T(8,128)(2,1)}, u32[]{:S(2)}, u32[]{:S(2)}) %all-to-all-start.17) | async-done | bytes 4194336 | tf_op jit(solution)/shard_map/all_to_all | solution.py:34
  439.4 10.0 %all_to_all.110 = f32[4,4,2048]{2,1,0:T(4,128)S(1)} all-to-all(f32[4,4,2048]{2,1,0:T(4,128)S(1)} %broadcast_in_dim.45), channel_id=1, replica_groups=mesh['x_hi'=2,'y'=4,'x_lo'=2,'z'=4,'core'=2] {'z'}, dimensions={0} | all-to-all | bytes 262144 | tf_op jit(solution)/shard_map/all_to_all | solution.py:34
  470.4 9.0 %all-to-all-done.12 = bf16[4,128,2048]{2,1,0:T(8,128)(2,1)} async-done(((bf16[4,128,2048]{2,1,0:T(8,128)(2,1)}), bf16[4,128,2048]{2,1,0:T(8,128)(2,1)}, u32[]{:S(2)}, u32[]{:S(2)}) %all-to-all-start.12) | async-done | bytes 2097184 | tf_op jit(solution)/shard_map/all_to_all | solution.py:34
  483.3 11.2 %all-to-all-done.16 = bf16[4,256,512]{2,1,0:T(8,128)(2,1)S(1)} async-done(((bf16[4,256,512]{2,1,0:T(8,128)(2,1)}), bf16[4,256,512]{2,1,0:T(8,128)(2,1)S(1)}, u32[]{:S(2)}, u32[]{:S(2)}) %all-to-all-start.16) | async-done | bytes 1048608 | tf_op jit(solution)/shard_map/all_to_all | solution.py:34
  517.0 6.4 %all-to-all-done.10 = bf16[4,2,3,256,128]{3,1,4,2,0:T(2,128)(2,1)S(1)} async-done(((bf16[4,2,3,256,128]{3,1,4,2,0:T(2,128)(2,1)}), bf16[4,2,3,256,128]{3,1,4,2,0:T(2,128)(2,1)S(1)}, u32[]{:S(2)}, u32[]{:S(2)}) %all-to-all-start.10) | async-done | bytes 1572896 | tf_op jit(solution)/shard_map/all_to_all | solution.py:34
  555.0 8.2 %all-to-all-done.11 = bf16[2,3,256,128]{2,3,1,0:T(8,128)(2,1)S(1)} async-done(((bf16[2,3,256,128]{2,3,1,0:T(8,128)(2,1)}), bf16[2,3,256,128]{2,3,1,0:T(8,128)(2,1)S(1)}, u32[]{:S(2)}, u32[]{:S(2)}) %all-to-all-start.11) | async-done | bytes 393248 | tf_op jit(solution)/shard_map/all_to_all | solution.py:34
  566.6 5.4 fusion.7
  594.5 5.8 all-to-all-done.8
  619.9 5.8 all-to-all-done.9
  (360 shorter events, 327.8 us)
Async XLA Ops:
  2.8 29.3 %all-to-all-start.1 = ((bf16[4,128,1024]{2,1,0:T(8,128)(2,1)}), bf16[4,128,1024]{2,1,0:T(8,128)(2,1)}, u32[]{:S(2)}, u32[]{:S(2)}) async-start(bf16[4,128,1024]{2,1,0:T(8,128)(2,1)} %broadcast_in_dim.40), calls=%async_computation.1 | async-start | bytes 2097152 | tf_op jit(solution)/shard_map/all_to_all | solution.py:34
  33.2 19.5 %all-to-all-start.2 = ((bf16[4,128,1024]{2,1,0:T(8,128)(2,1)}), bf16[4,128,1024]{2,1,0:T(8,128)(2,1)}, u32[]{:S(2)}, u32[]{:S(2)}) async-start(bf16[4,128,1024]{2,1,0:T(8,128)(2,1)} %broadcast_in_dim.41), calls=%async_computation.2 | async-start | bytes 2097152 | tf_op jit(solution)/shard_map/all_to_all | solution.py:34
  44.1 38.9 %collective-permute-start.1 = (bf16[512,1024]{1,0:T(8,128)(2,1)}, bf16[512,1024]{1,0:T(8,128)(2,1)}, u32[]{:S(2)}, u32[]{:S(2)}) collective-permute-start(bf16[512,1024]{1,0:T(8,128)(2,1)} %bitcast.23), channel_id=1, source_target_pairs={{0,8},{1,73},{8,64},{9,1},{64,72},{65,9},{72,0},{73,65},{2,10},{3,... | collective-permute-start | bytes 3145736 | tf_op jit(solution)/shard_map/ppermute | solution.py:30
  52.6 30.4 %collective-permute-start.4 = (bf16[512,1024]{1,0:T(8,128)(2,1)}, bf16[512,1024]{1,0:T(8,128)(2,1)}, u32[]{:S(2)}, u32[]{:S(2)}) collective-permute-start(bf16[512,1024]{1,0:T(8,128)(2,1)} %bitcast.34), channel_id=1, source_target_pairs={{0,8},{1,73},{8,64},{9,1},{64,72},{65,9},{72,0},{73,65},{2,10},{3,... | collective-permute-start | bytes 3145736 | tf_op jit(solution)/shard_map/ppermute | solution.py:30
  55.9 19.9 %all-to-all-start = ((bf16[16,128,128]{2,1,0:T(8,128)(2,1)}), bf16[16,128,128]{2,1,0:T(8,128)(2,1)}, u32[]{:S(2)}, u32[]{:S(2)}) async-start(bf16[16,128,128]{2,1,0:T(8,128)(2,1)} %bitcast.271), calls=%async_computation | async-start | bytes 1048576 | tf_op jit(solution)/shard_map/all_to_all | solution.py:34
  61.3 25.4 %collective-permute-start = (bf16[512,1024]{1,0:T(8,128)(2,1)}, bf16[512,1024]{1,0:T(8,128)(2,1)}, u32[]{:S(2)}, u32[]{:S(2)}) collective-permute-start(bf16[512,1024]{1,0:T(8,128)(2,1)} %bitcast.23), channel_id=1, source_target_pairs={{0,1},{1,0},{2,3},{3,2},{4,5},{5,4},{6,7},{7,6},{8,9},{9,8},{10,11... | collective-permute-start | bytes 3145736 | tf_op jit(solution)/shard_map/ppermute | solution.py:21
  95.7 31.4 %all-to-all-start.3 = ((bf16[4,128,2048]{2,1,0:T(8,128)(2,1)}), bf16[4,128,2048]{2,1,0:T(8,128)(2,1)}, u32[]{:S(2)}, u32[]{:S(2)}) async-start(bf16[4,128,2048]{2,1,0:T(8,128)(2,1)} %broadcast_in_dim.42), calls=%async_computation.3 | async-start | bytes 4194304 | tf_op jit(solution)/shard_map/all_to_all | solution.py:34
  129.7 30.6 %all-to-all-start.5 = ((bf16[4,128,2048]{2,1,0:T(8,128)(2,1)}), bf16[4,128,2048]{2,1,0:T(8,128)(2,1)}, u32[]{:S(2)}, u32[]{:S(2)}) async-start(bf16[4,128,2048]{2,1,0:T(8,128)(2,1)} %broadcast_in_dim.43), calls=%async_computation.5 | async-start | bytes 4194304 | tf_op jit(solution)/shard_map/all_to_all | solution.py:34
  134.2 29.7 %collective-permute-start.7 = (bf16[2048,512]{1,0:T(8,128)(2,1)}, bf16[2048,512]{1,0:T(8,128)(2,1)}, u32[]{:S(2)}, u32[]{:S(2)}) collective-permute-start(bf16[2048,512]{1,0:T(8,128)(2,1)} %param.38), channel_id=1, source_target_pairs={{0,8},{1,73},{8,64},{9,1},{64,72},{65,9},{72,0},{73,65},{2,10},{3,... | collective-permute-start | bytes 6291464 | tf_op jit(solution)/shard_map/ppermute | solution.py:30
  138.3 48.1 %collective-permute-start.8 = (bf16[512,2048]{1,0:T(8,128)(2,1)}, bf16[512,2048]{1,0:T(8,128)(2,1)}, u32[]{:S(2)}, u32[]{:S(2)}) collective-permute-start(bf16[512,2048]{1,0:T(8,128)(2,1)} %param.39), channel_id=1, source_target_pairs={{0,8},{1,73},{8,64},{9,1},{64,72},{65,9},{72,0},{73,65},{2,10},{3,... | collective-permute-start | bytes 6291464 | tf_op jit(solution)/shard_map/ppermute | solution.py:30
  138.4 49.7 %collective-permute-start.6 = (bf16[512,2048]{1,0:T(8,128)(2,1)}, bf16[512,2048]{1,0:T(8,128)(2,1)}, u32[]{:S(2)}, u32[]{:S(2)}) collective-permute-start(bf16[512,2048]{1,0:T(8,128)(2,1)} %bitcast.39), channel_id=1, source_target_pairs={{0,1},{1,0},{2,3},{3,2},{4,5},{5,4},{6,7},{7,6},{8,9},{9,8},{10,11... | collective-permute-start | bytes 6291464 | tf_op jit(solution)/shard_map/ppermute | solution.py:21
  160.3 34.3 %collective-permute-start.10 = (bf16[512,2048]{1,0:T(8,128)(2,1)}, bf16[512,2048]{1,0:T(8,128)(2,1)S(1)}, u32[]{:S(2)}, u32[]{:S(2)}) collective-permute-start(bf16[512,2048]{1,0:T(8,128)(2,1)} %bitcast.41), channel_id=1, source_target_pairs={{0,1},{1,0},{2,3},{3,2},{4,5},{5,4},{6,7},{7,6},{8,9},{9,8},{10,11... | collective-permute-start | bytes 6291464 | tf_op jit(solution)/shard_map/ppermute | solution.py:21
  219.8 31.7 %all-to-all-start.6 = ((bf16[4,128,2048]{2,1,0:T(8,128)(2,1)}), bf16[4,128,2048]{2,1,0:T(8,128)(2,1)}, u32[]{:S(2)}, u32[]{:S(2)}) async-start(bf16[4,128,2048]{2,1,0:T(8,128)(2,1)} %bitcast.268), calls=%async_computation.6 | async-start | bytes 4194304 | tf_op jit(solution)/shard_map/all_to_all | solution.py:34
  251.5 30.4 %all-to-all-start.4 = ((bf16[4,128,2048]{2,1,0:T(8,128)(2,1)}), bf16[4,128,2048]{2,1,0:T(8,128)(2,1)}, u32[]{:S(2)}, u32[]{:S(2)}) async-start(bf16[4,128,2048]{2,1,0:T(8,128)(2,1)} %bitcast.267), calls=%async_computation.4 | async-start | bytes 4194304 | tf_op jit(solution)/shard_map/all_to_all | solution.py:34
  301.2 28.9 %all-to-all-start.7 = ((bf16[16,128,128]{2,1,0:T(8,128)(2,1)}), bf16[16,128,128]{2,1,0:T(8,128)(2,1)}, u32[]{:S(2)}, u32[]{:S(2)}) async-start(bf16[16,128,128]{2,1,0:T(8,128)(2,1)} %bitcast.276), calls=%async_computation.7 | async-start | bytes 1048576 | tf_op jit(solution)/shard_map/all_to_all | solution.py:34
  330.2 55.1 %all-to-all-start.15 = ((bf16[4,2,256,1024]{3,2,1,0:T(8,128)(2,1)}), bf16[4,2,256,1024]{3,2,1,0:T(8,128)(2,1)}, u32[]{:S(2)}, u32[]{:S(2)}) async-start(bf16[4,2,256,1024]{3,2,1,0:T(8,128)(2,1)} %bitcast.265), calls=%async_computation.15 | async-start | bytes 8388608 | tf_op jit(solution)/shard_map/all_to_all | solution.py:34
  385.3 54.0 %all-to-all-start.17 = ((bf16[4,512,1024]{2,1,0:T(8,128)(2,1)}), bf16[4,512,1024]{2,1,0:T(8,128)(2,1)}, u32[]{:S(2)}, u32[]{:S(2)}) async-start(bf16[4,512,1024]{2,1,0:T(8,128)(2,1)} %bitcast.264), calls=%async_computation.17 | async-start | bytes 8388608 | tf_op jit(solution)/shard_map/all_to_all | solution.py:34
  451.0 28.4 %all-to-all-start.12 = ((bf16[4,128,2048]{2,1,0:T(8,128)(2,1)}), bf16[4,128,2048]{2,1,0:T(8,128)(2,1)}, u32[]{:S(2)}, u32[]{:S(2)}) async-start(bf16[4,128,2048]{2,1,0:T(8,128)(2,1)} %broadcast_in_dim.44), calls=%async_computation.12 | async-start | bytes 4194304 | tf_op jit(solution)/shard_map/all_to_all | solution.py:34
  465.0 101.6 %collective-permute-start.12 = (bf16[8,128,2048]{2,1,0:T(8,128)(2,1)}, bf16[8,128,2048]{2,1,0:T(8,128)(2,1)}, u32[]{:S(2)}, u32[]{:S(2)}) collective-permute-start(bf16[8,128,2048]{2,1,0:T(8,128)(2,1)} %dynamic-slice_bitcast_fusion), channel_id=1, source_target_pairs={{0,1},{1,0},{2,3},{3,2},{4,5},{5,4},{6,7},{7,6},{8,9},{9,8},{10,11... | collective-permute-start | bytes 12582920 | tf_op jit(solution)/shard_map/ppermute | solution.py:21
  483.0 59.7 %collective-permute-start.16 = (bf16[512,2048]{1,0:T(8,128)(2,1)}, bf16[512,2048]{1,0:T(8,128)(2,1)}, u32[]{:S(2)}, u32[]{:S(2)}) collective-permute-start(bf16[512,2048]{1,0:T(8,128)(2,1)} %bitcast.78), channel_id=1, source_target_pairs={{0,1},{1,0},{2,3},{3,2},{4,5},{5,4},{6,7},{7,6},{8,9},{9,8},{10,11... | collective-permute-start | bytes 6291464 | tf_op jit(solution)/shard_map/ppermute | solution.py:21
  504.5 18.9 %all-to-all-start.10 = ((bf16[4,2,3,256,128]{3,1,4,2,0:T(2,128)(2,1)}), bf16[4,2,3,256,128]{3,1,4,2,0:T(2,128)(2,1)S(1)}, u32[]{:S(2)}, u32[]{:S(2)}) async-start(bf16[4,2,3,256,128]{3,1,4,2,0:T(2,128)(2,1)} %bitcast.258), calls=%async_computation.10 | async-start | bytes 3145728 | tf_op jit(solution)/shard_map/all_to_all | solution.py:34
  563.1 16.1 %all-to-all-start.13 = ((bf16[4,128,1024]{2,1,0:T(8,128)(2,1)}), bf16[4,128,1024]{2,1,0:T(8,128)(2,1)S(1)}, u32[]{:S(2)}, u32[]{:S(2)}) async-start(bf16[4,128,1024]{2,1,0:T(8,128)(2,1)} %bitcast.80), calls=%async_computation.13 | async-start | bytes 2097152 | tf_op jit(solution)/shard_map/all_to_all | solution.py:34
  580.2 20.1 %all-to-all-start.8 = ((bf16[4,2,128,1024]{3,2,1,0:T(8,128)(2,1)}), bf16[4,2,128,1024]{3,2,1,0:T(8,128)(2,1)S(1)}, u32[]{:S(2)}, u32[]{:S(2)}) async-start(bf16[4,2,128,1024]{3,2,1,0:T(8,128)(2,1)} %copy.109), calls=%async_computation.8 | async-start | bytes 4194304 | tf_op jit(solution)/shard_map/all_to_all | solution.py:34
  586.1 18.2 %collective-permute-start.14 = (bf16[4,128,1024]{2,1,0:T(8,128)(2,1)}, bf16[4,128,1024]{2,1,0:T(8,128)(2,1)}, u32[]{:S(2)}, u32[]{:S(2)}) collective-permute-start(bf16[4,128,1024]{2,1,0:T(8,128)(2,1)} %dynamic-slice_bitcast_fusion.1), channel_id=1, source_target_pairs={{0,8},{8,0},{1,9},{9,1},{2,10},{10,2},{3,11},{11,3},{4,12},{12,4},... | collective-permute-start | bytes 3145736 | tf_op jit(solution)/shard_map/ppermute | solution.py:25
  (82 other events, 533.6 us)

commit v3 on v2

--- a/solution.py
+++ b/solution.py
@@ -30,23 +30,20 @@
     return lax.ppermute(values, ("x_hi", "x_lo", "core"), pairs)
 
 
-def exchange(values, axes):
-    return lax.all_to_all(values, axes, 0, 0)
-
-
-def spread(values, axes, count=4):
-    return exchange(jnp.broadcast_to(values[None], (count, *values.shape)), axes)
-
-
-def total(values):
-    return jnp.sum(values.astype(F32), axis=0)
+def shift(axes, sizes, step):
+    return lambda values: lax.ppermute(values, axes, [(i, (i + step) % sizes) for i in range(sizes)])
+
+
+z_up, z_down, z_far = (shift("z", 4, step) for step in (1, -1, 2))
+y_up, y_down, y_far = (shift("y", 4, step) for step in (1, -1, 2))
+x_up, x_down, x_far = (shift(("x_hi", "x_lo"), 4, step) for step in (1, -1, 2))
 
 
 def norm_stats(values):
     centre = jnp.mean(values, axis=-1, keepdims=True)
     offsets = values - centre
-    spread = jnp.mean(offsets * offsets, axis=-1, keepdims=True)
-    inverse = lax.rsqrt(spread + EPS)
+    variance = jnp.mean(offsets * offsets, axis=-1, keepdims=True)
+    inverse = lax.rsqrt(variance + EPS)
     return (offsets * inverse, inverse)
 
 
@@ -109,25 +106,24 @@
     return (grad_queries.astype(BF), grad_keys.astype(BF), grad_values.astype(BF))
 
 
-def gather_rows(rows):
-    mine = spread(rows, "z").reshape(512, rows.shape[1])
-    return jnp.concatenate([mine, core_swap(mine)], axis=0)
-
-
-def scatter_rows(partial_sums):
-    mine, others = partial_sums[:512], partial_sums[512:]
-    halves = (mine.astype(F32) + core_swap(others).astype(F32)).astype(BF)
-    return total(exchange(halves.reshape(4, 128, 2048), "z"))
+def scatter(values, axes):
+    return lax.psum_scatter(values, axes, scatter_dimension=0, tiled=True).astype(F32)
 
 
 def pick(values, index, axis):
     return lax.dynamic_index_in_dim(values, index, axis, False)
 
 
+def reduce_ring(values, place, up, down, far):
+    parts = [pick(values, (place + by) % 4, 0) for by in range(4)]
+    return sum(
+        move(part).astype(F32) for move, part in zip((lambda v: v, up, far, down), parts)
+    )
+
+
 def sum_of_all(values):
-    values = values + core_swap(values)
-    for axes in ("z", ("x_hi", "x_lo"), "y"):
-        values = total(spread(values, axes))
+    for move in (core_swap, z_far, z_up, x_far, x_up, y_far, y_up):
+        values = values + move(values)
     return values
 
 
@@ -148,44 +144,39 @@
     tensor = x_lo * 8 + z * 2 + core
     length = lengths[0]
 
-    out_groups = []
-    for half in range(2):
-        mine = spread(out_weight[:, half * 1024 : (half + 1) * 1024], "z").reshape(512, 1024)
-        both = [mine, x_partner(mine)]
-        out_groups.append([group for part in both for group in (part, core_swap(part))])
+    out_full = lax.all_gather(out_weight, TENSOR, axis=0, tiled=True)
     live_rows = (tensor * 128 + jnp.arange(128, dtype=jnp.int32) < length).astype(F32)[:, None]
     incoming_rows = cotangent.astype(F32) * live_rows
+    sent_rows = incoming_rows.astype(BF)
+    along_z = jnp.stack([sent_rows, z_down(sent_rows), z_far(sent_rows), z_up(sent_rows)])
+    along_z = lax.dynamic_slice_in_dim(jnp.concatenate([along_z, along_z[:3]]), (4 - z) % 4, 4, 0)
+    from_core = core_swap(along_z)
+    incoming = jnp.stack(
+        [jnp.where(core == 0, along_z, from_core), jnp.where(core == 0, from_core, along_z)], axis=1
+    ).reshape(1024, 2048)
     up_both = jnp.concatenate([up_weight, x_partner(up_weight)], axis=1)
     down_both = jnp.concatenate([down_weight, x_partner(down_weight)], axis=0)
-    incoming = gather_rows(incoming_rows.astype(BF))
 
     inputs = tokens.astype(F32)
     unit_first, _ = norm_stats(inputs)
     normed_first = (unit_first * ln1_gain + ln1_shift).astype(BF)
     projected = jnp.einsum("td,cdh->cth", normed_first, qkv_weight, preferred_element_type=F32).astype(BF)
     attended, totals = attend_forward(projected[0], projected[1], projected[2], length)
-    attended_rows = exchange(attended.reshape(16, 128, HD), TENSOR).reshape(2, 4, 2, 128, HD)
-    head_groups = [
-        pick(pick(attended_rows, at_x, 0), at_core, 1).transpose(1, 0, 2).reshape(128, 512)
-        for at_x in (x_lo, 1 - x_lo)
-        for at_core in (core, 1 - core)
-    ]
-    branch_rows = jnp.concatenate(
-        [sum(dot(heads, w, (1, 0)) for heads, w in zip(head_groups, groups)) for groups in out_groups], axis=1
-    )
+    attended_rows = lax.all_to_all(attended, TENSOR, 0, 1, tiled=True)
+    branch_rows = dot(attended_rows, out_full, (1, 0))
     token_rows = lax.dynamic_slice_in_dim(tokens, tensor * 128, 128, 0).astype(F32)
     middle_rows = token_rows + branch_rows
     unit_second, inverse_second = norm_stats(middle_rows)
     normed_rows = (unit_second * ln2_gain + ln2_shift).astype(BF)
 
-    normed_second = gather_rows(normed_rows)
+    normed_second = lax.all_gather(normed_rows, ("z", "core"), axis=0, tiled=True)
     hidden = dot(normed_second, up_both, (1, 0))
     activated, gelu_pull = jax.vjp(partial(jax.nn.gelu, approximate=True), hidden)
     activated = activated.astype(BF)
     grad_act = dot(incoming, down_both, (1, 1))
     grad_hidden = gelu_pull(grad_act)[0].astype(BF)
     grad_normed_part = dot(grad_hidden, up_both, (1, 1)).astype(BF)
-    grad_normed_second = scatter_rows(grad_normed_part)
+    grad_normed_second = scatter(grad_normed_part, ("z", "core"))
 
     mixed_part = dot(activated, down_both, (1, 0)).astype(BF)
     grad_down = dot(activated, incoming, (0, 0)).astype(BF)
@@ -195,26 +186,13 @@
     gain_second = jnp.sum(grad_normed_second * unit_second, axis=0)
     shift_second = jnp.sum(grad_normed_second, axis=0)
     grad_branch = grad_middle.astype(BF)
-    grad_heads = jnp.stack(
-        [
-            sum(dot(grad_branch[:, i * 1024 : (i + 1) * 1024], out_groups[i][g], (1, 1)) for i in range(2)).astype(BF)
-            for g in range(4)
-        ]
-    ).reshape(2, 2, 128, 4, HD)
-    grad_heads = jnp.where(x_lo == 0, grad_heads, grad_heads[::-1])
-    grad_heads = jnp.where(core == 0, grad_heads, grad_heads[:, ::-1])
-    grad_attended = exchange(grad_heads.transpose(0, 3, 1, 2, 4).reshape(16, 128, HD), TENSOR).reshape(2048, HD)
-
-    mixed_rows = scatter_rows(mixed_part)
+    grad_attended = lax.all_to_all(dot(grad_branch, out_full, (1, 1)).astype(BF), TENSOR, 1, 0, tiled=True)
+    mixed_rows = scatter(mixed_part, ("z", "core"))
     output = (middle_rows + mixed_rows).astype(BF)
 
-    branch_back = gather_rows(grad_branch)
-    by_place = attended.reshape(2, 4, 2, 128, HD)
-    own_half, sent_half = (
-        jnp.concatenate([pick(pick(by_place, at_x, 0), at_core, 1) for at_core in (core, 1 - core)]).reshape(1024, HD)
-        for at_x in (x_lo, 1 - x_lo)
-    )
-    both_heads = jnp.concatenate([own_half, x_pair(sent_half)], axis=1)
+    branch_back = lax.all_gather(grad_branch, ("z", "core"), axis=0, tiled=True)
+    by_half = attended.reshape(2, 1024, HD)
+    both_heads = jnp.concatenate([pick(by_half, x_lo, 0), x_pair(pick(by_half, 1 - x_lo, 0))], axis=1)
     grad_out = dot(both_heads, branch_back, (0, 0)).astype(BF)
 
     grad_queries, grad_keys, grad_values = attend_backward(
@@ -237,30 +215,36 @@
     def over_x(values):
         return pick(values, x_lo, 0).astype(F32) + x_pair(pick(values, 1 - x_lo, 0)).astype(F32)
 
-    left = total(exchange(halves[..., :1024].transpose(1, 0, 2, 3), "z")).astype(BF)
+    def over_z(values):
+        return reduce_ring(values, z, z_up, z_down, z_far)
+
+    left = over_z(halves[..., :1024].transpose(1, 0, 2, 3)).astype(BF)
     right = over_x(halves[..., 1024:]).astype(BF)
-    grad_normed_first = jnp.concatenate([over_x(left), total(exchange(right, "z"))], axis=-1)
+    grad_normed_first = jnp.concatenate([over_x(left), over_z(right)], axis=-1)
     unit_rows, inverse_rows = norm_stats(token_rows)
     grad_tokens = (grad_middle + norm_back(grad_normed_first, ln1_gain, unit_rows, inverse_rows)).astype(BF)
 
     def own_first(values):
         return jnp.where(x_lo == 0, values, values[::-1])
+
+    def over_y(values):
+        return reduce_ring(values, y, y_up, y_down, y_far)
+
+    def over_ring(values):
+        return reduce_ring(values, x_hi * 2 + x_lo, x_up, x_down, x_far)
 
     def sum_columns(grad):
         rows = grad.shape[0] // 2
         blocks = own_first(grad.reshape(2, rows, 2, 1024)).transpose(2, 0, 1, 3).reshape(4, rows, 1024)
-        over_x = total(exchange(blocks, ("x_hi", "x_lo"))).astype(BF)
-        return total(exchange(over_x.reshape(rows, 4, 256).transpose(1, 0, 2), "y"))
+        return over_y(over_ring(blocks).astype(BF).reshape(rows, 4, 256).transpose(1, 0, 2))
 
     grad_down = sum_columns(grad_down)
     grad_out = sum_columns(grad_out)
-    up_sums = total(exchange(grad_up.reshape(2, 4, 256, 1024).transpose(1, 0, 2, 3), "y")).astype(BF)
+    up_sums = over_y(grad_up.reshape(2, 4, 256, 1024).transpose(1, 0, 2, 3)).astype(BF)
     up_blocks = own_first(up_sums.reshape(2, 256, 2, 512).transpose(2, 0, 1, 3)).transpose(1, 0, 2, 3)
-    grad_up = total(exchange(up_blocks.reshape(4, 256, 512), ("x_hi", "x_lo")))
-    qkv_sums = total(
-        exchange(grad_qkv_part.astype(BF).reshape(3, 2, 4, 256, 128).transpose(2, 1, 0, 3, 4), "y")
-    ).astype(BF)
-    grad_qkv = total(exchange(qkv_sums, "x_hi"))
+    grad_up = over_ring(up_blocks.reshape(4, 256, 512))
+    qkv_sums = over_y(grad_qkv_part.astype(BF).reshape(3, 2, 4, 256, 128).transpose(2, 1, 0, 3, 4)).astype(BF)
+    grad_qkv = pick(qkv_sums, x_hi, 0).astype(F32) + shift("x_hi", 2, 1)(pick(qkv_sums, 1 - x_hi, 0)).astype(F32)
     return (output, grad_tokens, grad_qkv, grad_out, grad_up, grad_down, sums[:2], sums[2:])
 
 

time: 638 us -> 470 us (0.74)
  waiting for transfers between devices: 241 us -> 136 us
  starting transfers between devices: 104 us -> 75.6 us
  other arithmetic: 74 us -> 53.5 us
  matrix products: 117 us -> 99.1 us
  between operations: 3.03 us -> 15.9 us
  blocking collectives: 9.99 us -> 0 us
    all_to_all x21 -> x2, waiting for transfers between devices: 218 us -> 16.8 us  [the longest x1 16.8 us: body(): attended_rows = lax.all_to_all(attended, TENSOR, 0, 1, tiled=True)]
    all_to_all x21 -> x2, starting transfers between devices: 89.1 us -> 10.7 us  [the longest x1 6.47 us: body(): attended_rows = lax.all_to_all(attended, TENSOR, 0, 1, tiled=True)]
    ppermute x0 -> x37, waiting for transfers between devices: none -> 76.1 us  [shift(): lax.ppermute(values, axes, [(i, (i + step) % sizes) for i in range(sizes)])]
    ppermute x0 -> x37, starting transfers between devices: none -> 56.2 us  [shift(): lax.ppermute(values, axes, [(i, (i + step) % sizes) for i in range(sizes)])]
    reduce_scatter x0 -> x2, waiting for transfers between devices: none -> 23.3 us  [scatter(): lax.psum_scatter(values, axes, scatter_dimension=0, tiled=True).astype(F32)]
    reduce_sum x17 -> x3, other arithmetic: 25.9 us -> 3.91 us  [norm_stats(): variance = jnp.mean(offsets * offsets, axis=-1, keepdims=True)]
    ppermute x4 -> x2, waiting for transfers between devices: 21.5 us -> 0.01 us  [x_partner(): return lax.ppermute(values, ('x_hi', 'x_lo', 'core'), pairs)]
    unnamed x141 -> x122, local copies, waits for them, and re-layouts: 18.2 us -> 34.3 us
  transfers between devices with their start and end apart: 39 -> 52, of which waited for: 23 -> 17; matrix products, arithmetic and copies ran while one was open for 33% -> 41% of each run, Pallas kernels for 0% -> 0%
where the time goes in v3:
time: 470 us; the launch traced here: 465 us
  waiting for transfers between devices  136 us (29%)
  matrix products  99.1 us (21%)
  local copies, waits for them, and re-layouts  84.7 us (18%)
  starting transfers between devices  75.6 us (16%)
  other arithmetic  53.5 us (11%)
  between operations  15.9 us (3%)
    dot_general x33, matrix products, dot(): lax.dot_general(left, right, ((dims[:1], dims[1:]), ((), ())), preferred_...  83.2 us
    ppermute x37, waiting for transfers between devices, shift(): lax.ppermute(values, axes, [(i, (i + step) % sizes) for i in range(sizes)])  76.1 us
    ppermute x37, starting transfers between devices, shift(): lax.ppermute(values, axes, [(i, (i + step) % sizes) for i in range(sizes)])  56.2 us
    unnamed x122, local copies, waits for them, and re-layouts  34.3 us
    reduce_scatter x2, waiting for transfers between devices, scatter(): lax.psum_scatter(values, axes, scatter_dimension=0, tiled=True).astype(F32)  23.3 us
    all_to_all x1, waiting for transfers between devices, body(): attended_rows = lax.all_to_all(attended, TENSOR, 0, 1, tiled=True)  16.8 us
    all_gather x1, waiting for transfers between devices, body(): out_full = lax.all_gather(out_weight, TENSOR, axis=0, tiled=True)  13.5 us
    reshape x4, local copies, waits for them, and re-layouts, sum_columns(): grad.reshape(2, rows, 2, 1024)  12.6 us
  transfers between devices with their start and end apart: 52, of which 17 were waited for; matrix products, arithmetic and copies ran while one was open for 41% of the time, Pallas kernels for 0%

profile of v3, /device:TPU:0, one launch (start us, length us, event | category | flops | bytes accessed | tf_op | source)
XLA Modules:
  0.0 465.1 jit_solution(11829841564606268216)
XLA Ops:
  16.8 5.4 %fusion.21 = bf16[3,2048,128]{2,1,0:T(8,128)(2,1)S(1)} fusion(bf16[3,2048,128]{2,1,0:T(8,128)(2,1)S(1)} %copy-done.19, bf16[2048,2048]{1,0:T(8,128)(2,1)S(1)} %copy-done.4, f32[2048]{0:T(1024)S(1)} %copy-done.41, f32[2048]{0:T(1024)S(1)} %copy-done.29, f32[2048]{0:T(1024)S(1)} %add_rsqrt_fusion, f32[2048]{0:T(1024)S(1)} %broadcast_multiply_fusion), kind=kOutput, calls=%fused_computation.52 | convolution fusion | flops 3247177728 | bytes 11567104 | tf_op jit(solution)/shard_map/td,cdh->cth/dot_general | solution.py:163
  33.1 6.5 %all-to-all-start = ((bf16[16,128,128]{1,2,0:T(8,128)(2,1)}), bf16[16,128,128]{1,2,0:T(8,128)(2,1)}, u32[]{:S(2)}, u32[]{:S(2)}) async-start(bf16[16,128,128]{1,2,0:T(8,128)(2,1)} %copy.27), calls=%async_computation | async-start | bytes 1048576 | tf_op jit(solution)/shard_map/all_to_all | solution.py:165
  39.7 16.8 %all-to-all-done = bf16[16,128,128]{1,2,0:T(8,128)(2,1)} async-done(((bf16[16,128,128]{1,2,0:T(8,128)(2,1)}), bf16[16,128,128]{1,2,0:T(8,128)(2,1)}, u32[]{:S(2)}, u32[]{:S(2)}) %all-to-all-start) | async-done | bytes 524320 | tf_op jit(solution)/shard_map/all_to_all | solution.py:165
  56.5 13.5 %all-gather.4.cloned.1.call-done = bf16[2048,2048]{1,0:T(8,128)(2,1)} async-done(((bf16[128,2048]{1,0:T(8,128)(2,1)}), bf16[2048,2048]{1,0:T(8,128)(2,1)}) %all-gather.4.cloned.1.call-update) | async-done | bytes 8388624 | tf_op jit(solution)/shard_map/all_gather | solution.py:147
  70.0 5.0 %fusion.123 = (f32[128]{0:T(128)S(1)}, f32[128,2048]{1,0:T(8,128)S(1)}) fusion(bf16[128,2048]{0,1:T(8,128)(2,1)} %bitcast.17, bf16[2048,2048]{1,0:T(8,128)(2,1)} %all-gather.4.cloned.1.call-done, bf16[2048,2048]{1,0:T(8,128)(2,1)} %param.31, s32[]{:T(128)S(6)} %select_n.260), kind=kOutput, calls=%fused_computation.284 | convolution fusion | flops 1074528128 | bytes 10486276 | tf_op jit(solution)/shard_map/dot_general | solution.py:60
  86.7 17.6 %collective-permute-done.2 = bf16[128,2048]{1,0:T(8,128)(2,1)} collective-permute-done((bf16[128,2048]{1,0:T(8,128)(2,1)}, bf16[128,2048]{1,0:T(8,128)(2,1)}, u32[]{:S(2)}, u32[]{:S(2)}) %collective-permute-start.2) | collective-permute-done | bytes 524320 | tf_op jit(solution)/shard_map/ppermute | solution.py:34
  108.2 13.3 %collective-permute-done.4 = bf16[128,2048]{1,0:T(8,128)(2,1)} collective-permute-done((bf16[128,2048]{1,0:T(8,128)(2,1)}, bf16[128,2048]{1,0:T(8,128)(2,1)}, u32[]{:S(2)}, u32[]{:S(2)}) %collective-permute-start.4) | collective-permute-done | bytes 524320 | tf_op jit(solution)/shard_map/ppermute | solution.py:34
  147.6 7.7 %fusion.124 = f32[1024,1024]{1,0:T(8,128)S(1)} fusion(bf16[1024,2048]{1,0:T(8,128)(2,1)} %all-gather.6.cloned.1.call-done, bf16[2048,1024]{1,0:T(8,128)(2,1)} %constant_dynamic-update-slice_fusion), kind=kOutput, calls=%fused_computation.285 | convolution fusion | flops 4294967296 | bytes 12582912 | tf_op jit(solution)/shard_map/dot_general | solution.py:60
  155.3 7.0 %fusion.14 = bf16[1024,1024]{1,0:T(8,128)(2,1)S(1)} fusion(f32[1024,1024]{1,0:T(8,128)S(1)} %fusion.124, bf16[1024,2048]{1,0:T(8,128)(2,1)S(1)} %bitcast.326, bf16[1024,2048]{1,0:T(8,128)(2,1)S(1)} %copy-done.22), kind=kOutput, calls=%fused_computation.21 | convolution fusion | flops 4315938816 | bytes 14680064 | tf_op jit(solution)/shard_map/dot_general | solution.py:60
  163.6 8.5 %convolution_convert_fusion.2 = bf16[1024,2048]{1,0:T(8,128)(2,1)} fusion(bf16[1024,1024]{1,0:T(8,128)(2,1)S(1)} %fusion.14, bf16[2048,1024]{1,0:T(8,128)(2,1)} %constant_dynamic-update-slice_fusion), kind=kOutput, calls=%fused_computation.36 | convolution fusion | flops 4297064448 | bytes 10485760 | tf_op jit(solution)/shard_map/dot_general | solution.py:60
  172.4 10.2 %convolution_convert_fusion.3 = bf16[1024,2048]{1,0:T(8,128)(2,1)} fusion(bf16[1024,2048]{1,0:T(8,128)(2,1)} %copy-done.21, f32[1024,1024]{1,0:T(8,128)} %copy-done.49), kind=kOutput, calls=%fused_computation.37 | convolution fusion | flops 4306501632 | bytes 12582912 | tf_op jit(solution)/shard_map/dot_general | solution.py:60
  188.3 10.7 %convolution_convert_fusion = bf16[1024,2048]{1,0:T(8,128)(2,1)} fusion(bf16[1024,2048]{1,0:T(8,128)(2,1)} %bitcast.325, f32[1024,1024]{1,0:T(8,128)} %copy-done.49), kind=kOutput, calls=%fused_computation.34 | convolution fusion | flops 4306501632 | bytes 12582912 | tf_op jit(solution)/shard_map/dot_general | solution.py:60
  199.0 7.9 %reshape.535 = bf16[2,512,2,1024]{3,2,1,0:T(2,128)(2,1)} reshape(bf16[1024,2048]{1,0:T(8,128)(2,1)} %convolution_convert_fusion) | data formatting | bytes 8388608 | tf_op jit(solution)/shard_map/reshape | solution.py:238
  222.2 6.3 %convolution_convert_fusion.1 = bf16[2048,1024]{1,0:T(8,128)(2,1)} fusion(bf16[1024,2048]{1,0:T(8,128)(2,1)S(1)} %copy-done.48, bf16[1024,1024]{1,0:T(8,128)(2,1)S(1)} %copy-done.51), kind=kOutput, calls=%fused_computation.35 | convolution fusion | flops 4297064448 | bytes 10485760 | tf_op jit(solution)/shard_map/dot_general | solution.py:60
  230.4 23.3 %reduce-scatter.3.cloned.1.call-done = bf16[128,2048]{1,0:T(8,128)(2,1)} async-done(((bf16[1024,2048]{1,0:T(8,128)(2,1)}), bf16[128,2048]{1,0:T(8,128)(2,1)}) %reduce-scatter.3.cloned.1.call-update) | async-done | bytes 524304 | tf_op jit(solution)/shard_map/reduce_scatter | solution.py:110
  257.3 6.5 %fusion.52 = bf16[16,16,8,128]{3,2,1,0:T(8,128)(2,1)S(1)} fusion(bf16[128,2048]{1,0:T(8,128)(2,1)} %get-tuple-element.136, bf16[2048,2048]{1,0:T(8,128)(2,1)} %all-gather.4.cloned.1.call-done), kind=kOutput, calls=%fused_computation.110 | convolution fusion | flops 1074003968 | bytes 9437184 | tf_op jit(solution)/shard_map/dot_general | solution.py:60
  302.9 5.0 %bitcast_convert_fusion = bf16[2048,2048]{1,0:T(8,128)(2,1)S(1)} fusion(bf16[3,2048,128]{2,1,0:T(8,128)(2,1)S(1)} %copy-done.20, bf16[1,2048,128]{2,1,0:T(8,128)(2,1)S(1)} %fusion.32, bf16[1,2048,128]{2,1,0:T(8,128)(2,1)S(1)} %fusion.33, bf16[1,512,128]{2,1,0:T(8,128)(2,1)S(1)} %fusion.59, bf16[1,512,128]{2,1,0:T(8,128)(2,1)S(1)} %copy-done.27, ...), kind=kOutput, calls=%fused_computation.8 | convolution fusion | flops 3234856960 | bytes 11534336 | tf_op jit(solution)/shard_map/cth,cdh->td/dot_general | solution.py:202
  312.7 5.4 %bitcast_convert_fusion.1 = (bf16[3,2048,128]{1,2,0:T(8,128)(2,1)}, f32[3,128,2048]{2,1,0:T(8,128)S(1)}) fusion(bf16[2048,2048]{1,0:T(8,128)(2,1)S(1)} %bitcast.312, f32[2048]{0:T(1024)S(1)} %copy-done.42, f32[2048]{0:T(1024)S(1)} %copy-done.30, f32[2048]{0:T(1024)S(1)} %copy-done.44, f32[2048]{0:T(1024)S(1)} %copy-done.39, ...), kind=kOutput, calls=%fused_computation.43 | convolution fusion | flops 3256614912 | bytes 14712832 | tf_op jit(solution)/shard_map/td,cth->cdh/dot_general | solution.py:203
  346.2 6.8 %collective-permute-done.42 = f32[4,2048]{1,0:T(4,128)S(1)} collective-permute-done((f32[4,2048]{1,0:T(4,128)S(1)}, f32[4,2048]{1,0:T(4,128)S(1)}, u32[]{:S(2)}, u32[]{:S(2)}) %collective-permute-start.42) | collective-permute-done | bytes 32800 | tf_op jit(solution)/shard_map/ppermute | solution.py:34
  378.6 5.4 %fusion.7 = bf16[8,128,2048]{2,1,0:T(8,128)(2,1)S(1)} fusion(bf16[8,128,2048]{2,1,0:T(8,128)(2,1)} %collective-permute-done.6, bf16[8,2,128,2048]{3,2,1,0:T(8,128)(2,1)} %bitcast.317, s32[]{:T(128)S(6)} %select_n.270), kind=kLoop, calls=%fused_computation.11 | loop fusion | flops 8388608 | bytes 12582916 | tf_op jit(solution)/shard_map/convert_element_type | solution.py:213
  392.5 14.1 %collective-permute-done.7 = bf16[2,128,1024]{2,1,0:T(8,128)(2,1)S(1)} collective-permute-done((bf16[2,128,1024]{2,1,0:T(8,128)(2,1)S(1)}, bf16[2,128,1024]{2,1,0:T(8,128)(2,1)S(1)}, u32[]{:S(2)}, u32[]{:S(2)}) %collective-permute-start.7) | collective-permute-done | bytes 524320 | tf_op jit(solution)/shard_map/ppermute | solution.py:34
  409.6 5.1 %collective-permute-done.11 = bf16[4,128,1024]{2,1,0:T(8,128)(2,1)S(1)} collective-permute-done((bf16[4,128,1024]{2,1,0:T(8,128)(2,1)S(1)}, bf16[4,128,1024]{2,1,0:T(8,128)(2,1)S(1)}, u32[]{:S(2)}, u32[]{:S(2)}) %collective-permute-start.11) | collective-permute-done | bytes 1048608 | tf_op jit(solution)/shard_map/ppermute | solution.py:25
  418.2 7.2 %collective-permute-done.18 = bf16[3,256,128]{2,1,0:T(8,128)(2,1)S(1)} collective-permute-done((bf16[3,256,128]{2,1,0:T(8,128)(2,1)S(1)}, bf16[3,256,128]{2,1,0:T(8,128)(2,1)S(1)}, u32[]{:S(2)}, u32[]{:S(2)}) %collective-permute-start.18) | collective-permute-done | bytes 196640 | tf_op jit(solution)/shard_map/ppermute | solution.py:34
  442.4 7.1 %collective-permute-done.20 = bf16[128,1024]{1,0:T(8,128)(2,1)S(1)} collective-permute-done((bf16[128,1024]{1,0:T(8,128)(2,1)S(1)}, bf16[128,1024]{1,0:T(8,128)(2,1)S(1)}, u32[]{:S(2)}, u32[]{:S(2)}) %collective-permute-start.20) | collective-permute-done | bytes 262176 | tf_op jit(solution)/shard_map/ppermute | solution.py:34
  (348 shorter events, 227.0 us)
Async XLA Ops:
  7.2 62.8 %all-gather.4.cloned.1.call-start = ((), (), s32[]{:S(2)}) async-start(), calls=%async_computation.4 | async-start | bytes 8912896 | tf_op jit(solution)/shard_map/all_gather | solution.py:147
  33.1 23.3 %all-to-all-start = ((bf16[16,128,128]{1,2,0:T(8,128)(2,1)}), bf16[16,128,128]{1,2,0:T(8,128)(2,1)}, u32[]{:S(2)}, u32[]{:S(2)}) async-start(bf16[16,128,128]{1,2,0:T(8,128)(2,1)} %copy.27), calls=%async_computation | async-start | bytes 1048576 | tf_op jit(solution)/shard_map/all_to_all | solution.py:165
  39.6 108.0 %all-gather.6.cloned.1.call-start = ((), (), s32[]{:S(2)}) async-start(), calls=%async_computation.5 | async-start | bytes 4718592 | tf_op jit(solution)/shard_map/all_gather | solution.py:172
  77.1 151.4 %reduce-scatter.5.cloned.1.call-start = ((), (), s32[]{:S(2)}) async-start(), calls=%async_computation.7 | async-start | bytes 4718592 | tf_op jit(solution)/shard_map/reduce_scatter | solution.py:110
  79.5 24.8 %collective-permute-start.2 = (bf16[128,2048]{1,0:T(8,128)(2,1)}, bf16[128,2048]{1,0:T(8,128)(2,1)}, u32[]{:S(2)}, u32[]{:S(2)}) collective-permute-start(bf16[128,2048]{1,0:T(8,128)(2,1)} %get-tuple-element.139), channel_id=1, source_target_pairs={{0,6},{2,0},{4,2},{6,4},{1,7},{3,1},{5,3},{7,5},{8,14},{10,8},{12,... | collective-permute-start | bytes 1572872 | tf_op jit(solution)/shard_map/ppermute | solution.py:34
  82.4 23.9 %collective-permute-start.3 = (bf16[128,2048]{1,0:T(8,128)(2,1)}, bf16[128,2048]{1,0:T(8,128)(2,1)}, u32[]{:S(2)}, u32[]{:S(2)}) collective-permute-start(bf16[128,2048]{1,0:T(8,128)(2,1)} %get-tuple-element.139), channel_id=1, source_target_pairs={{0,4},{2,6},{4,0},{6,2},{1,5},{3,7},{5,1},{7,3},{8,12},{10,14},{12... | collective-permute-start | bytes 1572872 | tf_op jit(solution)/shard_map/ppermute | solution.py:34
  83.1 38.4 %collective-permute-start.4 = (bf16[128,2048]{1,0:T(8,128)(2,1)}, bf16[128,2048]{1,0:T(8,128)(2,1)}, u32[]{:S(2)}, u32[]{:S(2)}) collective-permute-start(bf16[128,2048]{1,0:T(8,128)(2,1)} %get-tuple-element.139), channel_id=1, source_target_pairs={{0,2},{2,4},{4,6},{6,0},{1,3},{3,5},{5,7},{7,1},{8,10},{10,12},{12... | collective-permute-start | bytes 1572872 | tf_op jit(solution)/shard_map/ppermute | solution.py:34
  83.8 52.1 %collective-permute-start = (bf16[2048,512]{1,0:T(8,128)(2,1)}, bf16[2048,512]{1,0:T(8,128)(2,1)}, u32[]{:S(2)}, u32[]{:S(2)}) collective-permute-start(bf16[2048,512]{1,0:T(8,128)(2,1)} %param.38), channel_id=1, source_target_pairs={{0,8},{1,73},{8,64},{9,1},{64,72},{65,9},{72,0},{73,65},{2,10},{3,... | collective-permute-start | bytes 6291464 | tf_op jit(solution)/shard_map/ppermute | solution.py:30
  85.1 53.9 %collective-permute-start.1 = (bf16[512,2048]{1,0:T(8,128)(2,1)}, bf16[512,2048]{1,0:T(8,128)(2,1)}, u32[]{:S(2)}, u32[]{:S(2)}) collective-permute-start(bf16[512,2048]{1,0:T(8,128)(2,1)} %param.39), channel_id=1, source_target_pairs={{0,8},{1,73},{8,64},{9,1},{64,72},{65,9},{72,0},{73,65},{2,10},{3,... | collective-permute-start | bytes 6291464 | tf_op jit(solution)/shard_map/ppermute | solution.py:30
  172.1 81.5 %reduce-scatter.3.cloned.1.call-start = ((), (), s32[]{:S(2)}) async-start(), calls=%async_computation.6 | async-start | bytes 4718592 | tf_op jit(solution)/shard_map/reduce_scatter | solution.py:110
  215.4 61.4 %collective-permute-start.32 = (bf16[512,1024]{1,0:T(8,128)(2,1)}, bf16[512,1024]{1,0:T(8,128)(2,1)}, u32[]{:S(2)}, u32[]{:S(2)}) collective-permute-start(bf16[512,1024]{1,0:T(8,128)(2,1)} %get-tuple-element.140), channel_id=1, source_target_pairs={{0,8},{8,64},{64,72},{72,0},{1,9},{9,65},{65,73},{73,1},{2,10},{10... | collective-permute-start | bytes 3145736 | tf_op jit(solution)/shard_map/ppermute | solution.py:34
  218.6 59.6 %collective-permute-start.33 = (bf16[512,1024]{1,0:T(8,128)(2,1)}, bf16[512,1024]{1,0:T(8,128)(2,1)}, u32[]{:S(2)}, u32[]{:S(2)}) collective-permute-start(bf16[512,1024]{1,0:T(8,128)(2,1)} %get-tuple-element.142), channel_id=1, source_target_pairs={{0,64},{8,72},{64,0},{72,8},{1,65},{9,73},{65,1},{73,9},{2,66},{10... | collective-permute-start | bytes 3145736 | tf_op jit(solution)/shard_map/ppermute | solution.py:34
  221.3 56.9 %collective-permute-start.34 = (bf16[512,1024]{1,0:T(8,128)(2,1)}, bf16[512,1024]{1,0:T(8,128)(2,1)}, u32[]{:S(2)}, u32[]{:S(2)}) collective-permute-start(bf16[512,1024]{1,0:T(8,128)(2,1)} %get-tuple-element.141), channel_id=1, source_target_pairs={{0,72},{8,0},{64,8},{72,64},{1,73},{9,1},{65,9},{73,65},{2,74},{10... | collective-permute-start | bytes 3145736 | tf_op jit(solution)/shard_map/ppermute | solution.py:34
  268.9 164.9 %all-gather.8.cloned.1.call-start = ((), (), s32[]{:S(2)}) async-start(), calls=%async_computation.8 | async-start | bytes 4718592 | tf_op jit(solution)/shard_map/all_gather | solution.py:193
  272.6 48.7 %collective-permute-start.26 = (bf16[2,256,1024]{2,1,0:T(8,128)(2,1)}, bf16[2,256,1024]{2,1,0:T(8,128)(2,1)}, u32[]{:S(2)}, u32[]{:S(2)}) collective-permute-start(bf16[2,256,1024]{2,1,0:T(8,128)(2,1)} %get-tuple-element.143), channel_id=1, source_target_pairs={{0,16},{16,32},{32,48},{48,0},{1,17},{17,33},{33,49},{49,1},{2,18}... | collective-permute-start | bytes 3145736 | tf_op jit(solution)/shard_map/ppermute | solution.py:34
  274.1 48.7 %collective-permute-start.27 = (bf16[2,256,1024]{2,1,0:T(8,128)(2,1)}, bf16[2,256,1024]{2,1,0:T(8,128)(2,1)}, u32[]{:S(2)}, u32[]{:S(2)}) collective-permute-start(bf16[2,256,1024]{2,1,0:T(8,128)(2,1)} %get-tuple-element.145), channel_id=1, source_target_pairs={{0,32},{16,48},{32,0},{48,16},{1,33},{17,49},{33,1},{49,17},{2,34}... | collective-permute-start | bytes 3145736 | tf_op jit(solution)/shard_map/ppermute | solution.py:34
  276.8 47.2 %collective-permute-start.28 = (bf16[2,256,1024]{2,1,0:T(8,128)(2,1)}, bf16[2,256,1024]{2,1,0:T(8,128)(2,1)}, u32[]{:S(2)}, u32[]{:S(2)}) collective-permute-start(bf16[2,256,1024]{2,1,0:T(8,128)(2,1)} %get-tuple-element.144), channel_id=1, source_target_pairs={{0,48},{16,0},{32,16},{48,32},{1,49},{17,1},{33,17},{49,33},{2,50}... | collective-permute-start | bytes 3145736 | tf_op jit(solution)/shard_map/ppermute | solution.py:34
  312.6 66.0 %collective-permute-start.6 = (bf16[8,128,2048]{2,1,0:T(8,128)(2,1)}, bf16[8,128,2048]{2,1,0:T(8,128)(2,1)}, u32[]{:S(2)}, u32[]{:S(2)}) collective-permute-start(bf16[8,128,2048]{2,1,0:T(8,128)(2,1)} %dynamic-slice_bitcast_fusion), channel_id=1, source_target_pairs={{0,1},{1,0},{2,3},{3,2},{4,5},{5,4},{6,7},{7,6},{8,9},{9,8},{10,11... | collective-permute-start | bytes 12582920 | tf_op jit(solution)/shard_map/ppermute | solution.py:21
  322.8 21.9 %collective-permute-start.37 = (bf16[512,256]{0,1:T(8,128)(2,1)S(1)}, bf16[512,256]{0,1:T(8,128)(2,1)}, u32[]{:S(2)}, u32[]{:S(2)}) collective-permute-start(bf16[512,256]{0,1:T(8,128)(2,1)S(1)} %get-tuple-element.158), channel_id=1, source_target_pairs={{0,48},{16,0},{32,16},{48,32},{1,49},{17,1},{33,17},{49,33},{2,50}... | collective-permute-start | bytes 786440 | tf_op jit(solution)/shard_map/ppermute | solution.py:34
  384.9 21.7 %collective-permute-start.7 = (bf16[2,128,1024]{2,1,0:T(8,128)(2,1)S(1)}, bf16[2,128,1024]{2,1,0:T(8,128)(2,1)S(1)}, u32[]{:S(2)}, u32[]{:S(2)}) collective-permute-start(bf16[2,128,1024]{2,1,0:T(8,128)(2,1)S(1)} %get-tuple-element.150), channel_id=1, source_target_pairs={{0,2},{2,4},{4,6},{6,0},{1,3},{3,5},{5,7},{7,1},{8,10},{10,12},{12... | collective-permute-start | bytes 1572872 | tf_op jit(solution)/shard_map/ppermute | solution.py:34
  385.0 21.6 %collective-permute-start.8 = (bf16[2,128,1024]{2,1,0:T(8,128)(2,1)S(1)}, bf16[2,128,1024]{2,1,0:T(8,128)(2,1)S(1)}, u32[]{:S(2)}, u32[]{:S(2)}) collective-permute-start(bf16[2,128,1024]{2,1,0:T(8,128)(2,1)S(1)} %get-tuple-element.152), channel_id=1, source_target_pairs={{0,4},{2,6},{4,0},{6,2},{1,5},{3,7},{5,1},{7,3},{8,12},{10,14},{12... | collective-permute-start | bytes 1572872 | tf_op jit(solution)/shard_map/ppermute | solution.py:34
  388.6 26.1 %collective-permute-start.11 = (bf16[4,128,1024]{2,1,0:T(8,128)(2,1)S(1)}, bf16[4,128,1024]{2,1,0:T(8,128)(2,1)S(1)}, u32[]{:S(2)}, u32[]{:S(2)}) collective-permute-start(bf16[4,128,1024]{2,1,0:T(8,128)(2,1)S(1)} %dynamic-slice_bitcast_fusion.7), channel_id=1, source_target_pairs={{0,8},{8,0},{1,9},{9,1},{2,10},{10,2},{3,11},{11,3},{4,12},{12,4},... | collective-permute-start | bytes 3145736 | tf_op jit(solution)/shard_map/ppermute | solution.py:25
  390.1 43.6 %collective-permute-start.19 = (bf16[1024,128]{1,0:T(8,128)(2,1)S(1)}, bf16[1024,128]{1,0:T(8,128)(2,1)}, u32[]{:S(2)}, u32[]{:S(2)}) collective-permute-start(bf16[1024,128]{1,0:T(8,128)(2,1)S(1)} %copy-done.24), channel_id=1, source_target_pairs={{0,8},{8,0},{1,9},{9,1},{2,10},{10,2},{3,11},{11,3},{4,12},{12,4},... | collective-permute-start | bytes 786440 | tf_op jit(solution)/shard_map/ppermute | solution.py:25
  407.0 22.0 %collective-permute-start.10 = (bf16[128,1024]{1,0:T(8,128)(2,1)S(1)}, bf16[128,1024]{1,0:T(8,128)(2,1)S(1)}, u32[]{:S(2)}, u32[]{:S(2)}) collective-permute-start(bf16[128,1024]{1,0:T(8,128)(2,1)S(1)} %dynamic-slice_bitcast_fusion.25), channel_id=1, source_target_pairs={{0,8},{8,0},{1,9},{9,1},{2,10},{10,2},{3,11},{11,3},{4,12},{12,4},... | collective-permute-start | bytes 786440 | tf_op jit(solution)/shard_map/ppermute | solution.py:25
  (82 other events, 1439.5 us)
Sparse Core Ops, SparseCore 0:
  9.7 60.2 all-gather.3
  77.2 50.3 all-gather.5
  172.2 41.4 reduce-scatter.4
  216.0 37.6 reduce-scatter.2
  284.8 35.3 all-gather.7

commit v4 on v3

v4 whole, which is shorter than its diff:
```python
import functools

import jax
import jax.numpy as jnp
from jax import lax
from jax.experimental import pallas as pl
from jax.experimental.pallas import tpu as pltpu
from jax.sharding import Mesh
from jax.sharding import PartitionSpec as P

HD = 128
EPS = 1e-05
MASKED_SCORE = -1e30
BF = jnp.bfloat16
F32 = jnp.float32

AXES = ("x_hi", "y", "x_lo", "z", "core")
BATCH, TENSOR = AXES[:2], AXES[2:]


def core_swap(values):
    return lax.ppermute(values, "core", [(0, 1), (1, 0)])


def x_pair(values):
    return lax.ppermute(values, "x_lo", [(0, 1), (1, 0)])


def x_partner(values):
    pairs = [(r * 2 + c, ((r + (1, -1)[c]) % 4) * 2 + c) for r in range(4) for c in range(2)]
    return lax.ppermute(values, ("x_hi", "x_lo", "core"), pairs)


def shift(axes, sizes, step):
    return lambda values: lax.ppermute(values, axes, [(i, (i + step) % sizes) for i in range(sizes)])


z_up, z_down, z_far = (shift("z", 4, step) for step in (1, -1, 2))
y_up, y_down, y_far = (shift("y", 4, step) for step in (1, -1, 2))
x_up, x_down, x_far = (shift(("x_hi", "x_lo"), 4, step) for step in (1, -1, 2))


def norm_stats(values):
    centre = jnp.mean(values, axis=-1, keepdims=True)
    offsets = values - centre
    variance = jnp.mean(offsets * offsets, axis=-1, keepdims=True)
    inverse = lax.rsqrt(variance + EPS)
    return (offsets * inverse, inverse)


def norm_back(grad_normed, gain, unit_rows, inverse):
    scaled = grad_normed * gain
    return inverse * (
        scaled
        - jnp.mean(scaled, axis=-1, keepdims=True)
        - unit_rows * jnp.mean(scaled * unit_rows, axis=-1, keepdims=True)
    )


def dot(left, right, dims):
    return lax.dot_general(left, right, ((dims[:1], dims[1:]), ((), ())), preferred_element_type=F32)


def params(limit=60, **kw):
    return pltpu.CompilerParams(vmem_limit_bytes=limit * 2**20, **kw)


def qkv_kernel(x_ref, gain_ref, shift_ref, w_ref, normed_ref, out_ref, weights):
    @pl.when(pl.program_id(0) == 0)
    def _():
        for c in range(3):
            weights[:, c * HD : (c + 1) * HD] = w_ref[c]

    x = x_ref[...].astype(F32)
    offsets = x - jnp.mean(x, axis=-1, keepdims=True)
    inverse = lax.rsqrt(jnp.mean(offsets * offsets, axis=-1, keepdims=True) + EPS)
    normed = (offsets * inverse * gain_ref[...] + shift_ref[...]).astype(BF)
    normed_ref[...] = normed
    out_ref[...] = dot(normed, weights[...], (1, 0)).astype(BF)

def project(tokens, gain, shift, weight):
    rows = 256
    return pl.pallas_call(
        qkv_kernel,
        grid=(2048 // rows,),
        in_specs=[
            pl.BlockSpec((rows, 2048), lambda i: (i, 0)),
            pl.BlockSpec((1, 2048), lambda i: (0, 0)),
            pl.BlockSpec((1, 2048), lambda i: (0, 0)),
            pl.BlockSpec((3, 2048, HD), lambda i: (0, 0, 0)),
        ],
        out_specs=[pl.BlockSpec((rows, 2048), lambda i: (i, 0)), pl.BlockSpec((rows, 3 * HD), lambda i: (i, 0))],
        out_shape=[jax.ShapeDtypeStruct((2048, 2048), BF), jax.ShapeDtypeStruct((2048, 3 * HD), BF)],
        scratch_shapes=[pltpu.VMEM((2048, 3 * HD), BF)],
        compiler_params=params(),
        cost_estimate=pl.CostEstimate(flops=2 * 2048 * 2048 * 384, bytes_accessed=20 << 20, transcendentals=0),
    )(tokens, gain[None], shift[None], weight)


QB = 512
SCALE = HD ** -0.5

def masked(scores, first_query, first_key, length):
    query = first_query + lax.broadcasted_iota(jnp.int32, scores.shape, 0)
    key = first_key + lax.broadcasted_iota(jnp.int32, scores.shape, 1)
    return jnp.where((key <= query) & (key < length), scores, MASKED_SCORE)

def forward_kernel(length_ref, qkv_ref, out_ref, total_ref):
    length = length_ref[0]
    for i in range(2048 // QB):
        q = qkv_ref[i * QB : (i + 1) * QB, :HD]
        parts = []
        for j in range(i + 1):
            k = qkv_ref[j * QB : (j + 1) * QB, HD : 2 * HD]
            parts.append(masked(dot(q, k, (1, 1)) * SCALE, i * QB, j * QB, length))
        peak = functools.reduce(jnp.maximum, [jnp.max(p, axis=-1, keepdims=True) for p in parts])
        total = jnp.zeros((QB, 1), F32)
        acc = jnp.zeros((QB, HD), F32)
        for j in range(i + 1):
            e = jnp.exp(parts[j] - peak)
            total += jnp.sum(e, axis=-1, keepdims=True)
            acc += dot(e.astype(BF), qkv_ref[j * QB : (j + 1) * QB, 2 * HD :], (1, 0))
        out_ref[i * QB : (i + 1) * QB] = (acc / total).astype(BF)
        total_ref[i * QB : (i + 1) * QB] = peak + jnp.log(total)

def attend(qkv, lengths):
    return pl.pallas_call(
        forward_kernel,
        in_specs=[pl.BlockSpec(memory_space=pltpu.SMEM), pl.BlockSpec(memory_space=pltpu.VMEM)],
        out_specs=[pl.BlockSpec(memory_space=pltpu.VMEM)] * 2,
        out_shape=[jax.ShapeDtypeStruct((2048, HD), BF), jax.ShapeDtypeStruct((2048, 1), F32)],
        compiler_params=params(),
        cost_estimate=pl.CostEstimate(flops=2 * 2 * 2048 * 2048 * 128, bytes_accessed=3 << 20, transcendentals=2048 * 1280),
    )(lengths, qkv)

def backward_kernel(length_ref, qkv_ref, grad_ref, total_ref, out_ref, gk, gv, probs, gprobs):
    length = length_ref[0]
    n = 2048 // QB
    gk[...] = jnp.zeros_like(gk)
    gv[...] = jnp.zeros_like(gv)
    for i in range(n):
        rows = slice(i * QB, (i + 1) * QB)
        q = qkv_ref[rows, :HD]
        g = grad_ref[rows]
        total = total_ref[rows]
        centre = jnp.zeros((QB, 1), F32)
        for j in range(i + 1):
            keys = slice(j * QB, (j + 1) * QB)
            s = masked(dot(q, qkv_ref[keys, HD : 2 * HD], (1, 1)) * SCALE, i * QB, j * QB, length)
            p = jnp.exp(s - total)
            gp = dot(g, qkv_ref[keys, 2 * HD :], (1, 1))
            centre += jnp.sum(p * gp, axis=-1, keepdims=True)
            probs[:, keys] = p
            gprobs[:, keys] = gp
        gq = jnp.zeros((QB, HD), F32)
        for j in range(i + 1):
            keys = slice(j * QB, (j + 1) * QB)
            p = probs[:, keys]
            gs = (p * (gprobs[:, keys] - centre)).astype(BF)
            gq += dot(gs, qkv_ref[keys, HD : 2 * HD], (1, 0))
            gk[keys] += dot(gs, q, (0, 0))
            gv[keys] += dot(p.astype(BF), g, (0, 0))
        out_ref[rows, :HD] = (gq * SCALE).astype(BF)
    out_ref[:, HD : 2 * HD] = (gk[...] * SCALE).astype(BF)
    out_ref[:, 2 * HD :] = gv[...].astype(BF)

def attend_back(qkv, grad, totals, lengths):
    return pl.pallas_call(
        backward_kernel,
        in_specs=[pl.BlockSpec(memory_space=pltpu.SMEM)] + [pl.BlockSpec(memory_space=pltpu.VMEM)] * 3,
        out_specs=pl.BlockSpec(memory_space=pltpu.VMEM),
        out_shape=jax.ShapeDtypeStruct((2048, 3 * HD), BF),
        scratch_shapes=[pltpu.VMEM((2048, HD), F32), pltpu.VMEM((2048, HD), F32), pltpu.VMEM((QB, 2048), F32), pltpu.VMEM((QB, 2048), F32)],
        compiler_params=params(),
        cost_estimate=pl.CostEstimate(flops=5 * 2 * 2048 * 1280 * 128, bytes_accessed=4 << 20, transcendentals=2048 * 1280),
    )(lengths, qkv, grad, totals)


GELU_A = 0.7978845608028654
GELU_B = 0.044715

def front_kernel(place_ref, n_ref, mine_ref, other_ref, uo, up, do, dp, act_ref, gh_ref, part_ref, inc_ref):
    core = place_ref[0]
    inc_ref[0, core] = mine_ref[0]
    inc_ref[0, 1 - core] = other_ref[0]
    n = n_ref[0].reshape(256, 2048)
    inc = inc_ref[0].reshape(256, 2048)
    part = jnp.zeros((256, 2048), F32)
    for h, (u, d) in enumerate(((uo, do), (up, dp))):
        cols = slice(h * 512, (h + 1) * 512)
        hidden = dot(n, u[...], (1, 0))
        square = hidden * hidden
        t = jnp.tanh(GELU_A * (hidden + GELU_B * hidden * square))
        act_ref[:, cols] = (0.5 * hidden * (1 + t)).astype(BF)
        slope = 0.5 * (1 + t) + 0.5 * hidden * (1 - t * t) * (GELU_A * (1 + 3 * GELU_B * square))
        gh = (dot(inc, d[...], (1, 1)) * slope).astype(BF)
        gh_ref[:, cols] = gh
        part += dot(gh, u[...], (1, 1))
    part_ref[0] = part.astype(BF).reshape(2, 128, 2048)

def front(place, normed, mine, other, uo, up, do, dp):
    whole = lambda a: pl.BlockSpec(a.shape, lambda i, p: (0,) * a.ndim)
    blk = pl.BlockSpec((1, 2, 128, 2048), lambda i, p: (i, 0, 0, 0))
    one = pl.BlockSpec((1, 128, 2048), lambda i, p: ((i + 4 - p[1]) % 4, 0, 0))
    col = pl.BlockSpec((256, 1024), lambda i, p: (i, 0))
    return pl.pallas_call(
        front_kernel,
        grid_spec=pltpu.PrefetchScalarGridSpec(
            num_scalar_prefetch=1, grid=(4,),
            in_specs=[blk, one, one, whole(uo), whole(up), whole(do), whole(dp)],
            out_specs=[col, col, blk, blk],
        ),
        out_shape=[jax.ShapeDtypeStruct((1024, 1024), BF)] * 2 + [jax.ShapeDtypeStruct((4, 2, 128, 2048), BF)] * 2,
        compiler_params=params(),
        cost_estimate=pl.CostEstimate(flops=6 * 1024 * 1024 * 2048, bytes_accessed=28 << 20, transcendentals=1 << 20),
    )(place, normed, mine, other, uo, up, do, dp)


def mixed_kernel(act_ref, do, dp, out_ref):
    a = act_ref[...]
    out_ref[...] = (dot(a[:, :512], do[...], (1, 0)) + dot(a[:, 512:], dp[...], (1, 0))).astype(BF)

def mix(act, do, dp):
    whole = lambda a: pl.BlockSpec(a.shape, lambda i: (0,) * a.ndim)
    return pl.pallas_call(
        mixed_kernel, grid=(4,),
        in_specs=[pl.BlockSpec((256, 1024), lambda i: (i, 0)), whole(do), whole(dp)],
        out_specs=pl.BlockSpec((256, 2048), lambda i: (i, 0)),
        out_shape=jax.ShapeDtypeStruct((1024, 2048), BF),
        compiler_params=params(),
        cost_estimate=pl.CostEstimate(flops=2 * 1024 * 1024 * 2048, bytes_accessed=10 << 20, transcendentals=0),
    )(act, do, dp)


def grads_kernel(n_ref, inc_ref, act_ref, gh_ref, down_ref, up_ref):
    down_ref[...] = dot(act_ref[...], inc_ref[...], (0, 0)).astype(BF)
    up_ref[...] = dot(n_ref[...], gh_ref[...], (0, 0)).astype(BF)

def weight_grads(n, inc, act, gh):
    return pl.pallas_call(
        grads_kernel, grid=(4,),
        in_specs=[pl.BlockSpec((1024, 2048), lambda j: (0, 0))] * 2 + [pl.BlockSpec((1024, 256), lambda j: (0, j))] * 2,
        out_specs=[pl.BlockSpec((256, 2048), lambda j: (j, 0)), pl.BlockSpec((2048, 256), lambda j: (0, j))],
        out_shape=[jax.ShapeDtypeStruct((1024, 2048), BF), jax.ShapeDtypeStruct((2048, 1024), BF)],
        compiler_params=params(),
        cost_estimate=pl.CostEstimate(flops=4 * 1024 * 1024 * 2048, bytes_accessed=20 << 20, transcendentals=0),
    )(n, inc, act, gh)


def first_kernel(gp_ref, w_ref, out_ref):
    g = gp_ref[...]
    out_ref[...] = sum(dot(g[:, c * HD : (c + 1) * HD], w_ref[c], (1, 1)) for c in range(3)).astype(BF)

def first_back(gp, w):
    return pl.pallas_call(
        first_kernel, grid=(8,),
        in_specs=[pl.BlockSpec((256, 384), lambda i: (i, 0)), pl.BlockSpec((3, 2048, HD), lambda i: (0, 0, 0))],
        out_specs=pl.BlockSpec((256, 2048), lambda i: (i, 0)),
        out_shape=jax.ShapeDtypeStruct((2048, 2048), BF),
        compiler_params=params(),
        cost_estimate=pl.CostEstimate(flops=2 * 2048 * 2048 * 384, bytes_accessed=11 << 20, transcendentals=0),
    )(gp, w)

def stack_kernel(*refs):
    out, sem = refs[-2:]
    copies = [pltpu.make_async_copy(ref, out.at[i], sem.at[i]) for i, ref in enumerate(refs[:-2])]
    for copy in copies:
        copy.start()
    for copy in copies:
        copy.wait()

def stack(*arrays):
    return pl.pallas_call(
        stack_kernel,
        in_specs=[pl.BlockSpec(memory_space=pl.ANY)] * len(arrays),
        out_specs=pl.BlockSpec(memory_space=pl.ANY),
        out_shape=jax.ShapeDtypeStruct((len(arrays), *arrays[0].shape), arrays[0].dtype),
        scratch_shapes=[pltpu.SemaphoreType.DMA((len(arrays),))],
    )(*arrays)

def qkv_grads_kernel(n_ref, gp_ref, w_ref, out_ref, gain_ref, shift_ref, sums):
    @pl.when(pl.program_id(0) == 0)
    def _():
        sums[...] = jnp.sum(gp_ref[...].astype(F32), axis=0, keepdims=True)

    grad = dot(n_ref[...], gp_ref[...], (0, 0))
    out_ref[...] = grad.astype(BF)
    gain = jnp.zeros((256, 1), F32)
    shift = jnp.zeros((256, 1), F32)
    for c in range(3):
        cols = slice(c * HD, (c + 1) * HD)
        w = w_ref[c].astype(F32)
        gain += jnp.sum(w * grad[:, cols], axis=-1, keepdims=True)
        shift += jnp.sum(w * sums[:, cols], axis=-1, keepdims=True)
    gain_ref[...] = gain
    shift_ref[...] = shift

def qkv_grads(normed, gp, w):
    return pl.pallas_call(
        qkv_grads_kernel, grid=(8,),
        in_specs=[
            pl.BlockSpec((2048, 256), lambda i: (0, i)),
            pl.BlockSpec((2048, 384), lambda i: (0, 0)),
            pl.BlockSpec((3, 256, HD), lambda i: (0, i, 0)),
        ],
        out_specs=[pl.BlockSpec((256, 384), lambda i: (i, 0))] + [pl.BlockSpec((256, 1), lambda i: (i, 0))] * 2,
        out_shape=[jax.ShapeDtypeStruct((2048, 384), BF)] + [jax.ShapeDtypeStruct((2048, 1), F32)] * 2,
        scratch_shapes=[pltpu.VMEM((1, 384), F32)],
        compiler_params=params(),
        cost_estimate=pl.CostEstimate(flops=2 * 2048 * 2048 * 384, bytes_accessed=12 << 20, transcendentals=0),
    )(normed, gp, w)


def scatter(values, axes):
    return lax.psum_scatter(values, axes, scatter_dimension=0, tiled=True).astype(F32)


def pick(values, index, axis):
    return lax.dynamic_index_in_dim(values, index, axis, False)


def over_y(values, y, axis):
    parts = [pick(values, (y + by) % 4, axis) for by in range(4)]
    return sum(move(part).astype(F32) for move, part in zip((lambda v: v, y_up, y_far, y_down), parts))


def over_x(own, partner, x_hi, x_lo, axis):
    size = own.shape[axis] // 2
    up_hi = jnp.where(x_lo == 0, x_hi, 1 - x_hi)

    def part(values, at):
        return lax.dynamic_slice_in_dim(values, at * size, size, axis)

    return (
        part(own, x_hi).astype(F32)
        + x_far(part(own, 1 - x_hi)).astype(F32)
        + x_up(part(partner, up_hi)).astype(F32)
        + x_down(part(partner, 1 - up_hi)).astype(F32)
    )


def sum_of_all(values):
    for move in (core_swap, z_far, z_up, x_far, x_up, y_far, y_up):
        values = values + move(values)
    return values


def body(
    tokens,
    ln1_gain,
    ln1_shift,
    qkv_weight,
    out_weight,
    ln2_gain,
    ln2_shift,
    up_weight,
    down_weight,
    lengths,
    cotangent,
):
    x_hi, y, x_lo, z, core = (lax.axis_index(axis) for axis in AXES)
    tensor = x_lo * 8 + z * 2 + core
    length = lengths[0]

    out_full = lax.all_gather(out_weight, TENSOR, axis=0, tiled=True)
    live_rows = (tensor * 128 + jnp.arange(128, dtype=jnp.int32) < length).astype(F32)[:, None]
    incoming_rows = cotangent.astype(F32) * live_rows
    sent_rows = incoming_rows.astype(BF)
    along_z = stack(sent_rows, z_down(sent_rows), z_far(sent_rows), z_up(sent_rows))
    up_partner = x_partner(up_weight)
    down_partner = x_partner(down_weight)

    normed_first, projected = project(tokens, ln1_gain, ln1_shift, qkv_weight)
    attended, totals = attend(projected, lengths)
    attended, along_z = lax.optimization_barrier((attended, along_z))
    from_core = core_swap(along_z)
    attended_rows = lax.all_to_all(attended, TENSOR, 0, 1, tiled=True)
    attended_rows, from_core, up_partner = lax.optimization_barrier((attended_rows, from_core, up_partner))
    branch_rows = dot(attended_rows, out_full, (1, 0))
    token_rows = lax.dynamic_slice_in_dim(tokens, tensor * 128, 128, 0).astype(F32)
    middle_rows = token_rows + branch_rows
    unit_second, inverse_second = norm_stats(middle_rows)
    normed_rows = (unit_second * ln2_gain + ln2_shift).astype(BF)

    normed_second = lax.all_gather(normed_rows, ("z", "core"), axis=0, tiled=True)
    activated, grad_hidden, grad_normed_part, incoming = front(
        jnp.stack([core, z]),
        normed_second.reshape(4, 2, 128, 2048),
        along_z,
        from_core,
        up_weight,
        up_partner,
        down_weight,
        down_partner,
    )
    incoming = incoming.reshape(1024, 2048)
    grad_normed_second = scatter(grad_normed_part.reshape(1024, 2048), ("z", "core"))
    grad_down, grad_up = weight_grads(normed_second, incoming, activated, grad_hidden)
    mixed_part = mix(activated, down_weight, down_partner)

    grad_middle = incoming_rows + norm_back(grad_normed_second, ln2_gain, unit_second, inverse_second)
    gain_second = jnp.sum(grad_normed_second * unit_second, axis=0)
    shift_second = jnp.sum(grad_normed_second, axis=0)
    grad_branch = grad_middle.astype(BF)
    grad_attended = lax.all_to_all(dot(grad_branch, out_full, (1, 1)).astype(BF), TENSOR, 1, 0, tiled=True)
    mixed_rows = scatter(mixed_part, ("z", "core"))
    output = (middle_rows + mixed_rows).astype(BF)

    branch_back = lax.all_gather(grad_branch, ("z", "core"), axis=0, tiled=True)
    by_half = attended.reshape(2, 1024, HD)
    both_heads = jnp.concatenate([pick(by_half, x_lo, 0), x_pair(pick(by_half, 1 - x_lo, 0))], axis=1)
    grad_out = dot(both_heads, branch_back, (0, 0)).astype(BF)

    grad_projected = attend_back(projected, grad_attended, totals, lengths)
    grad_normed_first = scatter(first_back(grad_projected, qkv_weight), TENSOR)
    grad_qkv, gain_first, shift_first = qkv_grads(normed_first, grad_projected, qkv_weight)
    shift_first = shift_first[:, 0]
    gain_first = (gain_first[:, 0] - ln1_shift * shift_first) / ln1_gain
    sums = sum_of_all(jnp.stack([gain_first, gain_second, shift_first, shift_second]))

    unit_rows, inverse_rows = norm_stats(token_rows)
    grad_tokens = (grad_middle + norm_back(grad_normed_first, ln1_gain, unit_rows, inverse_rows)).astype(BF)

    def sum_columns(grad):
        rows = grad.shape[0] // 2
        along_x = over_x(grad[:rows], grad[rows:], x_hi, x_lo, 1).astype(BF)
        return over_y(along_x.reshape(rows, 4, 256), y, 1)

    grad_down = sum_columns(grad_down)
    grad_out = sum_columns(grad_out)
    up_sums = over_y(grad_up.reshape(2, 4, 256, 1024), y, 1).astype(BF)
    up_sums = up_sums.reshape(512, 1024)
    grad_up = over_x(up_sums[:, :512], up_sums[:, 512:], x_hi, x_lo, 0)
    qkv_sums = over_y(grad_qkv.reshape(2, 4, 256, 384), y, 1).astype(BF)
    grad_qkv = pick(qkv_sums, x_hi, 0).astype(F32) + shift("x_hi", 2, 1)(pick(qkv_sums, 1 - x_hi, 0)).astype(F32)
    grad_qkv = grad_qkv.reshape(256, 3, HD).transpose(1, 0, 2)
    return (output, grad_tokens, grad_qkv, grad_out, grad_up, grad_down, sums[:2], sums[2:])


def solution(mesh):
    return jax.shard_map(
        body,
        mesh=Mesh(mesh.devices.reshape(2, 4, 2, 4, 2), AXES),
        in_specs=(
            P(BATCH, None),
            P(),
            P(),
            P(None, None, TENSOR),
            P(TENSOR, None),
            P(),
            P(),
            P(None, TENSOR),
            P(TENSOR, None),
            P(BATCH),
            P(AXES, None),
        ),
        out_specs=(
            P(AXES, None),
            P(AXES, None),
            P(None, BATCH, TENSOR),
            P(TENSOR, BATCH),
            P(BATCH, TENSOR),
            P(TENSOR, BATCH),
            P(),
            P(),
        ),
        check_vma=False,
    )
```

time: 470 us -> 535 us (1.14)
  Pallas kernels: 0 us -> 163 us
  matrix products: 99.1 us -> 14.9 us
  waiting for transfers between devices: 136 us -> 211 us
  local copies, waits for them, and re-layouts: 84.7 us -> 20.4 us
  other arithmetic: 53.5 us -> 28.1 us
  starting transfers between devices: 75.6 us -> 57.6 us
  blocking collectives: 0 us -> 14.7 us
    pallas_call x0 -> x9, Pallas kernels: none -> 163 us  [the longest x1 64.7 us: stack(): pl.pallas_call(stack_kernel, in_specs=[pl.BlockSpec(memory_space=pl.ANY)]...]
    dot_general x33 -> x3, matrix products: 83.2 us -> 14.9 us  [dot(): lax.dot_general(left, right, ((dims[:1], dims[1:]), ((), ())), preferred_...]
    reduce_scatter x2 -> x3, waiting for transfers between devices: 23.3 us -> 67.1 us  [scatter(): lax.psum_scatter(values, axes, scatter_dimension=0, tiled=True).astype(F32)]
    unnamed x122 -> x30, local copies, waits for them, and re-layouts: 34.3 us -> 2.08 us
    ppermute x2, waiting for transfers between devices: 0.01 us -> 26.4 us  [x_partner(): return lax.ppermute(values, ('x_hi', 'x_lo', 'core'), pairs)]
    ppermute x37 -> x31, waiting for transfers between devices: 76.1 us -> 102 us  [shift(): lax.ppermute(values, axes, [(i, (i + step) % sizes) for i in range(sizes)])]
    dot_general x3 -> x0, matrix products: 15.9 us -> none  [the longest x1 5.43 us: body(): jnp.einsum('td,cth->cdh', normed_first, stacked, preferred_element_type=F32)]
    all_to_all x0 -> x1, blocking collectives: none -> 14.7 us  [body(): lax.all_to_all(dot(grad_branch, out_full, (1, 1)).astype(BF), TENSOR, 1,...]
  transfers between devices with their start and end apart: 52 -> 43, of which waited for: 17 -> 19; matrix products, arithmetic and copies ran while one was open for 41% -> 9% of each run, Pallas kernels for 0% -> 27%
where the time goes in v4:
time: 535 us; the launch traced here: 525 us
  waiting for transfers between devices  211 us (39%)
  Pallas kernels  163 us (30%)
  starting transfers between devices  57.6 us (11%)
  other arithmetic  28.1 us (5%)
  local copies, waits for them, and re-layouts  20.4 us (4%)
  between operations  15.7 us (3%)
  matrix products  14.9 us (3%)
  blocking collectives  14.7 us (3%)
    ppermute x31, waiting for transfers between devices, shift(): lax.ppermute(values, axes, [(i, (i + step) % sizes) for i in range(sizes)])  102 us
    reduce_scatter x3, waiting for transfers between devices, scatter(): lax.psum_scatter(values, axes, scatter_dimension=0, tiled=True).astype(F32)  67.1 us
    pallas_call x1, Pallas kernels, stack(): pl.pallas_call(stack_kernel, in_specs=[pl.BlockSpec(memory_space=pl.ANY)]...  64.7 us
    ppermute x31, starting transfers between devices, shift(): lax.ppermute(values, axes, [(i, (i + step) % sizes) for i in range(sizes)])  46.7 us
    ppermute x2, waiting for transfers between devices, x_partner(): return lax.ppermute(values, ('x_hi', 'x_lo', 'core'), pairs)  26.4 us
    pallas_call x1, Pallas kernels, front(): pl.pallas_call(front_kernel, grid_spec=pltpu.PrefetchScalarGridSpec(num_s...  20.5 us
    dot_general x3, matrix products, dot(): lax.dot_general(left, right, ((dims[:1], dims[1:]), ((), ())), preferred_...  14.9 us
    all_to_all x1, blocking collectives, body(): lax.all_to_all(dot(grad_branch, out_full, (1, 1)).astype(BF), TENSOR, 1,...  14.7 us
  transfers between devices with their start and end apart: 43, of which 19 were waited for; matrix products, arithmetic and copies ran while one was open for 9% of the time, Pallas kernels for 27%

profile of v4, /device:TPU:0, one launch (start us, length us, event | category | flops | bytes accessed | tf_op | source)
XLA Modules:
  0.0 525.3 jit_solution(11260035397053845530)
XLA Ops:
  16.7 13.2 %shard_map.170 = (bf16[2048,2048]{1,0:T(8,128)(2,1)}, bf16[2048,384]{1,0:T(8,128)(2,1)}) custom-call(bf16[2048,2048]{1,0:T(8,128)(2,1)} %x_ref.1, f32[1,2048]{1,0:T(1,128)} %bitcast.118, f32[1,2048]{1,0:T(1,128)} %bitcast.122, bf16[3,2048,128]{2,1,0:T(8,128)(2,1)} %w_ref.5), custom_call_target="tpu_custom_call" | custom-call | flops 3221225472 | bytes 20971520 | tf_op jit(solution)/shard_map/pallas_call | solution.py:83
  29.9 7.1 %shard_map.171 = (bf16[2048,128]{1,0:T(8,128)(2,1)}, f32[2048,1]{1,0:T(8,128)}) custom-call(s32[1]{0:T(128)} %copy.67.length_ref, bf16[2048,384]{1,0:T(8,128)(2,1)} %get-tuple-element.26.qkv_ref), custom_call_target="tpu_custom_call" | custom-call | flops 2147483648 | bytes 3145728 | tf_op jit(solution)/shard_map/pallas_call | solution.py:127
  37.1 15.7 %collective-permute-done.2.refs_3_ = bf16[128,2048]{1,0:T(8,128)(2,1)S(1)} collective-permute-done((bf16[128,2048]{1,0:T(8,128)(2,1)S(1)}, bf16[128,2048]{1,0:T(8,128)(2,1)S(1)}, u32[]{:S(2)}, u32[]{:S(2)}) %collective-permute-start.2) | collective-permute-done | bytes 524320 | tf_op jit(solution)/shard_map/ppermute | solution.py:35
  53.6 64.7 %shard_map.172.mine_ref = bf16[4,128,2048]{2,1,0:T(8,128)(2,1)} custom-call(bf16[128,2048]{1,0:T(8,128)(2,1)} %copy-done.2, bf16[128,2048]{1,0:T(8,128)(2,1)} %copy-done.4, bf16[128,2048]{1,0:T(8,128)(2,1)} %copy-done.5, bf16[128,2048]{1,0:T(8,128)(2,1)} %copy-done.6), custom_call_target="tpu_custom_call" | custom-call | tf_op jit(solution)/shard_map/pallas_call | solution.py:273
  119.4 6.8 %all-to-all-start = ((bf16[16,128,128]{1,2,0:T(8,128)(2,1)}), bf16[16,128,128]{1,2,0:T(8,128)(2,1)S(1)}, u32[]{:S(2)}, u32[]{:S(2)}) async-start(bf16[16,128,128]{1,2,0:T(8,128)(2,1)} %copy.22), calls=%async_computation | async-start | bytes 1048576 | tf_op jit(solution)/shard_map/all_to_all | solution.py:377
  126.3 10.8 %all-to-all-done = bf16[16,128,128]{1,2,0:T(8,128)(2,1)S(1)} async-done(((bf16[16,128,128]{1,2,0:T(8,128)(2,1)}), bf16[16,128,128]{1,2,0:T(8,128)(2,1)S(1)}, u32[]{:S(2)}, u32[]{:S(2)}) %all-to-all-start) | async-done | bytes 524320 | tf_op jit(solution)/shard_map/all_to_all | solution.py:377
  137.2 4.8 fusion.42
  145.0 26.4 %collective-permute-done.5.dp = bf16[512,2048]{1,0:T(8,128)(2,1)} collective-permute-done((bf16[512,2048]{1,0:T(8,128)(2,1)}, bf16[512,2048]{1,0:T(8,128)(2,1)}, u32[]{:S(2)}, u32[]{:S(2)}) %collective-permute-start.5) | collective-permute-done | bytes 2097184 | tf_op jit(solution)/shard_map/ppermute | solution.py:31
  175.1 20.5 %shard_map.173 = (bf16[1024,1024]{1,0:T(8,128)(2,1)}, bf16[1024,1024]{1,0:T(8,128)(2,1)}, bf16[4,2,128,2048]{3,2,1,0:T(8,128)(2,1)}, bf16[4,2,128,2048]{3,2,1,0:T(8,128)(2,1)}) custom-call(s32[2]{0:T(128)} %pad_add_fusion.place_ref, bf16[4,2,128,2048]{3,2,1,0:T(8,128)(2,1)} %bitcast.123, bf16[4,128,2048]{2,1,0:T(8,128)(2,1)} %shard_map.172.mine_ref, ...), custom_call_target="tpu_custom_call" | custom-call | flops 12884901888 | bytes 29360128 | tf_op jit(solution)/shard_map/pallas_call | solution.py:206
  195.6 8.7 %shard_map.174 = bf16[1024,2048]{1,0:T(8,128)(2,1)} custom-call(bf16[1024,1024]{1,0:T(8,128)(2,1)} %get-tuple-element.33.act_ref, bf16[512,2048]{1,0:T(8,128)(2,1)} %do.3, bf16[512,2048]{1,0:T(8,128)(2,1)} %collective-permute-done.5.dp), custom_call_target="tpu_custom_call" | custom-call | flops 4294967296 | bytes 10485760 | tf_op jit(solution)/shard_map/pallas_call | solution.py:225
  204.4 29.3 %reduce-scatter.6.cloned.1.call-done = bf16[128,2048]{1,0:T(8,128)(2,1)} async-done(((bf16[1024,2048]{1,0:T(8,128)(2,1)}), bf16[128,2048]{1,0:T(8,128)(2,1)}) %reduce-scatter.6.cloned.1.call-update) | async-done | bytes 524304 | tf_op jit(solution)/shard_map/reduce_scatter | solution.py:315
  235.3 37.7 %reduce-scatter.4.cloned.1.call-done = bf16[128,2048]{1,0:T(8,128)(2,1)} async-done(((bf16[1024,2048]{1,0:T(8,128)(2,1)}), bf16[128,2048]{1,0:T(8,128)(2,1)}) %reduce-scatter.4.cloned.1.call-update) | async-done | bytes 524304 | tf_op jit(solution)/shard_map/reduce_scatter | solution.py:315
  275.7 6.5 %fusion.8 = bf16[16,16,8,128]{3,2,1,0:T(8,128)(2,1)S(1)} fusion(bf16[128,2048]{1,0:T(8,128)(2,1)} %get-tuple-element.58, bf16[2048,2048]{1,0:T(8,128)(2,1)} %all-gather.4.cloned.1.call-done), kind=kOutput, calls=%fused_computation.18 | convolution fusion | flops 1074003968 | bytes 9437184 | tf_op jit(solution)/shard_map/dot_general | solution.py:61
  282.3 14.7 %all_to_all.38 = bf16[128,16,128]{2,0,1:T(8,128)(2,1)} all-to-all(bf16[128,16,128]{2,0,1:T(8,128)(2,1)S(1)} %bitcast.96), channel_id=1, replica_groups=mesh['x_hi'=2,'y'=4,'x_lo'=2,'z'=4,'core'=2] {'x_lo','z','core'}, dimensions={1} | all-to-all | bytes 1048576 | tf_op jit(solution)/shard_map/all_to_all | solution.py:405
  297.1 11.6 %shard_map.175.gp_ref = bf16[2048,384]{1,0:T(8,128)(2,1)} custom-call(s32[1]{0:T(128)} %copy.67.length_ref, bf16[2048,384]{1,0:T(8,128)(2,1)} %get-tuple-element.26.qkv_ref, bf16[2048,128]{1,0:T(8,128)(2,1)} %bitcast.99, f32[2048,1]{1,0:T(8,128)} %get-tuple-element.35.total_ref), custom_call_target="tpu_custom_call" | custom-call | flops 3355443200 | bytes 4194304 | tf_op jit(solution)/shard_map/pallas_call | solution.py:168
  308.7 11.0 %shard_map.176 = bf16[2048,2048]{1,0:T(8,128)(2,1)} custom-call(bf16[2048,384]{1,0:T(8,128)(2,1)} %shard_map.175.gp_ref, bf16[3,2048,128]{2,1,0:T(8,128)(2,1)} %w_ref.5), custom_call_target="tpu_custom_call" | custom-call | flops 3221225472 | bytes 11534336 | tf_op jit(solution)/shard_map/pallas_call | solution.py:255
  319.8 14.5 %shard_map.178 = (bf16[1024,2048]{1,0:T(8,128)(2,1)}, bf16[2048,1024]{1,0:T(8,128)(2,1)}) custom-call(bf16[1024,2048]{1,0:T(8,128)(2,1)} %all-gather.6.cloned.1.call-done.n_ref, bf16[1024,2048]{1,0:T(8,128)(2,1)} %bitcast.124, bf16[1024,1024]{1,0:T(8,128)(2,1)} %get-tuple-element.33.act_ref, bf16[1024,1024]{1,0:T(8,128)(2,1)} %get-tuple-element.39.gh_ref), custom_call_target="tpu_custom_call" | custom-call | flops 8589934592 | bytes 20971520 | tf_op jit(solution)/shard_map/pallas_call | solution.py:240
  355.5 19.0 %collective-permute-done.24 = bf16[512,1024]{1,0:T(8,128)(2,1)} collective-permute-done((bf16[512,1024]{1,0:T(8,128)(2,1)}, bf16[512,1024]{1,0:T(8,128)(2,1)}, u32[]{:S(2)}, u32[]{:S(2)}) %collective-permute-start.24) | collective-permute-done | bytes 1048608 | tf_op jit(solution)/shard_map/ppermute | solution.py:35
  380.3 31.3 %collective-permute-done.23 = bf16[512,1024]{1,0:T(8,128)(2,1)} collective-permute-done((bf16[512,1024]{1,0:T(8,128)(2,1)}, bf16[512,1024]{1,0:T(8,128)(2,1)}, u32[]{:S(2)}, u32[]{:S(2)}) %collective-permute-start.23) | collective-permute-done | bytes 1048608 | tf_op jit(solution)/shard_map/ppermute | solution.py:35
  421.1 11.6 %shard_map.177 = (bf16[2048,384]{1,0:T(8,128)(2,1)}, f32[2048,1]{1,0:T(8,128)}, f32[2048,1]{1,0:T(8,128)}) custom-call(bf16[2048,2048]{1,0:T(8,128)(2,1)} %get-tuple-element.36.n_ref, bf16[2048,384]{1,0:T(8,128)(2,1)} %shard_map.175.gp_ref, bf16[3,2048,128]{2,1,0:T(8,128)(2,1)} %w_ref.5), custom_call_target="tpu_custom_call" | custom-call | flops 3221225472 | bytes 12582912 | tf_op jit(solution)/shard_map/pallas_call | solution.py:299
  443.5 5.3 %collective-permute-done.30 = f32[4,2048]{1,0:T(4,128)S(1)} collective-permute-done((f32[4,2048]{1,0:T(4,128)S(1)}, f32[4,2048]{1,0:T(4,128)S(1)}, u32[]{:S(2)}, u32[]{:S(2)}) %collective-permute-start.30) | collective-permute-done | bytes 32800 | tf_op jit(solution)/shard_map/ppermute | solution.py:35
  454.9 4.7 collective-permute-done.32
  466.0 7.1 %collective-permute-done.33 = f32[4,2048]{1,0:T(4,128)S(1)} collective-permute-done((f32[4,2048]{1,0:T(4,128)S(1)}, f32[4,2048]{1,0:T(4,128)S(1)}, u32[]{:S(2)}, u32[]{:S(2)}) %collective-permute-start.33) | collective-permute-done | bytes 32800 | tf_op jit(solution)/shard_map/ppermute | solution.py:35
  500.3 4.8 collective-permute-done.13
  (171 shorter events, 121.5 us)
Async XLA Ops:
  7.2 130.0 %all-gather.4.cloned.1.call-start = ((), (), s32[]{:S(2)}) async-start(), calls=%async_computation.5 | async-start | bytes 8912896 | tf_op jit(solution)/shard_map/all_gather | solution.py:365
  9.8 27.3 %collective-permute-start = (bf16[128,2048]{1,0:T(8,128)(2,1)S(1)}, bf16[128,2048]{1,0:T(8,128)(2,1)S(1)}, u32[]{:S(2)}, u32[]{:S(2)}) collective-permute-start(bf16[128,2048]{1,0:T(8,128)(2,1)S(1)} %fusion.23.refs_0_), channel_id=1, source_target_pairs={{0,6},{2,0},{4,2},{6,4},{1,7},{3,1},{5,3},{7,5},{8,14},{10,8},{12,... | collective-permute-start | bytes 1572872 | tf_op jit(solution)/shard_map/ppermute | solution.py:35
  14.0 23.1 %collective-permute-start.1 = (bf16[128,2048]{1,0:T(8,128)(2,1)S(1)}, bf16[128,2048]{1,0:T(8,128)(2,1)S(1)}, u32[]{:S(2)}, u32[]{:S(2)}) collective-permute-start(bf16[128,2048]{1,0:T(8,128)(2,1)S(1)} %fusion.23.refs_0_), channel_id=1, source_target_pairs={{0,4},{2,6},{4,0},{6,2},{1,5},{3,7},{5,1},{7,3},{8,12},{10,14},{12... | collective-permute-start | bytes 1572872 | tf_op jit(solution)/shard_map/ppermute | solution.py:35
  14.0 38.8 %collective-permute-start.2 = (bf16[128,2048]{1,0:T(8,128)(2,1)S(1)}, bf16[128,2048]{1,0:T(8,128)(2,1)S(1)}, u32[]{:S(2)}, u32[]{:S(2)}) collective-permute-start(bf16[128,2048]{1,0:T(8,128)(2,1)S(1)} %fusion.23.refs_0_), channel_id=1, source_target_pairs={{0,2},{2,4},{4,6},{6,0},{1,3},{3,5},{5,7},{7,1},{8,10},{10,12},{12... | collective-permute-start | bytes 1572872 | tf_op jit(solution)/shard_map/ppermute | solution.py:35
  15.2 121.9 %collective-permute-start.4 = (bf16[2048,512]{1,0:T(8,128)(2,1)}, bf16[2048,512]{1,0:T(8,128)(2,1)}, u32[]{:S(2)}, u32[]{:S(2)}) collective-permute-start(bf16[2048,512]{1,0:T(8,128)(2,1)} %uo.1), channel_id=1, source_target_pairs={{0,8},{1,73},{8,64},{9,1},{64,72},{65,9},{72,0},{73,65},{2,10},{3,... | collective-permute-start | bytes 6291464 | tf_op jit(solution)/shard_map/ppermute | solution.py:31
  118.3 18.8 %collective-permute-start.3 = (bf16[4,128,2048]{2,1,0:T(8,128)(2,1)}, bf16[4,128,2048]{2,1,0:T(8,128)(2,1)}, u32[]{:S(2)}, u32[]{:S(2)}) collective-permute-start(bf16[4,128,2048]{2,1,0:T(8,128)(2,1)} %shard_map.172.mine_ref), channel_id=1, source_target_pairs={{0,1},{1,0},{2,3},{3,2},{4,5},{5,4},{6,7},{7,6},{8,9},{9,8},{10,11... | collective-permute-start | bytes 6291464 | tf_op jit(solution)/shard_map/ppermute | solution.py:22
  119.4 17.7 %all-to-all-start = ((bf16[16,128,128]{1,2,0:T(8,128)(2,1)}), bf16[16,128,128]{1,2,0:T(8,128)(2,1)S(1)}, u32[]{:S(2)}, u32[]{:S(2)}) async-start(bf16[16,128,128]{1,2,0:T(8,128)(2,1)} %copy.22), calls=%async_computation | async-start | bytes 1048576 | tf_op jit(solution)/shard_map/all_to_all | solution.py:377
  126.2 48.8 %all-gather.6.cloned.1.call-start = ((), (), s32[]{:S(2)}) async-start(), calls=%async_computation.6 | async-start | bytes 4718592 | tf_op jit(solution)/shard_map/all_gather | solution.py:385
  143.3 90.4 %reduce-scatter.6.cloned.1.call-start = ((), (), s32[]{:S(2)}) async-start(), calls=%async_computation.8 | async-start | bytes 4718592 | tf_op jit(solution)/shard_map/reduce_scatter | solution.py:315
  143.4 28.1 %collective-permute-start.5 = (bf16[512,2048]{1,0:T(8,128)(2,1)}, bf16[512,2048]{1,0:T(8,128)(2,1)}, u32[]{:S(2)}, u32[]{:S(2)}) collective-permute-start(bf16[512,2048]{1,0:T(8,128)(2,1)} %do.3), channel_id=1, source_target_pairs={{0,8},{1,73},{8,64},{9,1},{64,72},{65,9},{72,0},{73,65},{2,10},{3,... | collective-permute-start | bytes 6291464 | tf_op jit(solution)/shard_map/ppermute | solution.py:31
  195.6 77.4 %reduce-scatter.4.cloned.1.call-start = ((), (), s32[]{:S(2)}) async-start(), calls=%async_computation.7 | async-start | bytes 4718592 | tf_op jit(solution)/shard_map/reduce_scatter | solution.py:315
  204.4 282.7 %all-gather.8.cloned.1.call-start = ((), (), s32[]{:S(2)}) async-start(), calls=%async_computation.10 | async-start | bytes 4718592 | tf_op jit(solution)/shard_map/all_gather | solution.py:409
  275.7 238.3 %reduce-scatter.8.cloned.1.call-start = ((), (), s32[]{:S(2)}) async-start(), calls=%async_computation.9 | async-start | bytes 8912896 | tf_op jit(solution)/shard_map/reduce_scatter | solution.py:315
  338.5 36.0 %collective-permute-start.24 = (bf16[512,1024]{1,0:T(8,128)(2,1)}, bf16[512,1024]{1,0:T(8,128)(2,1)}, u32[]{:S(2)}, u32[]{:S(2)}) collective-permute-start(bf16[512,1024]{1,0:T(8,128)(2,1)} %get-tuple-element.65), channel_id=1, source_target_pairs={{0,8},{8,64},{64,72},{72,0},{1,9},{9,65},{65,73},{73,1},{2,10},{10... | collective-permute-start | bytes 3145736 | tf_op jit(solution)/shard_map/ppermute | solution.py:35
  340.3 37.2 %collective-permute-start.25 = (bf16[512,1024]{1,0:T(8,128)(2,1)}, bf16[512,1024]{1,0:T(8,128)(2,1)}, u32[]{:S(2)}, u32[]{:S(2)}) collective-permute-start(bf16[512,1024]{1,0:T(8,128)(2,1)} %get-tuple-element.66), channel_id=1, source_target_pairs={{0,72},{8,0},{64,8},{72,64},{1,73},{9,1},{65,9},{73,65},{2,74},{10... | collective-permute-start | bytes 3145736 | tf_op jit(solution)/shard_map/ppermute | solution.py:35
  343.1 68.5 %collective-permute-start.23 = (bf16[512,1024]{1,0:T(8,128)(2,1)}, bf16[512,1024]{1,0:T(8,128)(2,1)}, u32[]{:S(2)}, u32[]{:S(2)}) collective-permute-start(bf16[512,1024]{1,0:T(8,128)(2,1)} %constant_dynamic-slice_fusion.6), channel_id=1, source_target_pairs={{0,64},{8,72},{64,0},{72,8},{1,65},{9,73},{65,1},{73,9},{2,66},{10... | collective-permute-start | bytes 3145736 | tf_op jit(solution)/shard_map/ppermute | solution.py:35
  349.2 137.8 %collective-permute-start.10 = (bf16[1024,128]{1,0:T(8,128)(2,1)}, bf16[1024,128]{1,0:T(8,128)(2,1)}, u32[]{:S(2)}, u32[]{:S(2)}) collective-permute-start(bf16[1024,128]{1,0:T(8,128)(2,1)} %get-tuple-element.85), channel_id=1, source_target_pairs={{0,8},{8,0},{1,9},{9,1},{2,10},{10,2},{3,11},{11,3},{4,12},{12,4},... | collective-permute-start | bytes 786440 | tf_op jit(solution)/shard_map/ppermute | solution.py:26
  354.0 81.9 %collective-permute-start.17 = (bf16[2,256,1024]{2,1,0:T(8,128)(2,1)}, bf16[2,256,1024]{2,1,0:T(8,128)(2,1)}, u32[]{:S(2)}, u32[]{:S(2)}) collective-permute-start(bf16[2,256,1024]{2,1,0:T(8,128)(2,1)} %get-tuple-element.62), channel_id=1, source_target_pairs={{0,16},{16,32},{32,48},{48,0},{1,17},{17,33},{33,49},{49,1},{2,18}... | collective-permute-start | bytes 3145736 | tf_op jit(solution)/shard_map/ppermute | solution.py:35
  374.5 64.2 %collective-permute-start.18 = (bf16[2,256,1024]{2,1,0:T(8,128)(2,1)}, bf16[2,256,1024]{2,1,0:T(8,128)(2,1)}, u32[]{:S(2)}, u32[]{:S(2)}) collective-permute-start(bf16[2,256,1024]{2,1,0:T(8,128)(2,1)} %get-tuple-element.64), channel_id=1, source_target_pairs={{0,32},{16,48},{32,0},{48,16},{1,33},{17,49},{33,1},{49,17},{2,34}... | collective-permute-start | bytes 3145736 | tf_op jit(solution)/shard_map/ppermute | solution.py:35
  377.6 62.6 %collective-permute-start.19 = (bf16[2,256,1024]{2,1,0:T(8,128)(2,1)}, bf16[2,256,1024]{2,1,0:T(8,128)(2,1)}, u32[]{:S(2)}, u32[]{:S(2)}) collective-permute-start(bf16[2,256,1024]{2,1,0:T(8,128)(2,1)} %get-tuple-element.63), channel_id=1, source_target_pairs={{0,48},{16,0},{32,16},{48,32},{1,49},{17,1},{33,17},{49,33},{2,50}... | collective-permute-start | bytes 3145736 | tf_op jit(solution)/shard_map/ppermute | solution.py:35
  419.4 42.6 %collective-permute-start.26 = (bf16[512,256]{1,0:T(8,128)(2,1)S(1)}, bf16[512,256]{1,0:T(8,128)(2,1)S(1)}, u32[]{:S(2)}, u32[]{:S(2)}) collective-permute-start(bf16[512,256]{1,0:T(8,128)(2,1)S(1)} %bitcast.105), channel_id=1, source_target_pairs={{0,16},{16,32},{32,48},{48,0},{1,17},{17,33},{33,49},{49,1},{2,18}... | collective-permute-start | bytes 786440 | tf_op jit(solution)/shard_map/ppermute | solution.py:35
  436.0 27.2 %collective-permute-start.27 = (bf16[512,256]{1,0:T(8,128)(2,1)S(1)}, bf16[512,256]{1,0:T(8,128)(2,1)S(1)}, u32[]{:S(2)}, u32[]{:S(2)}) collective-permute-start(bf16[512,256]{1,0:T(8,128)(2,1)S(1)} %bitcast.104), channel_id=1, source_target_pairs={{0,32},{16,48},{32,0},{48,16},{1,33},{17,49},{33,1},{49,17},{2,34}... | collective-permute-start | bytes 786440 | tf_op jit(solution)/shard_map/ppermute | solution.py:35
  438.7 25.4 %collective-permute-start.28 = (bf16[512,256]{1,0:T(8,128)(2,1)S(1)}, bf16[512,256]{1,0:T(8,128)(2,1)S(1)}, u32[]{:S(2)}, u32[]{:S(2)}) collective-permute-start(bf16[512,256]{1,0:T(8,128)(2,1)S(1)} %bitcast.103), channel_id=1, source_target_pairs={{0,48},{16,0},{32,16},{48,32},{1,49},{17,1},{33,17},{49,33},{2,50}... | collective-permute-start | bytes 786440 | tf_op jit(solution)/shard_map/ppermute | solution.py:35
  480.5 15.6 %collective-permute-start.7 = (bf16[2,256,384]{1,2,0:T(8,128)(2,1)S(1)}, bf16[2,256,384]{1,2,0:T(8,128)(2,1)}, u32[]{:S(2)}, u32[]{:S(2)}) collective-permute-start(bf16[2,256,384]{1,2,0:T(8,128)(2,1)S(1)} %bitcast.100), channel_id=1, source_target_pairs={{0,32},{16,48},{32,0},{48,16},{1,33},{17,49},{33,1},{49,17},{2,34}... | collective-permute-start | bytes 1179656 | tf_op jit(solution)/shard_map/ppermute | solution.py:35
  (30 other events, 412.0 us)
Sparse Core Ops, SparseCore 0:
  9.7 71.3 all-gather.3
  143.4 31.5 all-gather.5
  195.7 38.0 reduce-scatter.5
  236.0 36.9 reduce-scatter.3
  275.8 36.6 all-gather.7
  319.9 113.1 reduce-scatter.7
